TPU v7x, 128 devices: a whole 4x4x4 slice. The times are simulated.
128 devices in a mesh: grp: 4 (over x), fsdp: 32 (over y, z, core).
Axes of the slice: x: 4, y: 4, z: 4, core: 2. Of those that a mesh axis runs over, the one named last changes fastest.
Arguments:
- tokens: bfloat16 [8192, 4096], P('fsdp'), may hold values from -550 to 550
- attn_gain: float32 [4096], replicated, may hold values from 0.1 to 1.9
- ffn_gain: float32 [4096], replicated, may hold values from 0.1 to 1.9
- w_query: bfloat16 [4096, 4096], P('fsdp', 'grp'), may hold values from -2.421875 to 2.421875
- w_key: bfloat16 [4096, 256], P('fsdp'), may hold values from -0.078125 to 0.078125
- value_weight: bfloat16 [4096, 256], P('fsdp'), may hold values from -0.09375 to 0.09375
- w_out: bfloat16 [4096, 4096], P('grp', 'fsdp'), may hold values from -0.5 to 0.5
- routes: int32 [8192, 8], P('fsdp'), may hold values from 0 to 127, all different within a row; in each aligned block of 256 rows (0 to 255, 256 to 511, ...) at most 24 rows name the same one
- route_probs: bfloat16 [8192, 8], P('fsdp'), may hold values from 0.049804688 to 0.3984375
- w_gate_up: bfloat16 [128, 4096, 1536], P(('grp', 'fsdp')), may hold values from -0.09375 to 0.09375
- w_down: bfloat16 [128, 768, 4096], P(('grp', 'fsdp')), may hold values from -0.21875 to 0.21875
Outputs:
- attn_branch: bfloat16 [8192, 4096], P('fsdp')
- layer_out: bfloat16 [8192, 4096], P('fsdp', 'grp')
Inputs may be any that keep to these rules, and one draw needn't show every extreme that they name: `routes`: each row names 8 different experts. Among the 256 rows of one device (aligned blocks), no expert is named more than 24 times, a bound that some block reaches.
All inputs are finite; a program needn't handle non-finite values.
Results may differ from a plain program's by a relative error of at most 0.015.
Values may be sent and summed in bfloat16 or wider, within the bound.
No kernel may reach another device: no remote copies, remote signals or barrier semaphores. Data moves between devices by JAX's collectives and lax.ppermute only.
A program may use at most 128 MiB of HBM per device.

v0:
```python
import jax
import jax.numpy as jnp
from jax import lax
from jax.sharding import PartitionSpec as P

KEY_VALUE_HEADS = 2
HEAD_DIMENSION = 128
FFW = 768


EPSILON = 1e-06
FLOOR_SCORE = -1e30


def rms_scale(row_data, gain):
    floats = row_data.astype(jnp.float32)
    mean_sq = jnp.mean(floats * floats, axis=-1, keepdims=True)
    return (floats * lax.rsqrt(mean_sq + EPSILON) * gain).astype(jnp.bfloat16)


def attend_block(state, query_bf, key_block, value_block, key_start, positions):
    row_best, row_total, weighted = state
    scores = jnp.einsum(
        "thd,kd->thk", query_bf, key_block, preferred_element_type=jnp.float32
    ) * HEAD_DIMENSION ** (-0.5)
    key_pos = key_start + jnp.arange(key_block.shape[0], dtype=jnp.int32)
    allowed = (key_pos[None, :] <= positions[:, None])[:, None, :]
    masked = jnp.where(allowed, scores, FLOOR_SCORE)
    new_best = jnp.maximum(row_best, jnp.max(masked, axis=2))
    weights = jnp.where(allowed, jnp.exp(masked - new_best[:, :, None]), 0.0)
    rescale = jnp.exp(row_best - new_best)
    row_total = row_total * rescale + jnp.sum(weights, axis=2)
    weighted = weighted * rescale[:, :, None] + jnp.einsum(
        "thk,kd->thd", weights.astype(jnp.bfloat16), value_block, preferred_element_type=jnp.float32
    )
    return (new_best, row_total, weighted)


def on_device(
    tokens,
    attn_gain,
    ffn_gain,
    w_query,
    w_key,
    value_weight,
    w_out,
    routes,
    route_probs,
    w_gate_up,
    w_down,
):
    head_groups = lax.axis_size("grp")
    fsdp_size = lax.axis_size("fsdp")
    current_group = lax.axis_index("grp")
    my_rank = lax.axis_index("fsdp")
    tok_rows = tokens.shape[0]
    model_width = tokens.shape[1]
    head_width = w_query.shape[1]
    group_heads = head_width // HEAD_DIMENSION
    key_value_head = current_group * KEY_VALUE_HEADS // head_groups
    normed = rms_scale(tokens, attn_gain)
    key_cols = lax.dynamic_slice_in_dim(w_key, key_value_head * HEAD_DIMENSION, HEAD_DIMENSION, 1)
    value_cols = lax.dynamic_slice_in_dim(
        value_weight, key_value_head * HEAD_DIMENSION, HEAD_DIMENSION, 1
    )
    query = jnp.dot(
        normed,
        lax.all_gather(w_query, "fsdp", axis=0, tiled=True),
        preferred_element_type=jnp.float32,
    )
    key_local = jnp.dot(
        normed,
        lax.all_gather(key_cols, "fsdp", axis=0, tiled=True),
        preferred_element_type=jnp.float32,
    )
    value_local = jnp.dot(
        normed,
        lax.all_gather(value_cols, "fsdp", axis=0, tiled=True),
        preferred_element_type=jnp.float32,
    )
    query_bf = query.astype(jnp.bfloat16).reshape(tok_rows, group_heads, HEAD_DIMENSION)
    key_local = key_local.astype(jnp.bfloat16)
    value_local = value_local.astype(jnp.bfloat16)
    first_row = my_rank * tok_rows
    positions = first_row + jnp.arange(tok_rows, dtype=jnp.int32)
    last_query = first_row + tok_rows - 1
    attend_init = (
        jnp.full((tok_rows, group_heads), FLOOR_SCORE, jnp.float32),
        jnp.zeros((tok_rows, group_heads), jnp.float32),
        jnp.zeros((tok_rows, group_heads, HEAD_DIMENSION), jnp.float32),
    )
    state = attend_init
    key_rows = lax.all_gather(key_local, "fsdp", axis=0, tiled=True)
    value_rows = lax.all_gather(value_local, "fsdp", axis=0, tiled=True)
    row_count = key_rows.shape[0]
    key_span = 1024

    def visit(running, step_index):
        block_start = step_index * key_span
        key_block = lax.dynamic_slice_in_dim(key_rows, block_start, key_span, 0)
        value_block = lax.dynamic_slice_in_dim(value_rows, block_start, key_span, 0)
        needed = block_start <= last_query
        running = lax.cond(
            needed,
            lambda inner: attend_block(
                inner, query_bf, key_block, value_block, block_start, positions
            ),
            lambda inner: inner,
            running,
        )
        return (running, None)

    state, _ = lax.scan(visit, state, jnp.arange(row_count // key_span, dtype=jnp.int32))
    row_best, row_total, weighted = state
    attended = (weighted / row_total[:, :, None]).astype(jnp.bfloat16).reshape(tok_rows, head_width)
    head_part = jnp.dot(
        attended,
        lax.all_gather(w_out, "fsdp", axis=1, tiled=True),
        preferred_element_type=jnp.float32,
    ).astype(jnp.bfloat16)
    attn_branch = lax.psum(head_part.astype(jnp.float32).astype(jnp.bfloat16), "grp")
    resid = (tokens.astype(jnp.float32) + attn_branch.astype(jnp.float32)).astype(jnp.bfloat16)
    ffn_in = rms_scale(resid, ffn_gain)
    top_count = routes.shape[1]
    experts_all = head_groups * fsdp_size
    capacity = max(2, 3 * tok_rows * top_count // (2 * experts_all))
    group_rows = fsdp_size * capacity
    flat_routes = routes.reshape(-1)
    expert_hits = (
        flat_routes[:, None] == jnp.arange(experts_all, dtype=jnp.int32)[None, :]
    ).astype(jnp.int32)
    slot_ids = jnp.sum(jnp.cumsum(expert_hits, axis=0) * expert_hits, axis=1) - 1
    target = flat_routes * capacity + slot_ids
    local_target = target - current_group * group_rows
    slot_match = (
        local_target[:, None] == jnp.arange(group_rows, dtype=jnp.int32)[None, :]
    ).reshape(tok_rows, top_count, group_rows)
    chosen = jnp.any(slot_match, axis=1).astype(jnp.bfloat16)
    outbound = (
        jnp.einsum("tr,td->rd", chosen, ffn_in, preferred_element_type=jnp.float32)
        .astype(jnp.bfloat16)
        .reshape(fsdp_size, capacity, model_width)
    )
    gate_proj = w_gate_up[0]
    down_proj = w_down[0]
    col_width = model_width // head_groups
    arrived = lax.all_to_all(outbound, "fsdp", split_axis=0, concat_axis=0, tiled=True)
    slot_count = arrived.shape[1]
    arrived_rows = arrived.reshape(-1, model_width)
    gate_up = jnp.dot(arrived_rows, gate_proj, preferred_element_type=jnp.float32)
    hidden = (jax.nn.silu(gate_up[:, :FFW]) * gate_up[:, FFW:]).astype(jnp.bfloat16)
    result = jnp.dot(hidden, down_proj, preferred_element_type=jnp.float32).astype(jnp.bfloat16)
    returned = lax.all_to_all(
        result.reshape(fsdp_size, slot_count, model_width),
        "fsdp",
        split_axis=0,
        concat_axis=0,
        tiled=True,
    )
    mixing = jnp.sum(jnp.where(slot_match, route_probs[:, :, None], 0.0), axis=1)
    group_part = jnp.dot(
        mixing, returned.reshape(group_rows, model_width), preferred_element_type=jnp.float32
    ).astype(jnp.bfloat16)
    expert_mix = lax.psum_scatter(
        group_part.astype(jnp.float32).astype(jnp.bfloat16), "grp", scatter_dimension=1, tiled=True
    ).astype(jnp.float32)
    own_cols = lax.dynamic_slice_in_dim(resid, current_group * col_width, col_width, 1)
    layer_out = (own_cols.astype(jnp.float32) + expert_mix).astype(jnp.bfloat16)
    return (attn_branch, layer_out)


def solution(mesh):
    placed = (
        P("fsdp", None),
        P(),
        P(),
        P("fsdp", "grp"),
        P("fsdp", None),
        P("fsdp", None),
        P("grp", "fsdp"),
        P("fsdp", None),
        P("fsdp", None),
        P(("grp", "fsdp"), None, None),
        P(("grp", "fsdp"), None, None),
    )
    return jax.shard_map(
        on_device,
        mesh=mesh,
        in_specs=placed,
        out_specs=(P("fsdp", None), P("fsdp", "grp")),
        check_vma=False,
    )
```

profile of v0, /device:TPU:5, one launch (start us, length us, event | category | flops | bytes accessed | tf_op | source)
XLA Modules:
  0.0 635.0 jit_solution(16513742144885637357)
XLA Ops:
  13.0 43.6 %all-gather.13.cloned.1.call-done = bf16[4096,128]{1,0:T(8,128)(2,1)} async-done(((bf16[128,128]{1,0:T(8,128)(2,1)}), bf16[4096,128]{1,0:T(8,128)(2,1)}) %all-gather.13.cloned.1.call-update) | async-done | bytes 1048592 | tf_op jit(solution)/shard_map/all_gather | solution.py:78
  56.6 3.3 convolution_convert_fusion.5
  60.0 41.6 %all-gather.7.cloned.1.call-done = bf16[4096,128]{1,0:T(8,128)(2,1)} async-done(((bf16[128,128]{1,0:T(8,128)(2,1)}), bf16[4096,128]{1,0:T(8,128)(2,1)}) %all-gather.7.cloned.1.call-update) | async-done | bytes 1048592 | tf_op jit(solution)/shard_map/all_gather | solution.py:73
  101.6 2.7 convolution_convert_fusion.6
  104.9 51.2 %all-gather.11.cloned.1.call-done = bf16[4096,1024]{1,0:T(8,128)(2,1)} async-done(((bf16[128,1024]{1,0:T(8,128)(2,1)}), bf16[4096,1024]{1,0:T(8,128)(2,1)}) %all-gather.11.cloned.1.call-update) | async-done | bytes 8388624 | tf_op jit(solution)/shard_map/all_gather | solution.py:68
  156.1 5.8 fusion.38
  162.0 40.3 %all-gather.15.cloned.1.call-done = bf16[8192,128]{1,0:T(8,128)(2,1)} async-done(((bf16[256,128]{1,0:T(8,128)(2,1)}), bf16[8192,128]{1,0:T(8,128)(2,1)}) %all-gather.15.cloned.1.call-update) | async-done | bytes 2097168 | tf_op jit(solution)/shard_map/all_gather | solution.py:94
  202.3 45.9 %all-gather.9.cloned.1.call-done = bf16[8192,128]{1,0:T(8,128)(2,1)} async-done(((bf16[256,128]{1,0:T(8,128)(2,1)}), bf16[8192,128]{1,0:T(8,128)(2,1)}) %all-gather.9.cloned.1.call-update) | async-done | bytes 2097168 | tf_op jit(solution)/shard_map/all_gather | solution.py:93
  248.3 19.2 %while.15 = (s32[]{:T(128)}, f32[256,8]{0,1:T(8,128)S(1)}, f32[256,8]{0,1:T(8,128)S(1)}, f32[256,8,128]{2,0,1:T(8,128)S(1)}, s32[8]{0:T(128)S(1)}, /*index=5*/s3...) while((s32[]{:T(128)}, f32[256,8]{0,1:T(8,128)S(1)}, ...), condition=%wide.region_6.7_spmd.clone, body=%wide.region_1.6_spmd.clone.sunk | while | flops 1101796608 | bytes 29503820 | solution.py:113
  249.8 8.7 %conditional.3 = ((f32[256,8]{0,1:T(8,128)S(1)}, f32[256,8]{0,1:T(8,128)S(1)}, f32[256,8,128]{2,0,1:T(8,128)S(1)})) conditional(s32[]{:T(128)} %convert_element_type.154, (f32[256,8]{0,1:T(8,128)S(1)}, f32[256,8]{0,1:T(8,128)S(1)}, f32[256,8,128]{2,0,1:T(8,128)S(1)}) %tuple.52, (s32[]{:T(128)}, s32[]{:T(128)}, bf16[8192,128]{1,0:T(8,128)(2,1)}, ...), branch_computations={%region_2.2_spmd, %region_3.5_spmd} | conditional | flops 1101796608 | bytes 29502546 | solution.py:103
  250.1 2.4 fusion.2
  254.5 3.9 fusion.8
  268.0 41.3 %all-gather.17.cloned.1.call-done = bf16[1024,4096]{1,0:T(8,128)(2,1)} async-done(((bf16[1024,128]{1,0:T(8,128)(2,1)}), bf16[1024,4096]{1,0:T(8,128)(2,1)}) %all-gather.17.cloned.1.call-update) | async-done | bytes 8388624 | tf_op jit(solution)/shard_map/all_gather | solution.py:118
  309.2 7.1 %convolution_convert_fusion.2 = bf16[256,4096]{1,0:T(8,128)(2,1)} fusion(bf16[256,1024]{0,1:T(8,128)(2,1)S(1)} %bitcast.62, bf16[1024,4096]{1,0:T(8,128)(2,1)} %all-gather.17.cloned.1.call-done), kind=kOutput, calls=%fused_computation.37 | convolution fusion | flops 2148532224 | bytes 11010048 | tf_op jit(solution)/shard_map/dot_general | solution.py:116
  320.9 70.9 %all-reduce.2.cloned.1.call-done = bf16[256,4096]{1,0:T(8,128)(2,1)} async-done(((bf16[256,4096]{1,0:T(8,128)(2,1)}), bf16[256,4096]{1,0:T(8,128)(2,1)}) %all-reduce.2.cloned.1.call-update) | async-done | bytes 2097168 | tf_op jit(solution)/shard_map/psum | solution.py:121
  391.8 3.2 fusion.26
  397.0 80.9 %all_to_all.10 = bf16[32,24,4096]{2,1,0:T(8,128)(2,1)S(1)} all-to-all(bf16[32,24,4096]{2,1,0:T(8,128)(2,1)S(1)} %bitcast.58), channel_id=1, replica_groups=mesh['grp'=4,'fsdp'=32] {'fsdp'}, dimensions={0} | all-to-all | bytes 12582912 | tf_op jit(solution)/shard_map/all_to_all | solution.py:147
  477.9 11.7 %fusion.21 = f32[768,1536]{1,0:T(8,128)} fusion(bf16[768,4096]{1,0:T(8,128)(2,1)S(1)} %bitcast.61, bf16[1,4096,1536]{2,1,0:T(8,128)(2,1)S(1)} %bitcast.64), kind=kOutput, calls=%fused_computation.24 | convolution fusion | flops 9663676416 | bytes 23592960 | tf_op jit(solution)/shard_map/dot_general | solution.py:150
  489.6 10.3 %convolution_convert_fusion.1 = bf16[768,4096]{1,0:T(8,128)(2,1)} fusion(bf16[1,768,4096]{2,1,0:T(8,128)(2,1)} %param.25, f32[768,1536]{1,0:T(8,128)} %fusion.21), kind=kOutput, calls=%fused_computation.27 | convolution fusion | flops 4838522880 | bytes 17301504 | tf_op jit(solution)/shard_map/dot_general | solution.py:152
  499.9 4.8 all-to-all-start.1
  507.2 75.3 %all-to-all-done.1 = bf16[32,24,4096]{2,1,0:T(8,128)(2,1)} async-done(((bf16[32,24,4096]{2,1,0:T(8,128)(2,1)}), bf16[32,24,4096]{2,1,0:T(8,128)(2,1)}, u32[]{:S(2)}, u32[]{:S(2)}) %all-to-all-start.1) | async-done | bytes 6291488 | tf_op jit(solution)/shard_map/all_to_all | solution.py:153
  582.5 5.9 convolution_convert_fusion.3
  588.5 34.5 %reduce-scatter.2.cloned.1.call-done = bf16[256,1024]{1,0:T(8,128)(2,1)} async-done(((bf16[256,4096]{1,0:T(8,128)(2,1)}), bf16[256,1024]{1,0:T(8,128)(2,1)}) %reduce-scatter.2.cloned.1.call-update) | async-done | bytes 524304 | tf_op jit(solution)/shard_map/reduce_scatter | solution.py:164
  625.0 3.1 copy.70
  (100 shorter events, 25.1 us)
Async XLA Ops:
  7.2 0.8 copy-start
  7.2 94.4 %copy-start.2 = (bf16[256,4096]{1,0:T(8,128)(2,1)S(1)}, bf16[256,4096]{1,0:T(8,128)(2,1)}, u32[]{:S(2)}) copy-start(bf16[256,4096]{1,0:T(8,128)(2,1)} %param.15) | copy-start | bytes 6291460
  7.2 94.4 %copy-start.6 = (f32[4096]{0:T(1024)S(1)}, f32[4096]{0:T(1024)}, u32[]{:S(2)}) copy-start(f32[4096]{0:T(1024)} %param.16) | copy-start | bytes 49156
  7.2 49.4 %all-gather.13.cloned.1.call-start = ((), (), s32[]{:S(2)}) async-start(), calls=%async_computation.6 | async-start | bytes 1081344 | tf_op jit(solution)/shard_map/all_gather | solution.py:78
  8.7 92.9 %all-gather.7.cloned.1.call-start = ((), (), s32[]{:S(2)}) async-start(), calls=%async_computation.3 | async-start | bytes 1081344 | tf_op jit(solution)/shard_map/all_gather | solution.py:73
  10.1 146.0 %all-gather.11.cloned.1.call-start = ((), (), s32[]{:S(2)}) async-start(), calls=%async_computation.5 | async-start | bytes 8650752 | tf_op jit(solution)/shard_map/all_gather | solution.py:68
  10.8 191.5 %all-gather.15.cloned.1.call-start = ((), (), s32[]{:S(2)}) async-start(), calls=%async_computation.7 | async-start | bytes 2162688 | tf_op jit(solution)/shard_map/all_gather | solution.py:94
  59.9 188.3 %all-gather.9.cloned.1.call-start = ((), (), s32[]{:S(2)}) async-start(), calls=%async_computation.4 | async-start | bytes 2162688 | tf_op jit(solution)/shard_map/all_gather | solution.py:93
  104.3 205.0 %all-gather.17.cloned.1.call-start = ((), (), s32[]{:S(2)}) async-start(), calls=%async_computation.8 | async-start | bytes 8650752 | tf_op jit(solution)/shard_map/all_gather | solution.py:118
  104.8 287.0 %all-reduce.2.cloned.1.call-start = ((), (), s32[]{:S(2)}) async-start(), calls=%async_computation.9 | async-start | bytes 4194304 | tf_op jit(solution)/shard_map/psum | solution.py:121
  309.2 7.1 %copy-start.3 = (s32[256,8]{0,1:T(8,128)S(1)}, s32[256,8]{0,1:T(8,128)}, u32[]{:S(2)}) copy-start(s32[256,8]{0,1:T(8,128)} %param.22) | copy-start | bytes 24580
  317.7 77.3 %copy-start.4 = (f32[4096]{0:T(1024)S(1)}, f32[4096]{0:T(1024)}, u32[]{:S(2)}) copy-start(f32[4096]{0:T(1024)} %param.17) | copy-start | bytes 49156
  395.0 82.9 %slice-start = ((s8[12582912]{0:T(1024)(128)(4,1)}), s8[4194304]{0:T(1024)(128)(4,1)S(1)}, s32[]{:S(2)}) async-start(s8[12582912]{0:T(1024)(128)(4,1)} %bitcast.63), calls=%async_computation.11 | async-start | bytes 8388608
  395.0 82.9 %slice-start.1 = ((s8[12582912]{0:T(1024)(128)(4,1)}), s8[4194304]{0:T(1024)(128)(4,1)S(1)}, s32[]{:S(2)}) async-start(s8[12582912]{0:T(1024)(128)(4,1)} %bitcast.63), calls=%async_computation.12 | async-start | bytes 8388608
  397.0 80.9 %slice-start.2 = ((s8[12582912]{0:T(1024)(128)(4,1)}), s8[4194304]{0:T(1024)(128)(4,1)S(1)}, s32[]{:S(2)}) async-start(s8[12582912]{0:T(1024)(128)(4,1)} %bitcast.63), calls=%async_computation.13 | async-start | bytes 8388608
  499.9 4.9 copy-start.5
  499.9 82.7 %all-to-all-start.1 = ((bf16[32,24,4096]{2,1,0:T(8,128)(2,1)}), bf16[32,24,4096]{2,1,0:T(8,128)(2,1)}, u32[]{:S(2)}, u32[]{:S(2)}) async-start(bf16[32,24,4096]{2,1,0:T(8,128)(2,1)} %bitcast.60), calls=%async_computation.1 | async-start | bytes 12582912 | tf_op jit(solution)/shard_map/all_to_all | solution.py:153
  504.7 118.3 %reduce-scatter.2.cloned.1.call-start = ((), (), s32[]{:S(2)}) async-start(), calls=%async_computation.10 | async-start | bytes 2621440 | tf_op jit(solution)/shard_map/reduce_scatter | solution.py:164
  582.5 45.6 %copy-start.1 = (bf16[128,256]{1,0:T(8,128)(2,1)S(1)}, bf16[128,256]{1,0:T(8,128)(2,1)}, u32[]{:S(2)}) copy-start(bf16[128,256]{1,0:T(8,128)(2,1)} %param.20) | copy-start | bytes 196612
Sparse Core Ops, SparseCore 0:
  10.9 45.6 all-gather.12
  59.4 42.0 all-gather.6
  103.8 52.1 all-gather.10
  158.8 43.4 all-gather.14
  205.0 43.2 all-gather.8
  250.3 58.9 all-gather.16
  316.5 75.2 all-reduce.1
  588.6 34.3 reduce-scatter.1
where the time goes:
time: 638 us; the launch traced here: 635 us
  waiting for transfers between devices  446 us (70%)
  blocking collectives  80.9 us (13%)
  matrix products  55 us (9%)
  other arithmetic  15.4 us (2%)
  between operations  14.4 us (2%)
  local copies, waits for them, and re-layouts  12.3 us (2%)
    all_to_all x1, blocking collectives, on_device(): lax.all_to_all(outbound, 'fsdp', split_axis=0, concat_axis=0, tiled=True)  80.9 us
    all_to_all x1, waiting for transfers between devices, on_device(): lax.all_to_all(result.reshape(fsdp_size, slot_count, model_width), 'fsdp'...  75.3 us
    psum x1, waiting for transfers between devices, on_device(): lax.psum(head_part.astype(jnp.float32).astype(jnp.bfloat16), 'grp')  70.9 us
    all_gather x1, waiting for transfers between devices, on_device(): lax.all_gather(w_query, 'fsdp', axis=0, tiled=True)  51.2 us
    all_gather x1, waiting for transfers between devices, on_device(): key_rows = lax.all_gather(key_local, 'fsdp', axis=0, tiled=True)  45.9 us
    all_gather x1, waiting for transfers between devices, on_device(): lax.all_gather(value_cols, 'fsdp', axis=0, tiled=True)  43.6 us
    all_gather x1, waiting for transfers between devices, on_device(): lax.all_gather(key_cols, 'fsdp', axis=0, tiled=True)  41.6 us
    all_gather x1, waiting for transfers between devices, on_device(): lax.all_gather(w_out, 'fsdp', axis=1, tiled=True)  41.3 us
  transfers between devices with their start and end apart: 9, of which 9 were waited for; matrix products, arithmetic and copies ran while one was open for 6% of the time, Pallas kernels for 0%

commit v1 on v0

--- a/solution.py
+++ b/solution.py
@@ -125,17 +125,21 @@
     experts_all = head_groups * fsdp_size
     capacity = max(2, 3 * tok_rows * top_count // (2 * experts_all))
     group_rows = fsdp_size * capacity
-    flat_routes = routes.reshape(-1)
-    expert_hits = (
-        flat_routes[:, None] == jnp.arange(experts_all, dtype=jnp.int32)[None, :]
-    ).astype(jnp.int32)
-    slot_ids = jnp.sum(jnp.cumsum(expert_hits, axis=0) * expert_hits, axis=1) - 1
-    target = flat_routes * capacity + slot_ids
-    local_target = target - current_group * group_rows
-    slot_match = (
-        local_target[:, None] == jnp.arange(group_rows, dtype=jnp.int32)[None, :]
-    ).reshape(tok_rows, top_count, group_rows)
-    chosen = jnp.any(slot_match, axis=1).astype(jnp.bfloat16)
+    group_experts = fsdp_size
+    expert_ids = current_group * group_experts + jnp.arange(group_experts, dtype=jnp.int32)
+    named = routes[:, :, None] == expert_ids[None, None, :]
+    hits = jnp.any(named, axis=1)
+    token_ids = jnp.arange(tok_rows, dtype=jnp.int32)
+    earlier = (token_ids[None, :] < token_ids[:, None]).astype(jnp.bfloat16)
+    rank = jnp.dot(earlier, hits.astype(jnp.bfloat16), preferred_element_type=jnp.float32)
+    code = jnp.where(hits, rank, -1.0).astype(jnp.bfloat16)
+    row_ids = jnp.arange(group_rows, dtype=jnp.int32)
+    spread = (
+        row_ids[None, :] // capacity == jnp.arange(group_experts, dtype=jnp.int32)[:, None]
+    ).astype(jnp.bfloat16)
+    code_rows = jnp.dot(code, spread, preferred_element_type=jnp.float32)
+    slot_match = code_rows == (row_ids % capacity).astype(jnp.float32)[None, :]
+    chosen = slot_match.astype(jnp.bfloat16)
     outbound = (
         jnp.einsum("tr,td->rd", chosen, ffn_in, preferred_element_type=jnp.float32)
         .astype(jnp.bfloat16)
@@ -157,7 +161,11 @@
         concat_axis=0,
         tiled=True,
     )
-    mixing = jnp.sum(jnp.where(slot_match, route_probs[:, :, None], 0.0), axis=1)
+    named_probs = jnp.sum(jnp.where(named, route_probs[:, :, None], 0.0), axis=1)
+    prob_rows = jnp.dot(
+        named_probs.astype(jnp.bfloat16), spread, preferred_element_type=jnp.float32
+    )
+    mixing = jnp.where(slot_match, prob_rows, 0.0).astype(jnp.bfloat16)
     group_part = jnp.dot(
         mixing, returned.reshape(group_rows, model_width), preferred_element_type=jnp.float32
     ).astype(jnp.bfloat16)

time: 638 us -> 639 us (level)
  transfers between devices with their start and end apart: 9 -> 9, of which waited for: 9 -> 9; matrix products, arithmetic and copies ran while one was open for 6% -> 5% of each run, Pallas kernels for 0% -> 0%
where the time goes in v1:
time: 639 us; the launch traced here: 635 us
  waiting for transfers between devices  452 us (71%)
  blocking collectives  80.9 us (13%)
  matrix products  55.7 us (9%)
  between operations  14.4 us (2%)
  local copies, waits for them, and re-layouts  11.1 us (2%)
  other arithmetic  9.87 us (2%)
    all_to_all x1, blocking collectives, on_device(): lax.all_to_all(outbound, 'fsdp', split_axis=0, concat_axis=0, tiled=True)  80.9 us
    all_to_all x1, waiting for transfers between devices, on_device(): lax.all_to_all(result.reshape(fsdp_size, slot_count, model_width), 'fsdp'...  77.7 us
    psum x1, waiting for transfers between devices, on_device(): lax.psum(head_part.astype(jnp.float32).astype(jnp.bfloat16), 'grp')  74.8 us
    all_gather x1, waiting for transfers between devices, on_device(): lax.all_gather(w_query, 'fsdp', axis=0, tiled=True)  51.2 us
    all_gather x1, waiting for transfers between devices, on_device(): key_rows = lax.all_gather(key_local, 'fsdp', axis=0, tiled=True)  45.9 us
    all_gather x1, waiting for transfers between devices, on_device(): lax.all_gather(value_cols, 'fsdp', axis=0, tiled=True)  43.6 us
    all_gather x1, waiting for transfers between devices, on_device(): lax.all_gather(key_cols, 'fsdp', axis=0, tiled=True)  41.6 us
    all_gather x1, waiting for transfers between devices, on_device(): lax.all_gather(w_out, 'fsdp', axis=1, tiled=True)  41.3 us
  transfers between devices with their start and end apart: 9, of which 9 were waited for; matrix products, arithmetic and copies ran while one was open for 5% of the time, Pallas kernels for 0%

profile of v1, /device:TPU:5, one launch (start us, length us, event | category | flops | bytes accessed | tf_op | source)
XLA Modules:
  0.0 635.2 jit_solution(7689715145708267044)
XLA Ops:
  13.0 43.6 %all-gather.13.cloned.1.call-done = bf16[4096,128]{1,0:T(8,128)(2,1)} async-done(((bf16[128,128]{1,0:T(8,128)(2,1)}), bf16[4096,128]{1,0:T(8,128)(2,1)}) %all-gather.13.cloned.1.call-update) | async-done | bytes 1048592 | tf_op jit(solution)/shard_map/all_gather | solution.py:78
  56.6 3.3 convolution_convert_fusion.5
  60.0 41.6 %all-gather.7.cloned.1.call-done = bf16[4096,128]{1,0:T(8,128)(2,1)} async-done(((bf16[128,128]{1,0:T(8,128)(2,1)}), bf16[4096,128]{1,0:T(8,128)(2,1)}) %all-gather.7.cloned.1.call-update) | async-done | bytes 1048592 | tf_op jit(solution)/shard_map/all_gather | solution.py:73
  101.6 2.7 convolution_convert_fusion.6
  104.9 51.2 %all-gather.11.cloned.1.call-done = bf16[4096,1024]{1,0:T(8,128)(2,1)} async-done(((bf16[128,1024]{1,0:T(8,128)(2,1)}), bf16[4096,1024]{1,0:T(8,128)(2,1)}) %all-gather.11.cloned.1.call-update) | async-done | bytes 8388624 | tf_op jit(solution)/shard_map/all_gather | solution.py:68
  156.1 5.8 fusion.36
  162.0 40.3 %all-gather.15.cloned.1.call-done = bf16[8192,128]{1,0:T(8,128)(2,1)} async-done(((bf16[256,128]{1,0:T(8,128)(2,1)}), bf16[8192,128]{1,0:T(8,128)(2,1)}) %all-gather.15.cloned.1.call-update) | async-done | bytes 2097168 | tf_op jit(solution)/shard_map/all_gather | solution.py:94
  202.3 45.9 %all-gather.9.cloned.1.call-done = bf16[8192,128]{1,0:T(8,128)(2,1)} async-done(((bf16[256,128]{1,0:T(8,128)(2,1)}), bf16[8192,128]{1,0:T(8,128)(2,1)}) %all-gather.9.cloned.1.call-update) | async-done | bytes 2097168 | tf_op jit(solution)/shard_map/all_gather | solution.py:93
  248.3 19.2 %while.15 = (s32[]{:T(128)}, f32[256,8]{0,1:T(8,128)S(1)}, f32[256,8]{0,1:T(8,128)S(1)}, f32[256,8,128]{2,0,1:T(8,128)S(1)}, s32[8]{0:T(128)S(1)}, /*index=5*/s3...) while((s32[]{:T(128)}, f32[256,8]{0,1:T(8,128)S(1)}, ...), condition=%wide.region_6.7_spmd.clone, body=%wide.region_1.6_spmd.clone.sunk | while | flops 1101796608 | bytes 29503820 | solution.py:113
  249.8 8.7 %conditional.3 = ((f32[256,8]{0,1:T(8,128)S(1)}, f32[256,8]{0,1:T(8,128)S(1)}, f32[256,8,128]{2,0,1:T(8,128)S(1)})) conditional(s32[]{:T(128)} %convert_element_type.172, (f32[256,8]{0,1:T(8,128)S(1)}, f32[256,8]{0,1:T(8,128)S(1)}, f32[256,8,128]{2,0,1:T(8,128)S(1)}) %tuple.52, (s32[]{:T(128)}, s32[]{:T(128)}, bf16[8192,128]{1,0:T(8,128)(2,1)}, ...), branch_computations={%region_2.2_spmd, %region_3.5_spmd} | conditional | flops 1101796608 | bytes 29502546 | solution.py:103
  250.1 2.4 fusion.2
  254.5 3.9 fusion.8
  268.0 41.3 %all-gather.17.cloned.1.call-done = bf16[1024,4096]{1,0:T(8,128)(2,1)} async-done(((bf16[1024,128]{1,0:T(8,128)(2,1)}), bf16[1024,4096]{1,0:T(8,128)(2,1)}) %all-gather.17.cloned.1.call-update) | async-done | bytes 8388624 | tf_op jit(solution)/shard_map/all_gather | solution.py:118
  309.2 7.1 %convolution_convert_fusion.2 = bf16[256,4096]{1,0:T(8,128)(2,1)} fusion(bf16[256,1024]{0,1:T(8,128)(2,1)S(1)} %bitcast.55, bf16[1024,4096]{1,0:T(8,128)(2,1)} %all-gather.17.cloned.1.call-done), kind=kOutput, calls=%fused_computation.34 | convolution fusion | flops 2148532224 | bytes 11010048 | tf_op jit(solution)/shard_map/dot_general | solution.py:116
  317.0 74.8 %all-reduce.2.cloned.1.call-done = bf16[256,4096]{1,0:T(8,128)(2,1)} async-done(((bf16[256,4096]{1,0:T(8,128)(2,1)}), bf16[256,4096]{1,0:T(8,128)(2,1)}) %all-reduce.2.cloned.1.call-update) | async-done | bytes 2097168 | tf_op jit(solution)/shard_map/psum | solution.py:121
  391.9 3.2 fusion.24
  397.1 80.9 %all_to_all.10 = bf16[32,24,4096]{2,1,0:T(8,128)(2,1)S(1)} all-to-all(bf16[32,24,4096]{2,1,0:T(8,128)(2,1)S(1)} %bitcast.51), channel_id=1, replica_groups=mesh['grp'=4,'fsdp'=32] {'fsdp'}, dimensions={0} | all-to-all | bytes 12582912 | tf_op jit(solution)/shard_map/all_to_all | solution.py:151
  477.9 11.7 %fusion.21 = f32[768,1536]{1,0:T(8,128)} fusion(bf16[768,4096]{1,0:T(8,128)(2,1)S(1)} %bitcast.54, bf16[1,4096,1536]{2,1,0:T(8,128)(2,1)S(1)} %bitcast.57), kind=kOutput, calls=%fused_computation.24 | convolution fusion | flops 9663676416 | bytes 23592960 | tf_op jit(solution)/shard_map/dot_general | solution.py:154
  489.6 10.3 %convolution_convert_fusion.1 = bf16[768,4096]{1,0:T(8,128)(2,1)} fusion(bf16[1,768,4096]{2,1,0:T(8,128)(2,1)} %param.25, f32[768,1536]{1,0:T(8,128)} %fusion.21), kind=kOutput, calls=%fused_computation.27 | convolution fusion | flops 4838522880 | bytes 17301504 | tf_op jit(solution)/shard_map/dot_general | solution.py:156
  499.9 4.8 all-to-all-start.1
  504.9 77.7 %all-to-all-done.1 = bf16[32,24,4096]{2,1,0:T(8,128)(2,1)} async-done(((bf16[32,24,4096]{2,1,0:T(8,128)(2,1)}), bf16[32,24,4096]{2,1,0:T(8,128)(2,1)}, u32[]{:S(2)}, u32[]{:S(2)}) %all-to-all-start.1) | async-done | bytes 6291488 | tf_op jit(solution)/shard_map/all_to_all | solution.py:157
  582.6 6.1 convolution_convert_fusion.3
  588.7 34.5 %reduce-scatter.2.cloned.1.call-done = bf16[256,1024]{1,0:T(8,128)(2,1)} async-done(((bf16[256,4096]{1,0:T(8,128)(2,1)}), bf16[256,1024]{1,0:T(8,128)(2,1)}) %reduce-scatter.2.cloned.1.call-update) | async-done | bytes 524304 | tf_op jit(solution)/shard_map/reduce_scatter | solution.py:172
  625.2 3.1 copy.51
  (86 shorter events, 18.9 us)
Async XLA Ops:
  7.2 0.8 copy-start
  7.2 94.4 %copy-start.2 = (bf16[256,4096]{1,0:T(8,128)(2,1)S(1)}, bf16[256,4096]{1,0:T(8,128)(2,1)}, u32[]{:S(2)}) copy-start(bf16[256,4096]{1,0:T(8,128)(2,1)} %param.15) | copy-start | bytes 6291460
  7.2 94.4 %copy-start.6 = (f32[4096]{0:T(1024)S(1)}, f32[4096]{0:T(1024)}, u32[]{:S(2)}) copy-start(f32[4096]{0:T(1024)} %param.16) | copy-start | bytes 49156
  7.2 49.4 %all-gather.13.cloned.1.call-start = ((), (), s32[]{:S(2)}) async-start(), calls=%async_computation.6 | async-start | bytes 1081344 | tf_op jit(solution)/shard_map/all_gather | solution.py:78
  8.7 92.9 %all-gather.7.cloned.1.call-start = ((), (), s32[]{:S(2)}) async-start(), calls=%async_computation.3 | async-start | bytes 1081344 | tf_op jit(solution)/shard_map/all_gather | solution.py:73
  10.1 146.0 %all-gather.11.cloned.1.call-start = ((), (), s32[]{:S(2)}) async-start(), calls=%async_computation.5 | async-start | bytes 8650752 | tf_op jit(solution)/shard_map/all_gather | solution.py:68
  10.8 191.5 %all-gather.15.cloned.1.call-start = ((), (), s32[]{:S(2)}) async-start(), calls=%async_computation.7 | async-start | bytes 2162688 | tf_op jit(solution)/shard_map/all_gather | solution.py:94
  59.9 188.3 %all-gather.9.cloned.1.call-start = ((), (), s32[]{:S(2)}) async-start(), calls=%async_computation.4 | async-start | bytes 2162688 | tf_op jit(solution)/shard_map/all_gather | solution.py:93
  104.3 205.0 %all-gather.17.cloned.1.call-start = ((), (), s32[]{:S(2)}) async-start(), calls=%async_computation.8 | async-start | bytes 8650752 | tf_op jit(solution)/shard_map/all_gather | solution.py:118
  104.8 287.0 %all-reduce.2.cloned.1.call-start = ((), (), s32[]{:S(2)}) async-start(), calls=%async_computation.9 | async-start | bytes 4194304 | tf_op jit(solution)/shard_map/psum | solution.py:121
  309.2 7.2 %copy-start.3 = (s32[256,8]{0,1:T(8,128)S(1)}, s32[256,8]{0,1:T(8,128)}, u32[]{:S(2)}) copy-start(s32[256,8]{0,1:T(8,128)} %param.22) | copy-start | bytes 24580
  316.4 78.7 %copy-start.4 = (f32[4096]{0:T(1024)S(1)}, f32[4096]{0:T(1024)}, u32[]{:S(2)}) copy-start(f32[4096]{0:T(1024)} %param.17) | copy-start | bytes 49156
  395.1 82.9 %slice-start = ((s8[12582912]{0:T(1024)(128)(4,1)}), s8[4194304]{0:T(1024)(128)(4,1)S(1)}, s32[]{:S(2)}) async-start(s8[12582912]{0:T(1024)(128)(4,1)} %bitcast.56), calls=%async_computation.11 | async-start | bytes 8388608
  395.1 82.9 %slice-start.1 = ((s8[12582912]{0:T(1024)(128)(4,1)}), s8[4194304]{0:T(1024)(128)(4,1)S(1)}, s32[]{:S(2)}) async-start(s8[12582912]{0:T(1024)(128)(4,1)} %bitcast.56), calls=%async_computation.12 | async-start | bytes 8388608
  397.1 80.9 %slice-start.2 = ((s8[12582912]{0:T(1024)(128)(4,1)}), s8[4194304]{0:T(1024)(128)(4,1)S(1)}, s32[]{:S(2)}) async-start(s8[12582912]{0:T(1024)(128)(4,1)} %bitcast.56), calls=%async_computation.13 | async-start | bytes 8388608
  499.9 4.9 copy-start.5
  499.9 82.7 %all-to-all-start.1 = ((bf16[32,24,4096]{2,1,0:T(8,128)(2,1)}), bf16[32,24,4096]{2,1,0:T(8,128)(2,1)}, u32[]{:S(2)}, u32[]{:S(2)}) async-start(bf16[32,24,4096]{2,1,0:T(8,128)(2,1)} %bitcast.53), calls=%async_computation.1 | async-start | bytes 12582912 | tf_op jit(solution)/shard_map/all_to_all | solution.py:157
  504.8 118.4 %reduce-scatter.2.cloned.1.call-start = ((), (), s32[]{:S(2)}) async-start(), calls=%async_computation.10 | async-start | bytes 2621440 | tf_op jit(solution)/shard_map/reduce_scatter | solution.py:172
  582.6 45.8 %copy-start.1 = (bf16[128,256]{1,0:T(8,128)(2,1)S(1)}, bf16[128,256]{1,0:T(8,128)(2,1)}, u32[]{:S(2)}) copy-start(bf16[128,256]{1,0:T(8,128)(2,1)} %param.20) | copy-start | bytes 196612
Sparse Core Ops, SparseCore 0:
  10.9 45.6 all-gather.12
  59.4 42.0 all-gather.6
  103.8 52.1 all-gather.10
  158.8 43.4 all-gather.14
  205.0 43.2 all-gather.8
  250.3 58.9 all-gather.16
  316.5 75.3 all-reduce.1
  588.8 34.3 reduce-scatter.1

commit v2 on v1

v2 whole, which is shorter than its diff:
```python
import functools

import jax
import jax.numpy as jnp
from jax import lax
from jax.experimental import pallas as pl
from jax.experimental.pallas import tpu as pltpu
from jax.sharding import PartitionSpec as P

KEY_VALUE_HEADS = 2
HEAD_DIMENSION = 128
FFW = 768


EPSILON = 1e-06
FLOOR_SCORE = -1e30
LOG2_E = 1.4426950408889634
KEY_SPAN = 1024
QUERY_TILE = 128
HIDDEN_TILE = 256
NORM_TILE = 64


def rms_scale(row_data, gain):
    floats = row_data.astype(jnp.float32)
    mean_sq = jnp.mean(floats * floats, axis=-1, keepdims=True)
    return (floats * lax.rsqrt(mean_sq + EPSILON) * gain).astype(jnp.bfloat16)


def attend_kernel(rank_ref, query_ref, pairs_ref, out_ref, best, weighted, *, span, heads):
    rank = rank_ref[0]
    rows = query_ref.shape[0]
    factor = HEAD_DIMENSION**-0.5 * LOG2_E
    best[...] = jnp.full_like(best, FLOOR_SCORE)
    weighted[...] = jnp.zeros_like(weighted)

    def step(index, masked):
        start = pl.multiple_of(index * span, span)
        keys = pairs_ref[pl.ds(start, span), :HEAD_DIMENSION]
        values = pairs_ref[pl.ds(start, span), HEAD_DIMENSION:]
        values = jnp.concatenate([values, jnp.ones_like(values)], axis=1)
        for head in range(heads):
            for row in range(0, rows, QUERY_TILE):
                tile = slice(row, row + QUERY_TILE)
                query = query_ref[tile, head * HEAD_DIMENSION : (head + 1) * HEAD_DIMENSION]
                scores = lax.dot_general(
                    query, keys, (((1,), (1,)), ((), ())), preferred_element_type=jnp.float32
                )
                if masked:
                    key_pos = lax.broadcasted_iota(jnp.int32, scores.shape, 1) + start
                    query_pos = lax.broadcasted_iota(jnp.int32, scores.shape, 0) + (
                        rank * rows + row
                    )
                    scores = jnp.where(key_pos <= query_pos, scores, FLOOR_SCORE)
                old = best[head, tile]
                new = jnp.maximum(old, jnp.max(scores, axis=1, keepdims=True))
                weights = jnp.exp2((scores - jnp.tile(new, (1, span // HEAD_DIMENSION))) * factor)
                rescale = jnp.exp2((old - new) * factor)
                best[head, tile] = new
                weighted[head, tile] = weighted[head, tile] * jnp.tile(rescale, (1, 2)) + jnp.dot(
                    weights.astype(jnp.bfloat16), values, preferred_element_type=jnp.float32
                )

    full = rank * rows // span

    def visit(index, carry):
        step(index, False)
        return carry

    lax.fori_loop(0, full, visit, 0)
    step(full, True)
    for head in range(heads):
        out_ref[:, head * HEAD_DIMENSION : (head + 1) * HEAD_DIMENSION] = (
            weighted[head, :, :HEAD_DIMENSION] / weighted[head, :, HEAD_DIMENSION:]
        ).astype(out_ref.dtype)


def attend(rank, query, pairs):
    rows, width = query.shape
    heads = width // HEAD_DIMENSION
    keys = pairs.shape[0]
    span = min(KEY_SPAN, keys)
    return pl.pallas_call(
        functools.partial(attend_kernel, span=span, heads=heads),
        out_shape=jax.ShapeDtypeStruct(query.shape, query.dtype),
        in_specs=[
            pl.BlockSpec(memory_space=pltpu.SMEM),
            pl.BlockSpec(memory_space=pltpu.VMEM),
            pl.BlockSpec(memory_space=pltpu.VMEM),
        ],
        out_specs=pl.BlockSpec(memory_space=pltpu.VMEM),
        scratch_shapes=[
            pltpu.VMEM((heads, rows, HEAD_DIMENSION), jnp.float32),
            pltpu.VMEM((heads, rows, 2 * HEAD_DIMENSION), jnp.float32),
        ],
        compiler_params=pltpu.CompilerParams(vmem_limit_bytes=40 * 2**20),
        cost_estimate=pl.CostEstimate(
            flops=4 * rows * keys * width,
            bytes_accessed=4 * rows * width + 4 * keys * HEAD_DIMENSION,
            transcendentals=rows * keys * heads,
        ),
    )(rank, query, pairs)


def expert_kernel(rows_ref, gain_ref, gate_ref, up_ref, down_ref, out_ref, normed, hidden, *, wide):
    step = pl.program_id(0)
    parts, rows, width = rows_ref.shape

    @pl.when(step == 0)
    def _():
        def scale_rows(index, carry):
            tile = pl.ds(pl.multiple_of(index * NORM_TILE, NORM_TILE), NORM_TILE)
            floats = [rows_ref[part, tile, :].astype(jnp.float32) for part in range(parts)]
            squares = sum(values * values for values in floats)
            mean_sq = jnp.sum(squares, axis=1, keepdims=True) / (parts * width)
            scale = lax.rsqrt(mean_sq + EPSILON)
            for part in range(parts):
                normed[part, tile, :] = (floats[part] * scale * gain_ref[part]).astype(jnp.bfloat16)
            return carry

        lax.fori_loop(0, rows // NORM_TILE, scale_rows, 0)

    @pl.when(step < wide)
    def _():
        def project(weight_ref):
            return sum(
                jnp.dot(
                    normed[part],
                    weight_ref[0, part * width : (part + 1) * width, :],
                    preferred_element_type=jnp.float32,
                )
                for part in range(parts)
            )

        hidden[step] = (jax.nn.silu(project(gate_ref)) * project(up_ref)).astype(jnp.bfloat16)

    @pl.when(step >= wide)
    def _():
        out_ref[0] = sum(
            jnp.dot(
                hidden[tile],
                down_ref[0, tile * HIDDEN_TILE : (tile + 1) * HIDDEN_TILE, :],
                preferred_element_type=jnp.float32,
            )
            for tile in range(wide)
        ).astype(out_ref.dtype)


def run_expert(arrived, gain, w_gate_up, w_down):
    parts, rows, width = arrived.shape
    model_width = parts * width
    wide = FFW // HIDDEN_TILE
    return pl.pallas_call(
        functools.partial(expert_kernel, wide=wide),
        grid=(wide + parts,),
        out_shape=jax.ShapeDtypeStruct(arrived.shape, arrived.dtype),
        in_specs=[
            pl.BlockSpec((parts, rows, width), lambda i: (0, 0, 0)),
            pl.BlockSpec((parts, 1, width), lambda i: (0, 0, 0)),
            pl.BlockSpec((1, model_width, HIDDEN_TILE), lambda i: (0, 0, jnp.minimum(i, wide - 1))),
            pl.BlockSpec(
                (1, model_width, HIDDEN_TILE), lambda i: (0, 0, wide + jnp.minimum(i, wide - 1))
            ),
            pl.BlockSpec((1, FFW, width), lambda i: (0, 0, jnp.maximum(i - wide, 0))),
        ],
        out_specs=pl.BlockSpec((1, rows, width), lambda i: (jnp.maximum(i - wide, 0), 0, 0)),
        scratch_shapes=[
            pltpu.VMEM((parts, rows, width), jnp.bfloat16),
            pltpu.VMEM((wide, rows, HIDDEN_TILE), jnp.bfloat16),
        ],
        compiler_params=pltpu.CompilerParams(vmem_limit_bytes=54 * 2**20),
        cost_estimate=pl.CostEstimate(
            flops=6 * rows * model_width * FFW,
            bytes_accessed=4 * rows * model_width + 6 * model_width * FFW,
            transcendentals=rows * FFW,
        ),
    )(arrived, gain.reshape(parts, 1, width), w_gate_up, w_gate_up, w_down)


def on_device(
    tokens,
    attn_gain,
    ffn_gain,
    w_query,
    w_key,
    value_weight,
    w_out,
    routes,
    route_probs,
    w_gate_up,
    w_down,
):
    head_groups = lax.axis_size("grp")
    fsdp_size = lax.axis_size("fsdp")
    current_group = lax.axis_index("grp")
    my_rank = lax.axis_index("fsdp")
    tok_rows, model_width = tokens.shape
    head_width = w_query.shape[1]
    col_width = model_width // head_groups
    key_value_head = current_group * KEY_VALUE_HEADS // head_groups
    key_cols = lax.dynamic_slice_in_dim(w_key, key_value_head * HEAD_DIMENSION, HEAD_DIMENSION, 1)
    value_cols = lax.dynamic_slice_in_dim(
        value_weight, key_value_head * HEAD_DIMENSION, HEAD_DIMENSION, 1
    )
    w_joint = lax.all_gather(
        jnp.concatenate([w_query, key_cols, value_cols], axis=1), "fsdp", axis=0, tiled=True
    )
    normed = rms_scale(tokens, attn_gain)
    joint = jnp.dot(normed, w_joint, preferred_element_type=jnp.float32).astype(jnp.bfloat16)
    pairs = lax.all_gather(joint[:, head_width:], "fsdp", axis=0, tiled=True)
    attended = attend(my_rank.astype(jnp.int32).reshape(1), joint[:, :head_width], pairs)
    head_part = jnp.dot(
        attended,
        lax.all_gather(w_out, "fsdp", axis=1, tiled=True),
        preferred_element_type=jnp.float32,
    ).astype(jnp.bfloat16)
    branch_cols = lax.psum_scatter(head_part, "grp", scatter_dimension=1, tiled=True)
    attn_branch = lax.all_gather(branch_cols, "grp", axis=1, tiled=True)
    own_cols = lax.dynamic_slice_in_dim(tokens, current_group * col_width, col_width, 1)
    resid = (own_cols.astype(jnp.float32) + branch_cols.astype(jnp.float32)).astype(jnp.bfloat16)

    top_count = routes.shape[1]
    experts_all = head_groups * fsdp_size
    capacity = max(2, 3 * tok_rows * top_count // (2 * experts_all))
    slots = experts_all * capacity
    expert_ids = jnp.arange(experts_all, dtype=jnp.int32)
    named = routes[:, :, None] == expert_ids[None, None, :]
    hits = jnp.any(named, axis=1)
    token_ids = jnp.arange(tok_rows, dtype=jnp.int32)
    earlier = (token_ids[None, :] < token_ids[:, None]).astype(jnp.bfloat16)
    rank = jnp.dot(earlier, hits.astype(jnp.bfloat16), preferred_element_type=jnp.float32)
    code = jnp.where(hits, rank, -1.0).astype(jnp.bfloat16)
    slot_list = jnp.arange(slots, dtype=jnp.int32)
    spread = (slot_list[None, :] // capacity == expert_ids[:, None]).astype(jnp.bfloat16)
    code_slots = jnp.dot(code, spread, preferred_element_type=jnp.float32)
    slot_match = code_slots == (slot_list % capacity).astype(jnp.float32)[None, :]
    chosen = slot_match.astype(jnp.bfloat16)
    named_probs = jnp.sum(jnp.where(named, route_probs[:, :, None], 0.0), axis=1)
    prob_slots = jnp.dot(
        named_probs.astype(jnp.bfloat16), spread, preferred_element_type=jnp.float32
    )
    mixing = jnp.where(slot_match, prob_slots, 0.0).astype(jnp.bfloat16)

    outbound = lax.dot_general(
        chosen, resid, (((0,), (0,)), ((), ())), preferred_element_type=jnp.float32
    ).astype(jnp.bfloat16)
    arrived = lax.all_to_all(
        outbound.reshape(experts_all, capacity, col_width),
        ("grp", "fsdp"),
        split_axis=0,
        concat_axis=0,
        tiled=True,
    )
    result = run_expert(
        arrived.reshape(head_groups, fsdp_size * capacity, col_width), ffn_gain, w_gate_up, w_down
    )
    returned = lax.all_to_all(
        result.reshape(experts_all, capacity, col_width),
        ("grp", "fsdp"),
        split_axis=0,
        concat_axis=0,
        tiled=True,
    )
    expert_mix = jnp.dot(
        mixing, returned.reshape(slots, col_width), preferred_element_type=jnp.float32
    )
    layer_out = (resid.astype(jnp.float32) + expert_mix).astype(jnp.bfloat16)
    return (attn_branch, layer_out)


def solution(mesh):
    placed = (
        P("fsdp", None),
        P(),
        P(),
        P("fsdp", "grp"),
        P("fsdp", None),
        P("fsdp", None),
        P("grp", "fsdp"),
        P("fsdp", None),
        P("fsdp", None),
        P(("grp", "fsdp"), None, None),
        P(("grp", "fsdp"), None, None),
    )
    return jax.shard_map(
        on_device,
        mesh=mesh,
        in_specs=placed,
        out_specs=(P("fsdp", None), P("fsdp", "grp")),
        check_vma=False,
    )
```

time: 639 us -> 452 us (0.71)
  waiting for transfers between devices: 452 us -> 274 us
  matrix products: 55.7 us -> 24.2 us
  Pallas kernels: 0 us -> 29.6 us
    psum x1 -> x0, waiting for transfers between devices: 74.8 us -> none  [on_device(): lax.psum(head_part.astype(jnp.float32).astype(jnp.bfloat16), 'grp')]
    all_gather x5 -> x3, waiting for transfers between devices: 223 us -> 162 us  [the longest x1 59.7 us: on_device(): lax.all_gather(jnp.concatenate([w_query, key_cols, value_cols], axis=1),...]
    all_to_all x1, waiting for transfers between devices: 77.7 us -> 29.4 us  [on_device(): lax.all_to_all(result.reshape(experts_all, capacity, col_width), ('grp',...]
    dot_general x10 -> x4, matrix products: 48.6 us -> 17.2 us  [the longest x1 7.55 us: on_device(): jnp.dot(normed, w_joint, preferred_element_type=jnp.float32)]
    pallas_call x0 -> x2, Pallas kernels: none -> 29.6 us  [the longest x1 25.9 us: run_expert(): pl.pallas_call(functools.partial(expert_kernel, wide=wide), grid=(wide +...]
    all_gather x1, waiting for transfers between devices: 41.3 us -> 55.3 us  [on_device(): lax.all_gather(w_out, 'fsdp', axis=1, tiled=True)]
    reduce_scatter x1, waiting for transfers between devices: 34.5 us -> 26 us  [on_device(): lax.psum_scatter(head_part, 'grp', scatter_dimension=1, tiled=True)]
  transfers between devices with their start and end apart: 9 -> 6, of which waited for: 9 -> 6; matrix products, arithmetic and copies ran while one was open for 5% -> 2% of each run, Pallas kernels for 0% -> 1%
where the time goes in v2:
time: 452 us; the launch traced here: 449 us
  waiting for transfers between devices  274 us (61%)
  blocking collectives  83.3 us (18%)
  Pallas kernels  29.6 us (7%)
  matrix products  24.2 us (5%)
  between operations  13.9 us (3%)
  starting transfers between devices  8.7 us (2%)
  local copies, waits for them, and re-layouts  7.69 us (2%)
  other arithmetic  6.93 us (2%)
    all_to_all x1, blocking collectives, on_device(): lax.all_to_all(outbound.reshape(experts_all, capacity, col_width), ('grp'...  83.3 us
    all_gather x1, waiting for transfers between devices, on_device(): lax.all_gather(jnp.concatenate([w_query, key_cols, value_cols], axis=1),...  59.7 us
    all_gather x1, waiting for transfers between devices, on_device(): attn_branch = lax.all_gather(branch_cols, 'grp', axis=1, tiled=True)  57.5 us
    all_gather x1, waiting for transfers between devices, on_device(): lax.all_gather(w_out, 'fsdp', axis=1, tiled=True)  55.3 us
    all_gather x1, waiting for transfers between devices, on_device(): pairs = lax.all_gather(joint[:, head_width:], 'fsdp', axis=0, tiled=True)  45.2 us
    all_to_all x1, waiting for transfers between devices, on_device(): lax.all_to_all(result.reshape(experts_all, capacity, col_width), ('grp',...  29.4 us
    reduce_scatter x1, waiting for transfers between devices, on_device(): lax.psum_scatter(head_part, 'grp', scatter_dimension=1, tiled=True)  26 us
    pallas_call x1, Pallas kernels, run_expert(): pl.pallas_call(functools.partial(expert_kernel, wide=wide), grid=(wide +...  25.9 us
  transfers between devices with their start and end apart: 6, of which 6 were waited for; matrix products, arithmetic and copies ran while one was open for 2% of the time, Pallas kernels for 1%

profile of v2, /device:TPU:5, one launch (start us, length us, event | category | flops | bytes accessed | tf_op | source)
XLA Modules:
  0.0 448.6 jit_solution(10719903829917538207)
XLA Ops:
  7.2 0.8 constant_dynamic-slice_fusion
  8.0 1.7 pad_maximum_fusion
  9.8 2.1 fusion
  11.9 59.7 %all-gather.5.cloned.1.call-done = bf16[4096,1280]{1,0:T(8,128)(2,1)} async-done(((bf16[128,1280]{1,0:T(8,128)(2,1)}), bf16[4096,1280]{1,0:T(8,128)(2,1)}) %all-gather.5.cloned.1.call-update) | async-done | bytes 10485776 | tf_op jit(solution)/shard_map/all_gather | solution.py:205
  71.6 7.5 %convolution_convert_fusion.2 = bf16[256,1280]{1,0:T(8,128)(2,1)S(1)} fusion(bf16[4096,1280]{1,0:T(8,128)(2,1)} %all-gather.5.cloned.1.call-done, bf16[256,4096]{1,0:T(8,128)(2,1)} %param.11, f32[4096]{0:T(1024)} %param.12, f32[256]{0:T(256)S(1)} %add_rsqrt_fusion), kind=kOutput, calls=%fused_computation.10 | convolution fusion | flops 2688876544 | bytes 13255680 | tf_op jit(solution)/shard_map/dot_general | solution.py:209
  79.1 0.7 slice.9
  79.8 0.7 all-gather.9.cloned.1.call-update
  80.6 45.2 %all-gather.7.cloned.1.call-done.pairs_ref = bf16[8192,256]{1,0:T(8,128)(2,1)} async-done(((bf16[256,256]{1,0:T(8,128)(2,1)}), bf16[8192,256]{1,0:T(8,128)(2,1)}) %all-gather.7.cloned.1.call-update) | async-done | bytes 4194320 | tf_op jit(solution)/shard_map/all_gather | solution.py:210
  125.8 2.2 copy-done
  128.0 3.7 shard_map.122
  131.8 55.3 %all-gather.9.cloned.1.call-done = bf16[1024,4096]{1,0:T(8,128)(2,1)} async-done(((bf16[1024,128]{1,0:T(8,128)(2,1)}), bf16[1024,4096]{1,0:T(8,128)(2,1)}) %all-gather.9.cloned.1.call-update) | async-done | bytes 8388624 | tf_op jit(solution)/shard_map/all_gather | solution.py:214
  187.0 7.0 %convolution_convert_fusion.1 = bf16[256,4096]{1,0:T(8,128)(2,1)} fusion(bf16[256,1024]{1,0:T(8,128)(2,1)S(1)} %shard_map.122, bf16[1024,4096]{1,0:T(8,128)(2,1)} %all-gather.9.cloned.1.call-done), kind=kOutput, calls=%fused_computation.3 | convolution fusion | flops 2148532224 | bytes 11010048 | tf_op jit(solution)/shard_map/dot_general | solution.py:212
  194.7 0.9 convolution_compare_fusion
  195.6 26.0 %reduce-scatter.2.cloned.1.call-done = bf16[256,1024]{1,0:T(8,128)(2,1)} async-done(((bf16[256,4096]{1,0:T(8,128)(2,1)}), bf16[256,1024]{1,0:T(8,128)(2,1)}) %reduce-scatter.2.cloned.1.call-update) | async-done | bytes 524304 | tf_op jit(solution)/shard_map/reduce_scatter | solution.py:217
  221.6 2.9 convolution_convert_fusion
  224.5 83.3 %all_to_all.10 = bf16[128,24,1024]{2,1,0:T(8,128)(2,1)} all-to-all(bf16[128,24,1024]{2,1,0:T(8,128)(2,1)S(1)} %bitcast.13), channel_id=1, replica_groups=mesh['grp'=4,'fsdp'=32] {'grp','fsdp'}, dimensions={0} | all-to-all | bytes 12582912 | tf_op jit(solution)/shard_map/all_to_all | solution.py:247
  307.8 25.9 %shard_map.123 = bf16[4,768,1024]{2,1,0:T(8,128)(2,1)} custom-call(bf16[4,768,1024]{2,1,0:T(8,128)(2,1)} %bitcast.15, f32[4,1,1024]{2,1,0:T(1,128)} %bitcast.16, bf16[1,4096,1536]{2,1,0:T(8,128)(2,1)} %up_ref.1, bf16[1,4096,1536]{2,1,0:T(8,128)(2,1)} %up_ref.1, bf16[1,768,4096]{2,1,0:T(8,128)(2,1)} %down_ref.1), custom_call_target="tpu_custom_call" | custom-call | flops 14495514624 | bytes 31457280 | tf_op jit(solution)/shard_map/pallas_call | solution.py:153
  333.7 8.5 %all-to-all-start.1 = ((bf16[128,24,1024]{2,1,0:T(8,128)(2,1)}), bf16[128,24,1024]{2,1,0:T(8,128)(2,1)}, u32[]{:S(2)}, u32[]{:S(2)}) async-start(bf16[128,24,1024]{2,1,0:T(8,128)(2,1)} %bitcast.14), calls=%async_computation.2 | async-start | bytes 12582912 | tf_op jit(solution)/shard_map/all_to_all | solution.py:257
  342.8 0.7 copy.16
  343.6 2.7 fusion.16
  346.2 57.5 %all-gather.11.cloned.1.call-done = bf16[256,4096]{1,0:T(8,128)(2,1)} async-done(((bf16[256,1024]{1,0:T(8,128)(2,1)}), bf16[256,4096]{1,0:T(8,128)(2,1)}) %all-gather.11.cloned.1.call-update) | async-done | bytes 2097168 | tf_op jit(solution)/shard_map/all_gather | solution.py:218
  403.7 29.4 %all-to-all-done.1 = bf16[128,24,1024]{2,1,0:T(8,128)(2,1)} async-done(((bf16[128,24,1024]{2,1,0:T(8,128)(2,1)}), bf16[128,24,1024]{2,1,0:T(8,128)(2,1)}, u32[]{:S(2)}, u32[]{:S(2)}) %all-to-all-start.1) | async-done | bytes 6291488 | tf_op jit(solution)/shard_map/all_to_all | solution.py:257
  433.1 5.8 %fusion.9 = bf16[256,1024]{1,0:T(8,128)(2,1)} fusion(bf16[3072,1024]{1,0:T(8,128)(2,1)} %bitcast.5, pred[256,3072]{1,0:T(32,128)(4,1)S(1)} %convolution_compare_fusion, bf16[256,128]{1,0:T(8,128)(2,1)} %fusion.16, s32[3072]{0:T(1024)S(1)} %add_select_fusion, bf16[256,1024]{1,0:T(8,128)(2,1)S(1)} %copy-done.2, bf16[256,4096]{1,0:T(8,128)(2,1)S(1)} %copy-done.1, ...), kind=kOutput, calls=%fused_computation.16 | convolution fusion | flops 1815740416 | bytes 8728580 | tf_op jit(solution)/shard_map/dot_general | solution.py:264
  439.0 3.1 copy.21
  (24 shorter events, 1.4 us)
Async XLA Ops:
  7.2 64.4 %all-gather.5.cloned.1.call-start = ((), (), s32[]{:S(2)}) async-start(), calls=%async_computation.3 | async-start | bytes 10813440 | tf_op jit(solution)/shard_map/all_gather | solution.py:205
  9.7 116.1 %all-gather.7.cloned.1.call-start = ((), (), s32[]{:S(2)}) async-start(), calls=%async_computation.4 | async-start | bytes 4325376 | tf_op jit(solution)/shard_map/all_gather | solution.py:210
  79.8 107.2 %all-gather.9.cloned.1.call-start = ((), (), s32[]{:S(2)}) async-start(), calls=%async_computation.5 | async-start | bytes 8650752 | tf_op jit(solution)/shard_map/all_gather | solution.py:214
  80.5 141.0 %reduce-scatter.2.cloned.1.call-start = ((), (), s32[]{:S(2)}) async-start(), calls=%async_computation.6 | async-start | bytes 2621440 | tf_op jit(solution)/shard_map/reduce_scatter | solution.py:217
  125.8 2.2 copy-start
  131.7 62.3 %copy-start.3 = (s32[256,8]{0,1:T(8,128)S(1)}, s32[256,8]{0,1:T(8,128)}, u32[]{:S(2)}) copy-start(s32[256,8]{0,1:T(8,128)} %param.18) | copy-start | bytes 24580
  194.1 27.5 %copy-start.1 = (bf16[256,4096]{1,0:T(8,128)(2,1)S(1)}, bf16[256,4096]{1,0:T(8,128)(2,1)}, u32[]{:S(2)}) copy-start(bf16[256,4096]{1,0:T(8,128)(2,1)} %param.11) | copy-start | bytes 6291460
  333.7 9.1 %copy-start.4 = (bf16[256,8]{0,1:T(8,128)(2,1)S(1)}, bf16[256,8]{0,1:T(8,128)(2,1)}, u32[]{:S(2)}) copy-start(bf16[256,8]{0,1:T(8,128)(2,1)} %param.19) | copy-start | bytes 12292
  333.7 99.4 %copy-start.2 = (bf16[256,1024]{1,0:T(8,128)(2,1)S(1)}, bf16[256,1024]{1,0:T(8,128)(2,1)}, u32[]{:S(2)}) copy-start(bf16[256,1024]{1,0:T(8,128)(2,1)} %reduce-scatter.2.cloned.1.call-done) | copy-start | bytes 1572868
  333.7 99.4 %all-to-all-start.1 = ((bf16[128,24,1024]{2,1,0:T(8,128)(2,1)}), bf16[128,24,1024]{2,1,0:T(8,128)(2,1)}, u32[]{:S(2)}, u32[]{:S(2)}) async-start(bf16[128,24,1024]{2,1,0:T(8,128)(2,1)} %bitcast.14), calls=%async_computation.2 | async-start | bytes 12582912 | tf_op jit(solution)/shard_map/all_to_all | solution.py:257
  342.2 61.5 %all-gather.11.cloned.1.call-start = ((), (), s32[]{:S(2)}) async-start(), calls=%async_computation.7 | async-start | bytes 2621440 | tf_op jit(solution)/shard_map/all_gather | solution.py:218
Sparse Core Ops, SparseCore 0:
  10.8 60.6 all-gather.4
  79.9 45.8 all-gather.6
  128.0 58.9 all-gather.8
  194.2 27.3 reduce-scatter.1
  344.5 59.1 all-gather.10

commit v3 on v2

--- a/solution.py
+++ b/solution.py
@@ -15,7 +15,7 @@
 EPSILON = 1e-06
 FLOOR_SCORE = -1e30
 LOG2_E = 1.4426950408889634
-KEY_SPAN = 1024
+SIDE = 4
 QUERY_TILE = 128
 HIDDEN_TILE = 256
 NORM_TILE = 64
@@ -27,24 +27,69 @@
     return (floats * lax.rsqrt(mean_sq + EPSILON) * gain).astype(jnp.bfloat16)
 
 
-def attend_kernel(rank_ref, query_ref, pairs_ref, out_ref, best, weighted, *, span, heads):
+def to_other_core(rows):
+    return lax.ppermute(rows, "fsdp", [(i, i ^ 1) for i in range(2 * SIDE * SIDE)])
+
+
+def from_group(rows, shift):
+    return lax.ppermute(rows, "grp", [((i + shift) % SIDE, i) for i in range(SIDE)])
+
+
+def from_chips(rows):
+    chips = SIDE * SIDE
+    parts = lax.all_to_all(
+        jnp.broadcast_to(rows[None], (chips, *rows.shape)),
+        "fsdp",
+        split_axis=0,
+        concat_axis=0,
+        axis_index_groups=[[2 * chip + core for chip in range(chips)] for core in range(2)],
+        tiled=True,
+    )
+    return parts.reshape(chips * rows.shape[0], rows.shape[1])
+
+
+def by_core(core, mine, other):
+    return jnp.concatenate(
+        [jnp.where(core == 0, mine, other), jnp.where(core == 0, other, mine)], axis=0
+    )
+
+
+def attend_kernel(
+    rank_ref,
+    query_ref,
+    mine_ref,
+    other_ref,
+    out_ref,
+    best,
+    weighted,
+    *,
+    heads,
+    first_head,
+):
     rank = rank_ref[0]
     rows = query_ref.shape[0]
+    span = 4 * rows
+    core = rank % 2
     factor = HEAD_DIMENSION**-0.5 * LOG2_E
     best[...] = jnp.full_like(best, FLOOR_SCORE)
     weighted[...] = jnp.zeros_like(weighted)
 
     def step(index, masked):
         start = pl.multiple_of(index * span, span)
-        keys = pairs_ref[pl.ds(start, span), :HEAD_DIMENSION]
-        values = pairs_ref[pl.ds(start, span), HEAD_DIMENSION:]
+        mine = mine_ref[pl.ds(start, span), :]
+        other = other_ref[pl.ds(start, span), :]
+        keys = jnp.where(core == 0, mine, other)
+        values = jnp.where(core == 0, other, mine)
         values = jnp.concatenate([values, jnp.ones_like(values)], axis=1)
         for head in range(heads):
+            cols = slice((first_head + head) * HEAD_DIMENSION, (first_head + head + 1) * HEAD_DIMENSION)
             for row in range(0, rows, QUERY_TILE):
                 tile = slice(row, row + QUERY_TILE)
-                query = query_ref[tile, head * HEAD_DIMENSION : (head + 1) * HEAD_DIMENSION]
                 scores = lax.dot_general(
-                    query, keys, (((1,), (1,)), ((), ())), preferred_element_type=jnp.float32
+                    query_ref[tile, cols],
+                    keys,
+                    (((1,), (1,)), ((), ())),
+                    preferred_element_type=jnp.float32,
                 )
                 if masked:
                     key_pos = lax.broadcasted_iota(jnp.int32, scores.shape, 1) + start
@@ -75,31 +120,82 @@
         ).astype(out_ref.dtype)
 
 
-def attend(rank, query, pairs):
-    rows, width = query.shape
-    heads = width // HEAD_DIMENSION
-    keys = pairs.shape[0]
-    span = min(KEY_SPAN, keys)
+def attend(rank, query, gathered, first_head, heads):
+    rows = query.shape[0]
+    width = heads * HEAD_DIMENSION
+    keys = gathered[0].shape[0]
     return pl.pallas_call(
-        functools.partial(attend_kernel, span=span, heads=heads),
-        out_shape=jax.ShapeDtypeStruct(query.shape, query.dtype),
-        in_specs=[
-            pl.BlockSpec(memory_space=pltpu.SMEM),
-            pl.BlockSpec(memory_space=pltpu.VMEM),
-            pl.BlockSpec(memory_space=pltpu.VMEM),
-        ],
+        functools.partial(attend_kernel, heads=heads, first_head=first_head),
+        out_shape=jax.ShapeDtypeStruct((rows, width), query.dtype),
+        in_specs=[pl.BlockSpec(memory_space=pltpu.SMEM)]
+        + [pl.BlockSpec(memory_space=pltpu.VMEM)] * (1 + len(gathered)),
         out_specs=pl.BlockSpec(memory_space=pltpu.VMEM),
         scratch_shapes=[
             pltpu.VMEM((heads, rows, HEAD_DIMENSION), jnp.float32),
             pltpu.VMEM((heads, rows, 2 * HEAD_DIMENSION), jnp.float32),
         ],
-        compiler_params=pltpu.CompilerParams(vmem_limit_bytes=40 * 2**20),
+        compiler_params=pltpu.CompilerParams(vmem_limit_bytes=32 * 2**20),
         cost_estimate=pl.CostEstimate(
-            flops=4 * rows * keys * width,
+            flops=8 * rows * keys * width,
             bytes_accessed=4 * rows * width + 4 * keys * HEAD_DIMENSION,
             transcendentals=rows * keys * heads,
         ),
-    )(rank, query, pairs)
+    )(rank, query, *gathered)
+
+
+def project_kernel(group_ref, *refs):
+    *part_refs, weight_ref, out_ref, total = refs
+    step = pl.program_id(0)
+    groups = len(part_refs) // 2
+    half = part_refs[0].shape[1]
+    weights = jnp.concatenate([weight_ref[0, i] for i in range(weight_ref.shape[1])], axis=1)
+
+    def product(index):
+        return jnp.dot(
+            part_refs[2 * index][...], weights[:half], preferred_element_type=jnp.float32
+        ) + jnp.dot(
+            part_refs[2 * index + 1][...], weights[half:], preferred_element_type=jnp.float32
+        )
+
+    for index in range(groups):
+
+        @pl.when(step == index)
+        def _(index=index):
+            if index == 0:
+                total[...] = product(index)
+            elif index < groups - 1:
+                total[...] += product(index)
+            else:
+                out_ref[...] = (total[...] + product(index)).astype(out_ref.dtype)
+
+
+def project(group, parts, weights):
+    rows, half = parts[0].shape
+    groups, blocks, depth, block_cols = weights.shape
+    cols = blocks * block_cols
+    return pl.pallas_call(
+        project_kernel,
+        grid_spec=pltpu.PrefetchScalarGridSpec(
+            num_scalar_prefetch=1,
+            grid=(groups,),
+            in_specs=[pl.BlockSpec((rows, half), lambda i, group: (0, 0))] * len(parts)
+            + [
+                pl.BlockSpec(
+                    (1, blocks, depth, block_cols),
+                    lambda i, group: ((group[0] + i) % groups, 0, 0, 0),
+                ),
+            ],
+            out_specs=pl.BlockSpec((rows, cols), lambda i, group: (0, 0)),
+            scratch_shapes=[pltpu.VMEM((rows, cols), jnp.float32)],
+        ),
+        out_shape=jax.ShapeDtypeStruct((rows, cols), jnp.bfloat16),
+        compiler_params=pltpu.CompilerParams(vmem_limit_bytes=32 * 2**20),
+        cost_estimate=pl.CostEstimate(
+            flops=2 * groups * rows * depth * cols,
+            bytes_accessed=2 * groups * depth * (rows + cols),
+            transcendentals=0,
+        ),
+    )(group, *parts, weights)
 
 
 def expert_kernel(rows_ref, gain_ref, gate_ref, up_ref, down_ref, out_ref, normed, hidden, *, wide):
@@ -202,20 +298,45 @@
     value_cols = lax.dynamic_slice_in_dim(
         value_weight, key_value_head * HEAD_DIMENSION, HEAD_DIMENSION, 1
     )
-    w_joint = lax.all_gather(
-        jnp.concatenate([w_query, key_cols, value_cols], axis=1), "fsdp", axis=0, tiled=True
-    )
-    normed = rms_scale(tokens, attn_gain)
-    joint = jnp.dot(normed, w_joint, preferred_element_type=jnp.float32).astype(jnp.bfloat16)
-    pairs = lax.all_gather(joint[:, head_width:], "fsdp", axis=0, tiled=True)
-    attended = attend(my_rank.astype(jnp.int32).reshape(1), joint[:, :head_width], pairs)
-    head_part = jnp.dot(
-        attended,
-        lax.all_gather(w_out, "fsdp", axis=1, tiled=True),
-        preferred_element_type=jnp.float32,
-    ).astype(jnp.bfloat16)
-    branch_cols = lax.psum_scatter(head_part, "grp", scatter_dimension=1, tiled=True)
-    attn_branch = lax.all_gather(branch_cols, "grp", axis=1, tiled=True)
+    core = my_rank % 2
+    w_query_all = lax.all_gather(w_query, "fsdp", axis=0, tiled=True)
+    normed = lax.optimization_barrier(rms_scale(tokens, attn_gain))
+    normed_other = to_other_core(normed)
+    w_own = jnp.where(core == 0, key_cols, value_cols)
+    w_given = to_other_core(jnp.where(core == 0, value_cols, key_cols))
+    w_pair, normed = lax.optimization_barrier((by_core(core, w_own, w_given), normed))
+    w_kv = from_chips(w_pair)
+
+    def project_kv(rows):
+        return jnp.dot(rows, w_kv, preferred_element_type=jnp.float32).astype(jnp.bfloat16)
+
+    kv_local = by_core(core, project_kv(normed), project_kv(normed_other))
+    w_out_block, w_kv = lax.optimization_barrier((w_out, w_kv))
+    w_turned = lax.ppermute(
+        w_out_block,
+        ("grp", "fsdp"),
+        [
+            (g * fsdp_size + f, f // 8 * fsdp_size + g * 8 + f % 8)
+            for g in range(head_groups)
+            for f in range(fsdp_size)
+        ],
+    )
+    w_turned, kv_local = lax.optimization_barrier((w_turned, kv_local))
+    w_out_all = lax.all_gather(w_turned, "fsdp", axis=0, tiled=True)
+    kv_mine = from_chips(kv_local)
+    gathered = (kv_mine, to_other_core(kv_mine))
+    query = jnp.dot(normed, w_query_all, preferred_element_type=jnp.float32).astype(jnp.bfloat16)
+    rank_array = my_rank.astype(jnp.int32).reshape(1)
+    half_heads = head_width // HEAD_DIMENSION // 2
+    first = attend(rank_array, query, gathered, 0, half_heads)
+    first_all = [first] + [from_group(first, shift) for shift in range(1, head_groups)]
+    second = attend(rank_array, query, gathered, half_heads, half_heads)
+    second_all = [second] + [from_group(second, shift) for shift in range(1, head_groups)]
+    branch_cols = project(
+        current_group.astype(jnp.int32).reshape(1),
+        [part for pair in zip(first_all, second_all) for part in pair],
+        w_out_all.reshape(head_groups, fsdp_size // head_groups, *w_out.shape),
+    )
     own_cols = lax.dynamic_slice_in_dim(tokens, current_group * col_width, col_width, 1)
     resid = (own_cols.astype(jnp.float32) + branch_cols.astype(jnp.float32)).astype(jnp.bfloat16)
 
@@ -251,9 +372,12 @@
         concat_axis=0,
         tiled=True,
     )
+    arrived, branch_cols = lax.optimization_barrier((arrived, branch_cols))
+    attn_branch = lax.all_gather(branch_cols, "grp", axis=1, tiled=True)
     result = run_expert(
         arrived.reshape(head_groups, fsdp_size * capacity, col_width), ffn_gain, w_gate_up, w_down
     )
+    result, attn_branch = lax.optimization_barrier((result, attn_branch))
     returned = lax.all_to_all(
         result.reshape(experts_all, capacity, col_width),
         ("grp", "fsdp"),

time: 452 us -> 381 us (0.84)
  waiting for transfers between devices: 274 us -> 117 us
  blocking collectives: 83.3 us -> 155 us
  starting transfers between devices: 8.7 us -> 22.6 us
  Pallas kernels: 29.6 us -> 37.4 us
    all_gather x3 -> x2, waiting for transfers between devices: 160 us -> 11 us  [the longest x1 11 us: on_device(): w_out_all = lax.all_gather(w_turned, 'fsdp', axis=0, tiled=True)]
    all_to_all x0 -> x2, blocking collectives: none -> 66.6 us  [from_chips(): lax.all_to_all(jnp.broadcast_to(rows[None], (chips, *rows.shape)), 'fsdp'...]
    all_gather x1, waiting for transfers between devices: 57.5 us -> 3.39 us  [on_device(): attn_branch = lax.all_gather(branch_cols, 'grp', axis=1, tiled=True)]
    all_to_all x1, waiting for transfers between devices: 29.4 us -> 76.2 us  [on_device(): lax.all_to_all(result.reshape(experts_all, capacity, col_width), ('grp',...]
    reduce_scatter x1 -> x0, waiting for transfers between devices: 26 us -> none  [on_device(): lax.psum_scatter(head_part, 'grp', scatter_dimension=1, tiled=True)]
    ppermute x0 -> x10, waiting for transfers between devices: none -> 25.6 us  [the longest x6 14.9 us: from_group(): lax.ppermute(rows, 'grp', [((i + shift) % SIDE, i) for i in range(SIDE)])]
    ppermute x0 -> x10, starting transfers between devices: none -> 12.3 us  [the longest x6 5.37 us: from_group(): lax.ppermute(rows, 'grp', [((i + shift) % SIDE, i) for i in range(SIDE)])]
    pallas_call x1 -> x3, Pallas kernels: 3.7 us -> 11.4 us  [the longest x2 7.13 us: attend(): pl.pallas_call(functools.partial(attend_kernel, heads=heads, first_head=f...]
  transfers between devices with their start and end apart: 6 -> 14, of which waited for: 6 -> 8; matrix products, arithmetic and copies ran while one was open for 2% -> 5% of each run, Pallas kernels for 1% -> 9%
where the time goes in v3:
time: 381 us; the launch traced here: 380 us
  blocking collectives  155 us (41%)
  waiting for transfers between devices  117 us (31%)
  Pallas kernels  37.4 us (10%)
  starting transfers between devices  22.6 us (6%)
  matrix products  21.4 us (6%)
  between operations  13.9 us (4%)
  other arithmetic  7.07 us (2%)
  local copies, waits for them, and re-layouts  6.28 us (2%)
    all_to_all x1, blocking collectives, on_device(): lax.all_to_all(outbound.reshape(experts_all, capacity, col_width), ('grp'...  88.1 us
    all_to_all x1, waiting for transfers between devices, on_device(): lax.all_to_all(result.reshape(experts_all, capacity, col_width), ('grp',...  76.2 us
    all_to_all x2, blocking collectives, from_chips(): lax.all_to_all(jnp.broadcast_to(rows[None], (chips, *rows.shape)), 'fsdp'...  66.6 us
    pallas_call x1, Pallas kernels, run_expert(): pl.pallas_call(functools.partial(expert_kernel, wide=wide), grid=(wide +...  26 us
    ppermute x6, waiting for transfers between devices, from_group(): lax.ppermute(rows, 'grp', [((i + shift) % SIDE, i) for i in range(SIDE)])  14.9 us
    all_gather x1, waiting for transfers between devices, on_device(): w_out_all = lax.all_gather(w_turned, 'fsdp', axis=0, tiled=True)  11 us
    all_to_all x1, starting transfers between devices, on_device(): lax.all_to_all(result.reshape(experts_all, capacity, col_width), ('grp',...  10.1 us
  transfers between devices with their start and end apart: 14, of which 8 were waited for; matrix products, arithmetic and copies ran while one was open for 5% of the time, Pallas kernels for 9%

profile of v3, /device:TPU:5, one launch (start us, length us, event | category | flops | bytes accessed | tf_op | source)
XLA Modules:
  0.0 380.3 jit_solution(8742870628118233483)
XLA Ops:
  8.0 2.1 fusion
  12.8 3.6 collective-permute-done
  16.7 26.3 %all_to_all.20 = bf16[16,256,128]{2,1,0:T(8,128)(2,1)S(1)} all-to-all(bf16[16,256,128]{2,1,0:T(8,128)(2,1)S(1)} %broadcast_in_dim.20), channel_id=1, replica_groups={{0,2,4,6,8,10,12,14,16,18,20,22,24,26,28,30},{1,3,5,7,9,11,13,15,17,19,..., dimensions={0} | all-to-all | bytes 2097152 | tf_op jit(solution)/shard_map/all_to_all | solution.py:40
  43.0 4.1 %collective-permute-start.1 = (bf16[1024,128]{1,0:T(8,128)(2,1)S(1)}, bf16[1024,128]{1,0:T(8,128)(2,1)S(1)}, u32[]{:S(2)}, u32[]{:S(2)}) collective-permute-start(bf16[1024,128]{1,0:T(8,128)(2,1)S(1)} %copy-done.10), channel_id=1, source_target_pairs={{0,0},{1,1},{2,2},{3,3},{4,4},{5,5},{6,6},{7,7},{8,32},{9,33},{10,... | collective-permute-start | bytes 786440 | tf_op jit(solution)/shard_map/ppermute | solution.py:315
  47.0 2.3 convolution_convert_fusion.3
  50.1 7.1 %collective-permute-done.1 = bf16[1024,128]{1,0:T(8,128)(2,1)S(1)} collective-permute-done((bf16[1024,128]{1,0:T(8,128)(2,1)S(1)}, bf16[1024,128]{1,0:T(8,128)(2,1)S(1)}, u32[]{:S(2)}, u32[]{:S(2)}) %collective-permute-start.1) | collective-permute-done | bytes 262176 | tf_op jit(solution)/shard_map/ppermute | solution.py:315
  58.4 40.3 %all_to_all.21 = bf16[16,512,128]{2,1,0:T(8,128)(2,1)S(1)} all-to-all(bf16[16,512,128]{2,1,0:T(8,128)(2,1)S(1)} %broadcast_in_dim.21), channel_id=1, replica_groups={{0,2,4,6,8,10,12,14,16,18,20,22,24,26,28,30},{1,3,5,7,9,11,13,15,17,19,..., dimensions={0} | all-to-all | bytes 4194304 | tf_op jit(solution)/shard_map/all_to_all | solution.py:40
  98.7 2.1 collective-permute-start.3
  102.6 6.4 %convolution_convert_fusion.1.query_ref = bf16[256,1024]{1,0:T(8,128)(2,1)S(1)} fusion(bf16[256,4096]{1,0:T(8,128)(2,1)} %fusion.2, bf16[4096,1024]{1,0:T(8,128)(2,1)} %all-gather.4.cloned.1.call-done), kind=kOutput, calls=%fused_computation.11 | convolution fusion | flops 2147745792 | bytes 11010048 | tf_op jit(solution)/shard_map/dot_general | solution.py:328
  109.0 3.5 shard_map.122.refs_0_
  114.6 3.7 shard_map.123.refs_1_
  121.5 4.6 %collective-permute-done.8.refs_6_ = bf16[256,512]{1,0:T(8,128)(2,1)S(1)} collective-permute-done((bf16[256,512]{1,0:T(8,128)(2,1)S(1)}, bf16[256,512]{1,0:T(8,128)(2,1)S(1)}, u32[]{:S(2)}, u32[]{:S(2)}) %collective-permute-start.8) | collective-permute-done | bytes 262176 | tf_op jit(solution)/shard_map/ppermute | solution.py:35
  126.2 2.6 convolution_compare_fusion
  128.8 8.7 %collective-permute-done.9.refs_7_ = bf16[256,512]{1,0:T(8,128)(2,1)S(1)} collective-permute-done((bf16[256,512]{1,0:T(8,128)(2,1)S(1)}, bf16[256,512]{1,0:T(8,128)(2,1)S(1)}, u32[]{:S(2)}, u32[]{:S(2)}) %collective-permute-start.9) | collective-permute-done | bytes 262176 | tf_op jit(solution)/shard_map/ppermute | solution.py:35
  139.1 11.0 %all-gather.6.cloned.1.call-done = bf16[32768,128]{1,0:T(8,128)(2,1)} async-done(((bf16[1024,128]{1,0:T(8,128)(2,1)}), bf16[32768,128]{1,0:T(8,128)(2,1)}) %all-gather.6.cloned.1.call-update) | async-done | bytes 8388624 | tf_op jit(solution)/shard_map/all_gather | solution.py:325
  150.0 3.4 copy-done
  153.4 4.3 %shard_map.124 = bf16[256,1024]{1,0:T(8,128)(2,1)} custom-call(s32[1]{0:T(128)} %bitcast.group_ref, bf16[256,512]{1,0:T(8,128)(2,1)S(1)} %shard_map.122.refs_0_, bf16[256,512]{1,0:T(8,128)(2,1)S(1)} %shard_map.123.refs_1_, bf16[256,512]{1,0:T(8,128)(2,1)S(1)} %collective-permute-done.4.refs_2_, bf16[256,512]{1,0:T(8,128)(2,1)S(1)} %collective-permute-done.5.refs_3_, ...), custom_call_target="tpu_custom_call" | custom-call | flops 2147483648 | bytes 10485760 | tf_op jit(solution)/shard_map/pallas_call | solution.py:176
  157.7 3.3 convolution_convert_fusion
  161.0 88.1 %all_to_all.22 = bf16[128,24,1024]{2,1,0:T(8,128)(2,1)} all-to-all(bf16[128,24,1024]{2,1,0:T(8,128)(2,1)S(1)} %bitcast.24), channel_id=1, replica_groups=mesh['grp'=4,'fsdp'=32] {'grp','fsdp'}, dimensions={0} | all-to-all | bytes 12582912 | tf_op jit(solution)/shard_map/all_to_all | solution.py:368
  249.1 26.0 %shard_map.125 = bf16[4,768,1024]{2,1,0:T(8,128)(2,1)} custom-call(bf16[4,768,1024]{2,1,0:T(8,128)(2,1)} %bitcast.28, f32[4,1,1024]{2,1,0:T(1,128)} %bitcast.29, bf16[1,4096,1536]{2,1,0:T(8,128)(2,1)} %up_ref.1, bf16[1,4096,1536]{2,1,0:T(8,128)(2,1)} %up_ref.1, bf16[1,768,4096]{2,1,0:T(8,128)(2,1)} %down_ref.1), custom_call_target="tpu_custom_call" | custom-call | flops 14495514624 | bytes 31457280 | tf_op jit(solution)/shard_map/pallas_call | solution.py:249
  275.0 3.4 all-gather.8.cloned.1.call-done
  278.4 10.1 %all-to-all-start.3 = ((bf16[128,24,1024]{2,1,0:T(8,128)(2,1)}), bf16[128,24,1024]{2,1,0:T(8,128)(2,1)}, u32[]{:S(2)}, u32[]{:S(2)}) async-start(bf16[128,24,1024]{2,1,0:T(8,128)(2,1)} %bitcast.27), calls=%async_computation.3 | async-start | bytes 12582912 | tf_op jit(solution)/shard_map/all_to_all | solution.py:381
  290.0 76.2 %all-to-all-done.3 = bf16[128,24,1024]{2,1,0:T(8,128)(2,1)} async-done(((bf16[128,24,1024]{2,1,0:T(8,128)(2,1)}), bf16[128,24,1024]{2,1,0:T(8,128)(2,1)}, u32[]{:S(2)}, u32[]{:S(2)}) %all-to-all-start.3) | async-done | bytes 6291488 | tf_op jit(solution)/shard_map/all_to_all | solution.py:381
  366.3 6.2 %add_convert_fusion = bf16[256,1024]{1,0:T(8,128)(2,1)} fusion(bf16[3072,1024]{1,0:T(8,128)(2,1)} %bitcast.9, pred[256,3072]{1,0:T(32,128)(4,1)S(1)} %copy-done.3, bf16[256,128]{1,0:T(8,128)(2,1)S(1)} %fusion.11, s32[3072]{0:T(1024)S(1)} %get-tuple-element.24, bf16[256,1024]{1,0:T(8,128)(2,1)} %shard_map.124, bf16[256,4096]{1,0:T(8,128)(2,1)} %param.11, ...), kind=kOutput, calls=%fused_computation.16 | convolution fusion | flops 1815740416 | bytes 8728580 | tf_op jit(solution)/shard_map/dot_general | solution.py:388
  (57 shorter events, 17.1 us)
Async XLA Ops:
  7.2 2.9 copy-start.1
  7.2 2.9 copy-start.7
  7.2 95.4 %all-gather.4.cloned.1.call-start = ((), (), s32[]{:S(2)}) async-start(), calls=%async_computation.4 | async-start | bytes 8650752 | tf_op jit(solution)/shard_map/all_gather | solution.py:302
  7.9 142.1 %all-gather.6.cloned.1.call-start = ((), (), s32[]{:S(2)}) async-start(), calls=%async_computation.5 | async-start | bytes 8650752 | tf_op jit(solution)/shard_map/all_gather | solution.py:325
  10.1 2.7 copy-start.5
  10.1 2.6 copy-start.6
  12.1 30.9 %copy-start.10 = (bf16[1024,128]{1,0:T(8,128)(2,1)S(1)}, bf16[1024,128]{1,0:T(8,128)(2,1)}, u32[]{:S(2)}) copy-start(bf16[1024,128]{1,0:T(8,128)(2,1)} %param.17) | copy-start | bytes 786436
  12.1 37.3 %collective-permute-start.2 = (bf16[256,4096]{1,0:T(8,128)(2,1)}, bf16[256,4096]{1,0:T(8,128)(2,1)S(1)}, u32[]{:S(2)}, u32[]{:S(2)}) collective-permute-start(bf16[256,4096]{1,0:T(8,128)(2,1)} %fusion.2), channel_id=1, source_target_pairs={{0,1},{1,0},{2,3},{3,2},{4,5},{5,4},{6,7},{7,6},{8,9},{9,8},{10,11... | collective-permute-start | bytes 6291464 | tf_op jit(solution)/shard_map/ppermute | solution.py:31
  12.8 3.7 collective-permute-start
  43.0 14.2 %collective-permute-start.1 = (bf16[1024,128]{1,0:T(8,128)(2,1)S(1)}, bf16[1024,128]{1,0:T(8,128)(2,1)S(1)}, u32[]{:S(2)}, u32[]{:S(2)}) collective-permute-start(bf16[1024,128]{1,0:T(8,128)(2,1)S(1)} %copy-done.10), channel_id=1, source_target_pairs={{0,0},{1,1},{2,2},{3,3},{4,4},{5,5},{6,6},{7,7},{8,32},{9,33},{10,... | collective-permute-start | bytes 786440 | tf_op jit(solution)/shard_map/ppermute | solution.py:315
  57.9 220.5 %all-gather.8.cloned.1.call-start = ((), (), s32[]{:S(2)}) async-start(), calls=%async_computation.6 | async-start | bytes 2621440 | tf_op jit(solution)/shard_map/all_gather | solution.py:376
  58.4 42.4 %copy-start.8 = (s32[256,8]{0,1:T(8,128)S(1)}, s32[256,8]{0,1:T(8,128)}, u32[]{:S(2)}) copy-start(s32[256,8]{0,1:T(8,128)} %param.18) | copy-start | bytes 24580
  98.7 10.3 %collective-permute-start.3 = (bf16[8192,128]{1,0:T(8,128)(2,1)S(1)}, bf16[8192,128]{1,0:T(8,128)(2,1)}, u32[]{:S(2)}, u32[]{:S(2)}) collective-permute-start(bf16[8192,128]{1,0:T(8,128)(2,1)S(1)} %bitcast.21), channel_id=1, source_target_pairs={{0,1},{1,0},{2,3},{3,2},{4,5},{5,4},{6,7},{7,6},{8,9},{9,8},{10,11... | collective-permute-start | bytes 6291464 | tf_op jit(solution)/shard_map/ppermute | solution.py:31
  112.5 13.7 %collective-permute-start.8 = (bf16[256,512]{1,0:T(8,128)(2,1)S(1)}, bf16[256,512]{1,0:T(8,128)(2,1)S(1)}, u32[]{:S(2)}, u32[]{:S(2)}) collective-permute-start(bf16[256,512]{1,0:T(8,128)(2,1)S(1)} %shard_map.122.refs_0_), channel_id=1, source_target_pairs={{96,0},{0,32},{32,64},{64,96},{97,1},{1,33},{33,65},{65,97},{98,2}... | collective-permute-start | bytes 786440 | tf_op jit(solution)/shard_map/ppermute | solution.py:35
  113.4 15.4 %collective-permute-start.6 = (bf16[256,512]{1,0:T(8,128)(2,1)S(1)}, bf16[256,512]{1,0:T(8,128)(2,1)S(1)}, u32[]{:S(2)}, u32[]{:S(2)}) collective-permute-start(bf16[256,512]{1,0:T(8,128)(2,1)S(1)} %shard_map.122.refs_0_), channel_id=1, source_target_pairs={{64,0},{96,32},{0,64},{32,96},{65,1},{97,33},{1,65},{33,97},{66,2}... | collective-permute-start | bytes 786440 | tf_op jit(solution)/shard_map/ppermute | solution.py:35
  113.4 15.4 %collective-permute-start.4 = (bf16[256,512]{1,0:T(8,128)(2,1)S(1)}, bf16[256,512]{1,0:T(8,128)(2,1)S(1)}, u32[]{:S(2)}, u32[]{:S(2)}) collective-permute-start(bf16[256,512]{1,0:T(8,128)(2,1)S(1)} %shard_map.122.refs_0_), channel_id=1, source_target_pairs={{32,0},{64,32},{96,64},{0,96},{33,1},{65,33},{97,65},{1,97},{34,2}... | collective-permute-start | bytes 786440 | tf_op jit(solution)/shard_map/ppermute | solution.py:35
  118.3 19.2 %collective-permute-start.9 = (bf16[256,512]{1,0:T(8,128)(2,1)S(1)}, bf16[256,512]{1,0:T(8,128)(2,1)S(1)}, u32[]{:S(2)}, u32[]{:S(2)}) collective-permute-start(bf16[256,512]{1,0:T(8,128)(2,1)S(1)} %shard_map.123.refs_1_), channel_id=1, source_target_pairs={{96,0},{0,32},{32,64},{64,96},{97,1},{1,33},{33,65},{65,97},{98,2}... | collective-permute-start | bytes 786440 | tf_op jit(solution)/shard_map/ppermute | solution.py:35
  119.6 17.9 %collective-permute-start.7 = (bf16[256,512]{1,0:T(8,128)(2,1)S(1)}, bf16[256,512]{1,0:T(8,128)(2,1)S(1)}, u32[]{:S(2)}, u32[]{:S(2)}) collective-permute-start(bf16[256,512]{1,0:T(8,128)(2,1)S(1)} %shard_map.123.refs_1_), channel_id=1, source_target_pairs={{64,0},{96,32},{0,64},{32,96},{65,1},{97,33},{1,65},{33,97},{66,2}... | collective-permute-start | bytes 786440 | tf_op jit(solution)/shard_map/ppermute | solution.py:35
  126.2 12.9 %collective-permute-start.5 = (bf16[256,512]{1,0:T(8,128)(2,1)S(1)}, bf16[256,512]{1,0:T(8,128)(2,1)S(1)}, u32[]{:S(2)}, u32[]{:S(2)}) collective-permute-start(bf16[256,512]{1,0:T(8,128)(2,1)S(1)} %shard_map.123.refs_1_), channel_id=1, source_target_pairs={{32,0},{64,32},{96,64},{0,96},{33,1},{65,33},{97,65},{1,97},{34,2}... | collective-permute-start | bytes 786440 | tf_op jit(solution)/shard_map/ppermute | solution.py:35
  150.0 3.4 copy-start
  278.4 10.2 %copy-start.9 = (bf16[256,8]{0,1:T(8,128)(2,1)S(1)}, bf16[256,8]{0,1:T(8,128)(2,1)}, u32[]{:S(2)}) copy-start(bf16[256,8]{0,1:T(8,128)(2,1)} %param.19) | copy-start | bytes 12292
  278.4 87.8 %copy-start.3 = (pred[256,3072]{1,0:T(32,128)(4,1)S(1)}, pred[256,3072]{1,0:T(32,128)(4,1)}, u32[]{:S(2)}) copy-start(pred[256,3072]{1,0:T(32,128)(4,1)} %convolution_compare_fusion) | copy-start | bytes 2359300
  278.4 87.8 %all-to-all-start.3 = ((bf16[128,24,1024]{2,1,0:T(8,128)(2,1)}), bf16[128,24,1024]{2,1,0:T(8,128)(2,1)}, u32[]{:S(2)}, u32[]{:S(2)}) async-start(bf16[128,24,1024]{2,1,0:T(8,128)(2,1)} %bitcast.27), calls=%async_computation.3 | async-start | bytes 12582912 | tf_op jit(solution)/shard_map/all_to_all | solution.py:381
  366.3 6.2 %copy-start.2 = (bf16[256,4096]{1,0:T(8,128)(2,1)S(1)}, bf16[256,4096]{1,0:T(8,128)(2,1)}, u32[]{:S(2)}) copy-start(bf16[256,4096]{1,0:T(8,128)(2,1)} %all-gather.8.cloned.1.call-done) | copy-start | bytes 6291460
  (1 other events, 0.7 us)
Sparse Core Ops, SparseCore 0:
  10.3 82.2 all-gather.3
  95.4 54.5 all-gather.5
  249.2 29.1 all-gather.7

commit v4 on v3

--- a/solution.py
+++ b/solution.py
@@ -16,6 +16,7 @@
 FLOOR_SCORE = -1e30
 LOG2_E = 1.4426950408889634
 SIDE = 4
+PIECE_HEADS = 4
 QUERY_TILE = 128
 HIDDEN_TILE = 256
 NORM_TILE = 64
@@ -143,59 +144,55 @@
     )(rank, query, *gathered)
 
 
-def project_kernel(group_ref, *refs):
-    *part_refs, weight_ref, out_ref, total = refs
+def project_kernel(group_ref, *refs, groups):
+    part_refs, (weight_ref, *before, out_ref, total) = refs[:groups], refs[groups:]
     step = pl.program_id(0)
-    groups = len(part_refs) // 2
-    half = part_refs[0].shape[1]
     weights = jnp.concatenate([weight_ref[0, i] for i in range(weight_ref.shape[1])], axis=1)
-
-    def product(index):
-        return jnp.dot(
-            part_refs[2 * index][...], weights[:half], preferred_element_type=jnp.float32
-        ) + jnp.dot(
-            part_refs[2 * index + 1][...], weights[half:], preferred_element_type=jnp.float32
-        )
 
     for index in range(groups):
 
         @pl.when(step == index)
         def _(index=index):
-            if index == 0:
-                total[...] = product(index)
-            elif index < groups - 1:
-                total[...] += product(index)
+            product = jnp.dot(part_refs[index][...], weights, preferred_element_type=jnp.float32)
+            if index > 0:
+                product += total[...]
+            elif before:
+                product += before[0][...]
+            if index < groups - 1:
+                total[...] = product
             else:
-                out_ref[...] = (total[...] + product(index)).astype(out_ref.dtype)
-
-
-def project(group, parts, weights):
-    rows, half = parts[0].shape
-    groups, blocks, depth, block_cols = weights.shape
+                out_ref[...] = product.astype(out_ref.dtype)
+
+
+def project(group, parts, weights, piece, before, out_type):
+    groups, blocks, _, block_cols = weights.shape
+    rows, depth = parts[0].shape
     cols = blocks * block_cols
+    whole = pl.BlockSpec((rows, cols), lambda i, group: (0, 0))
     return pl.pallas_call(
-        project_kernel,
+        functools.partial(project_kernel, groups=groups),
         grid_spec=pltpu.PrefetchScalarGridSpec(
             num_scalar_prefetch=1,
             grid=(groups,),
-            in_specs=[pl.BlockSpec((rows, half), lambda i, group: (0, 0))] * len(parts)
+            in_specs=[pl.BlockSpec((rows, depth), lambda i, group: (0, 0))] * groups
             + [
                 pl.BlockSpec(
                     (1, blocks, depth, block_cols),
-                    lambda i, group: ((group[0] + i) % groups, 0, 0, 0),
+                    lambda i, group: ((group[0] + i) % groups, 0, piece, 0),
                 ),
-            ],
-            out_specs=pl.BlockSpec((rows, cols), lambda i, group: (0, 0)),
+            ]
+            + [whole] * len(before),
+            out_specs=whole,
             scratch_shapes=[pltpu.VMEM((rows, cols), jnp.float32)],
         ),
-        out_shape=jax.ShapeDtypeStruct((rows, cols), jnp.bfloat16),
-        compiler_params=pltpu.CompilerParams(vmem_limit_bytes=32 * 2**20),
+        out_shape=jax.ShapeDtypeStruct((rows, cols), out_type),
+        compiler_params=pltpu.CompilerParams(vmem_limit_bytes=52 * 2**20),
         cost_estimate=pl.CostEstimate(
             flops=2 * groups * rows * depth * cols,
             bytes_accessed=2 * groups * depth * (rows + cols),
             transcendentals=0,
         ),
-    )(group, *parts, weights)
+    )(group, *parts, weights, *before)
 
 
 def expert_kernel(rows_ref, gain_ref, gate_ref, up_ref, down_ref, out_ref, normed, hidden, *, wide):
@@ -302,10 +299,10 @@
     w_query_all = lax.all_gather(w_query, "fsdp", axis=0, tiled=True)
     normed = lax.optimization_barrier(rms_scale(tokens, attn_gain))
     normed_other = to_other_core(normed)
-    w_own = jnp.where(core == 0, key_cols, value_cols)
-    w_given = to_other_core(jnp.where(core == 0, value_cols, key_cols))
-    w_pair, normed = lax.optimization_barrier((by_core(core, w_own, w_given), normed))
-    w_kv = from_chips(w_pair)
+    w_both, normed = lax.optimization_barrier((jnp.stack([key_cols, value_cols]), normed))
+    w_kv = lax.all_to_all(
+        jnp.tile(w_both, (fsdp_size // 2, 1, 1)), "fsdp", split_axis=0, concat_axis=0, tiled=True
+    ).reshape(model_width, HEAD_DIMENSION)
 
     def project_kv(rows):
         return jnp.dot(rows, w_kv, preferred_element_type=jnp.float32).astype(jnp.bfloat16)
@@ -324,19 +321,21 @@
     w_turned, kv_local = lax.optimization_barrier((w_turned, kv_local))
     w_out_all = lax.all_gather(w_turned, "fsdp", axis=0, tiled=True)
     kv_mine = from_chips(kv_local)
+    query = jnp.dot(normed, w_query_all, preferred_element_type=jnp.float32).astype(jnp.bfloat16)
+    kv_mine, query = lax.optimization_barrier((kv_mine, query))
     gathered = (kv_mine, to_other_core(kv_mine))
-    query = jnp.dot(normed, w_query_all, preferred_element_type=jnp.float32).astype(jnp.bfloat16)
     rank_array = my_rank.astype(jnp.int32).reshape(1)
-    half_heads = head_width // HEAD_DIMENSION // 2
-    first = attend(rank_array, query, gathered, 0, half_heads)
-    first_all = [first] + [from_group(first, shift) for shift in range(1, head_groups)]
-    second = attend(rank_array, query, gathered, half_heads, half_heads)
-    second_all = [second] + [from_group(second, shift) for shift in range(1, head_groups)]
-    branch_cols = project(
-        current_group.astype(jnp.int32).reshape(1),
-        [part for pair in zip(first_all, second_all) for part in pair],
-        w_out_all.reshape(head_groups, fsdp_size // head_groups, *w_out.shape),
-    )
+    pieces = []
+    for head in range(0, head_width // HEAD_DIMENSION, PIECE_HEADS):
+        piece = attend(rank_array, query, gathered, head, PIECE_HEADS)
+        pieces.append([piece] + [from_group(piece, shift) for shift in range(1, head_groups)])
+    w_out_cols = w_out_all.reshape(head_groups, fsdp_size // head_groups, *w_out.shape)
+    group_array = current_group.astype(jnp.int32).reshape(1)
+    before = []
+    for index, piece in enumerate(pieces):
+        out_type = jnp.bfloat16 if index == len(pieces) - 1 else jnp.float32
+        before = [project(group_array, piece, w_out_cols, index, before, out_type)]
+    (branch_cols,) = before
     own_cols = lax.dynamic_slice_in_dim(tokens, current_group * col_width, col_width, 1)
     resid = (own_cols.astype(jnp.float32) + branch_cols.astype(jnp.float32)).astype(jnp.bfloat16)
 
@@ -360,7 +359,7 @@
     prob_slots = jnp.dot(
         named_probs.astype(jnp.bfloat16), spread, preferred_element_type=jnp.float32
     )
-    mixing = jnp.where(slot_match, prob_slots, 0.0).astype(jnp.bfloat16)
+    mixing = lax.optimization_barrier(jnp.where(slot_match, prob_slots, 0.0).astype(jnp.bfloat16))
 
     outbound = lax.dot_general(
         chosen, resid, (((0,), (0,)), ((), ())), preferred_element_type=jnp.float32
@@ -373,11 +372,18 @@
         tiled=True,
     )
     arrived, branch_cols = lax.optimization_barrier((arrived, branch_cols))
-    attn_branch = lax.all_gather(branch_cols, "grp", axis=1, tiled=True)
+    blocks = [branch_cols] + [from_group(branch_cols, shift) for shift in range(1, head_groups)]
     result = run_expert(
         arrived.reshape(head_groups, fsdp_size * capacity, col_width), ffn_gain, w_gate_up, w_down
     )
-    result, attn_branch = lax.optimization_barrier((result, attn_branch))
+    result, blocks = lax.optimization_barrier((result, blocks))
+    attn_branch = jnp.concatenate(
+        [
+            lax.select_n(lax.rem(group + head_groups - current_group, head_groups), *blocks)
+            for group in range(head_groups)
+        ],
+        axis=1,
+    )
     returned = lax.all_to_all(
         result.reshape(experts_all, capacity, col_width),
         ("grp", "fsdp"),

time: 381 us -> 372 us (0.976)
  blocking collectives: 155 us -> 84.3 us
  waiting for transfers between devices: 117 us -> 150 us
  starting transfers between devices: 22.6 us -> 43.3 us
  Pallas kernels: 37.4 us -> 42.9 us
    all_to_all x2 -> x0, blocking collectives: 66.6 us -> none  [from_chips(): lax.all_to_all(jnp.broadcast_to(rows[None], (chips, *rows.shape)), 'fsdp'...]
    all_to_all x0 -> x2, waiting for transfers between devices: none -> 23.5 us  [the longest x1 20.5 us: on_device(): lax.all_to_all(jnp.tile(w_both, (fsdp_size // 2, 1, 1)), 'fsdp', split_ax...]
    all_gather x1, waiting for transfers between devices: 0.01 us -> 22 us  [on_device(): w_query_all = lax.all_gather(w_query, 'fsdp', axis=0, tiled=True)]
    ppermute x6 -> x9, waiting for transfers between devices: 14.9 us -> 0.02 us  [from_group(): lax.ppermute(rows, 'grp', [((i + shift) % SIDE, i) for i in range(SIDE)])]
    ppermute x6 -> x9, starting transfers between devices: 5.37 us -> 17.6 us  [from_group(): lax.ppermute(rows, 'grp', [((i + shift) % SIDE, i) for i in range(SIDE)])]
    all_to_all x0 -> x2, starting transfers between devices: none -> 11.9 us  [the longest x1 8.21 us: on_device(): lax.all_to_all(jnp.tile(w_both, (fsdp_size // 2, 1, 1)), 'fsdp', split_ax...]
    all_gather x1, waiting for transfers between devices: 11 us -> 16.5 us  [on_device(): w_out_all = lax.all_gather(w_turned, 'fsdp', axis=0, tiled=True)]
    pallas_call x1 -> x2, Pallas kernels: 4.27 us -> 9.7 us  [project(): pl.pallas_call(functools.partial(project_kernel, groups=groups), grid_spe...]
  transfers between devices with their start and end apart: 14 -> 17, of which waited for: 8 -> 7; matrix products, arithmetic and copies ran while one was open for 5% -> 7% of each run, Pallas kernels for 9% -> 10%
where the time goes in v4:
time: 372 us; the launch traced here: 371 us
  waiting for transfers between devices  150 us (40%)
  blocking collectives  84.3 us (23%)
  starting transfers between devices  43.3 us (12%)
  Pallas kernels  42.9 us (12%)
  matrix products  21.1 us (6%)
  between operations  14.4 us (4%)
  other arithmetic  8.79 us (2%)
  local copies, waits for them, and re-layouts  6.94 us (2%)
    all_to_all x1, blocking collectives, on_device(): lax.all_to_all(outbound.reshape(experts_all, capacity, col_width), ('grp'...  84.3 us
    all_to_all x1, waiting for transfers between devices, on_device(): lax.all_to_all(result.reshape(experts_all, capacity, col_width), ('grp',...  73.6 us
    pallas_call x1, Pallas kernels, run_expert(): pl.pallas_call(functools.partial(expert_kernel, wide=wide), grid=(wide +...  25.9 us
    all_gather x1, waiting for transfers between devices, on_device(): w_query_all = lax.all_gather(w_query, 'fsdp', axis=0, tiled=True)  22 us
    all_to_all x1, waiting for transfers between devices, on_device(): lax.all_to_all(jnp.tile(w_both, (fsdp_size // 2, 1, 1)), 'fsdp', split_ax...  20.5 us
    ppermute x9, starting transfers between devices, from_group(): lax.ppermute(rows, 'grp', [((i + shift) % SIDE, i) for i in range(SIDE)])  17.6 us
    all_gather x1, waiting for transfers between devices, on_device(): w_out_all = lax.all_gather(w_turned, 'fsdp', axis=0, tiled=True)  16.5 us
    ppermute x1, waiting for transfers between devices, on_device(): lax.ppermute(w_out_block, ('grp', 'fsdp'), [(g * fsdp_size + f, f // 8 *...  11.1 us
  transfers between devices with their start and end apart: 17, of which 7 were waited for; matrix products, arithmetic and copies ran while one was open for 7% of the time, Pallas kernels for 10%

profile of v4, /device:TPU:5, one launch (start us, length us, event | category | flops | bytes accessed | tf_op | source)
XLA Modules:
  0.0 371.3 jit_solution(4006790828621131114)
XLA Ops:
  13.9 8.2 %all-to-all-start = ((bf16[32,128,128]{2,1,0:T(8,128)(2,1)}), bf16[32,128,128]{2,1,0:T(8,128)(2,1)S(1)}, u32[]{:S(2)}, u32[]{:S(2)}) async-start(bf16[32,128,128]{2,1,0:T(8,128)(2,1)} %bitcast.4), calls=%async_computation | async-start | bytes 2097152 | tf_op jit(solution)/shard_map/all_to_all | solution.py:303
  22.2 20.5 %all-to-all-done = bf16[32,128,128]{2,1,0:T(8,128)(2,1)S(1)} async-done(((bf16[32,128,128]{2,1,0:T(8,128)(2,1)}), bf16[32,128,128]{2,1,0:T(8,128)(2,1)S(1)}, u32[]{:S(2)}, u32[]{:S(2)}) %all-to-all-start) | async-done | bytes 1048608 | tf_op jit(solution)/shard_map/all_to_all | solution.py:303
  42.7 3.3 collective-permute-start
  46.0 2.3 convolution_convert_fusion.3
  49.1 11.1 %collective-permute-done = bf16[1024,128]{1,0:T(8,128)(2,1)S(1)} collective-permute-done((bf16[1024,128]{1,0:T(8,128)(2,1)}, bf16[1024,128]{1,0:T(8,128)(2,1)S(1)}, u32[]{:S(2)}, u32[]{:S(2)}) %collective-permute-start) | collective-permute-done | bytes 262176 | tf_op jit(solution)/shard_map/ppermute | solution.py:312
  62.7 3.7 %all-to-all-start.1 = ((bf16[16,512,128]{2,1,0:T(8,128)(2,1)}), bf16[16,512,128]{2,1,0:T(8,128)(2,1)S(1)}, u32[]{:S(2)}, u32[]{:S(2)}) async-start(bf16[16,512,128]{2,1,0:T(8,128)(2,1)} %broadcast_in_dim.18), calls=%async_computation.1 | async-start | bytes 4194304 | tf_op jit(solution)/shard_map/all_to_all | solution.py:41
  66.4 22.0 %all-gather.3.cloned.1.call-done = bf16[4096,1024]{1,0:T(8,128)(2,1)} async-done(((bf16[128,1024]{1,0:T(8,128)(2,1)}), bf16[4096,1024]{1,0:T(8,128)(2,1)}) %all-gather.3.cloned.1.call-update) | async-done | bytes 8388624 | tf_op jit(solution)/shard_map/all_gather | solution.py:299
  88.4 6.3 %convolution_convert_fusion.1.query_ref = bf16[256,1024]{1,0:T(8,128)(2,1)S(1)} fusion(bf16[256,4096]{1,0:T(8,128)(2,1)} %fusion.2, bf16[4096,1024]{1,0:T(8,128)(2,1)} %all-gather.3.cloned.1.call-done), kind=kOutput, calls=%fused_computation.11 | convolution fusion | flops 2147745792 | bytes 11010048 | tf_op jit(solution)/shard_map/dot_general | solution.py:324
  94.7 3.1 all-to-all-done.1
  100.8 2.1 collective-permute-done.2.other_ref
  102.9 3.6 shard_map.123.refs_0_
  109.3 4.5 %collective-permute-start.7 = (bf16[256,512]{1,0:T(8,128)(2,1)S(1)}, bf16[256,512]{1,0:T(8,128)(2,1)S(1)}, u32[]{:S(2)}, u32[]{:S(2)}) collective-permute-start(bf16[256,512]{1,0:T(8,128)(2,1)S(1)} %shard_map.123.refs_0_), channel_id=1, source_target_pairs={{64,0},{96,32},{0,64},{32,96},{65,1},{97,33},{1,65},{33,97},{66,2}... | collective-permute-start | bytes 786440 | tf_op jit(solution)/shard_map/ppermute | solution.py:36
  114.8 3.7 shard_map.122.refs_0_
  121.3 5.1 %collective-permute-start.5 = (bf16[256,512]{1,0:T(8,128)(2,1)S(1)}, bf16[256,512]{1,0:T(8,128)(2,1)S(1)}, u32[]{:S(2)}, u32[]{:S(2)}) collective-permute-start(bf16[256,512]{1,0:T(8,128)(2,1)S(1)} %shard_map.122.refs_0_), channel_id=1, source_target_pairs={{96,0},{0,32},{32,64},{64,96},{97,1},{1,33},{33,65},{65,97},{98,2}... | collective-permute-start | bytes 786440 | tf_op jit(solution)/shard_map/ppermute | solution.py:36
  126.4 2.7 convolution_compare_fusion
  129.0 16.5 %all-gather.5.cloned.1.call-done = bf16[32768,128]{1,0:T(8,128)(2,1)} async-done(((bf16[1024,128]{1,0:T(8,128)(2,1)}), bf16[32768,128]{1,0:T(8,128)(2,1)}) %all-gather.5.cloned.1.call-update) | async-done | bytes 8388624 | tf_op jit(solution)/shard_map/all_gather | solution.py:322
  145.5 5.2 %shard_map.124.refs_5_ = f32[256,1024]{1,0:T(8,128)} custom-call(s32[1]{0:T(128)} %bitcast.group_ref, bf16[256,512]{1,0:T(8,128)(2,1)S(1)} %shard_map.123.refs_0_, bf16[256,512]{1,0:T(8,128)(2,1)S(1)} %collective-permute-done.6.refs_1_, bf16[256,512]{1,0:T(8,128)(2,1)S(1)} %collective-permute-done.7.refs_2_, ...), custom_call_target="tpu_custom_call" | custom-call | flops 1073741824 | bytes 5242880 | tf_op jit(solution)/shard_map/pallas_call | solution.py:172
  150.7 4.6 %shard_map.125 = bf16[256,1024]{1,0:T(8,128)(2,1)S(1)} custom-call(s32[1]{0:T(128)} %bitcast.group_ref, bf16[256,512]{1,0:T(8,128)(2,1)S(1)} %shard_map.122.refs_0_, bf16[256,512]{1,0:T(8,128)(2,1)S(1)} %collective-permute-done.3.refs_1_, bf16[256,512]{1,0:T(8,128)(2,1)S(1)} %collective-permute-done.4.refs_2_, ...), custom_call_target="tpu_custom_call" | custom-call | flops 1073741824 | bytes 5242880 | tf_op jit(solution)/shard_map/pallas_call | solution.py:172
  155.3 2.9 convolution_convert_fusion
  158.2 84.3 %all_to_all.20 = bf16[128,24,1024]{2,1,0:T(8,128)(2,1)} all-to-all(bf16[128,24,1024]{2,1,0:T(8,128)(2,1)S(1)} %bitcast.29), channel_id=1, replica_groups=mesh['grp'=4,'fsdp'=32] {'grp','fsdp'}, dimensions={0} | all-to-all | bytes 12582912 | tf_op jit(solution)/shard_map/all_to_all | solution.py:367
  245.8 25.9 %shard_map.126 = bf16[4,768,1024]{2,1,0:T(8,128)(2,1)} custom-call(bf16[4,768,1024]{2,1,0:T(8,128)(2,1)} %bitcast.35, f32[4,1,1024]{2,1,0:T(1,128)} %bitcast.36, bf16[1,4096,1536]{2,1,0:T(8,128)(2,1)} %up_ref.1, bf16[1,4096,1536]{2,1,0:T(8,128)(2,1)} %up_ref.1, bf16[1,768,4096]{2,1,0:T(8,128)(2,1)} %down_ref.1), custom_call_target="tpu_custom_call" | custom-call | flops 14495514624 | bytes 31457280 | tf_op jit(solution)/shard_map/pallas_call | solution.py:246
  272.9 8.4 %all-to-all-start.3 = ((bf16[128,24,1024]{2,1,0:T(8,128)(2,1)}), bf16[128,24,1024]{2,1,0:T(8,128)(2,1)}, u32[]{:S(2)}, u32[]{:S(2)}) async-start(bf16[128,24,1024]{2,1,0:T(8,128)(2,1)} %bitcast.34), calls=%async_computation.3 | async-start | bytes 12582912 | tf_op jit(solution)/shard_map/all_to_all | solution.py:387
  285.4 73.6 %all-to-all-done.3 = bf16[128,24,1024]{2,1,0:T(8,128)(2,1)} async-done(((bf16[128,24,1024]{2,1,0:T(8,128)(2,1)}), bf16[128,24,1024]{2,1,0:T(8,128)(2,1)}, u32[]{:S(2)}, u32[]{:S(2)}) %all-to-all-start.3) | async-done | bytes 6291488 | tf_op jit(solution)/shard_map/all_to_all | solution.py:387
  358.9 5.5 %add_convert_fusion = bf16[256,1024]{1,0:T(8,128)(2,1)} fusion(bf16[256,1024]{1,0:T(8,128)(2,1)S(1)} %shard_map.125, bf16[256,4096]{1,0:T(8,128)(2,1)} %param.11, s32[]{:T(128)S(6)} %select_n.179, bf16[256,3072]{1,0:T(8,128)(2,1)S(1)} %fusion.3, bf16[3072,1024]{1,0:T(8,128)(2,1)} %bitcast.12), kind=kOutput, calls=%fused_computation.16 | convolution fusion | flops 1612447744 | bytes 9437188 | tf_op jit(solution)/shard_map/dot_general | solution.py:394
  (72 shorter events, 27.9 us)
Async XLA Ops:
  7.2 2.9 copy-start.2
  7.2 2.8 copy-start.11
  7.2 81.2 %all-gather.3.cloned.1.call-start = ((), (), s32[]{:S(2)}) async-start(), calls=%async_computation.4 | async-start | bytes 8650752 | tf_op jit(solution)/shard_map/all_gather | solution.py:299
  10.0 2.7 copy-start.12
  10.0 2.6 copy-start.13
  12.0 36.3 %collective-permute-start.1 = (bf16[256,4096]{1,0:T(8,128)(2,1)}, bf16[256,4096]{1,0:T(8,128)(2,1)S(1)}, u32[]{:S(2)}, u32[]{:S(2)}) collective-permute-start(bf16[256,4096]{1,0:T(8,128)(2,1)} %fusion.2), channel_id=1, source_target_pairs={{0,1},{1,0},{2,3},{3,2},{4,5},{5,4},{6,7},{7,6},{8,9},{9,8},{10,11... | collective-permute-start | bytes 6291464 | tf_op jit(solution)/shard_map/ppermute | solution.py:32
  13.9 28.8 %all-to-all-start = ((bf16[32,128,128]{2,1,0:T(8,128)(2,1)}), bf16[32,128,128]{2,1,0:T(8,128)(2,1)S(1)}, u32[]{:S(2)}, u32[]{:S(2)}) async-start(bf16[32,128,128]{2,1,0:T(8,128)(2,1)} %bitcast.4), calls=%async_computation | async-start | bytes 2097152 | tf_op jit(solution)/shard_map/all_to_all | solution.py:303
  22.2 123.4 %all-gather.5.cloned.1.call-start = ((), (), s32[]{:S(2)}) async-start(), calls=%async_computation.5 | async-start | bytes 8650752 | tf_op jit(solution)/shard_map/all_gather | solution.py:322
  42.7 17.5 %collective-permute-start = (bf16[1024,128]{1,0:T(8,128)(2,1)}, bf16[1024,128]{1,0:T(8,128)(2,1)S(1)}, u32[]{:S(2)}, u32[]{:S(2)}) collective-permute-start(bf16[1024,128]{1,0:T(8,128)(2,1)} %param.17), channel_id=1, source_target_pairs={{0,0},{1,1},{2,2},{3,3},{4,4},{5,5},{6,6},{7,7},{8,32},{9,33},{10,... | collective-permute-start | bytes 786440 | tf_op jit(solution)/shard_map/ppermute | solution.py:312
  62.7 35.1 %all-to-all-start.1 = ((bf16[16,512,128]{2,1,0:T(8,128)(2,1)}), bf16[16,512,128]{2,1,0:T(8,128)(2,1)S(1)}, u32[]{:S(2)}, u32[]{:S(2)}) async-start(bf16[16,512,128]{2,1,0:T(8,128)(2,1)} %broadcast_in_dim.18), calls=%async_computation.1 | async-start | bytes 4194304 | tf_op jit(solution)/shard_map/all_to_all | solution.py:41
  66.4 32.6 %copy-start.14 = (s32[256,8]{0,1:T(8,128)S(1)}, s32[256,8]{0,1:T(8,128)}, u32[]{:S(2)}) copy-start(s32[256,8]{0,1:T(8,128)} %param.18) | copy-start | bytes 24580
  97.8 5.1 %collective-permute-start.2 = (bf16[8192,128]{1,0:T(8,128)(2,1)S(1)}, bf16[8192,128]{1,0:T(8,128)(2,1)}, u32[]{:S(2)}, u32[]{:S(2)}) collective-permute-start(bf16[8192,128]{1,0:T(8,128)(2,1)S(1)} %bitcast.26), channel_id=1, source_target_pairs={{0,1},{1,0},{2,3},{3,2},{4,5},{5,4},{6,7},{7,6},{8,9},{9,8},{10,11... | collective-permute-start | bytes 6291464 | tf_op jit(solution)/shard_map/ppermute | solution.py:32
  107.3 14.0 %collective-permute-start.6 = (bf16[256,512]{1,0:T(8,128)(2,1)S(1)}, bf16[256,512]{1,0:T(8,128)(2,1)S(1)}, u32[]{:S(2)}, u32[]{:S(2)}) collective-permute-start(bf16[256,512]{1,0:T(8,128)(2,1)S(1)} %shard_map.123.refs_0_), channel_id=1, source_target_pairs={{32,0},{64,32},{96,64},{0,96},{33,1},{65,33},{97,65},{1,97},{34,2}... | collective-permute-start | bytes 786440 | tf_op jit(solution)/shard_map/ppermute | solution.py:36
  109.3 36.2 %collective-permute-start.7 = (bf16[256,512]{1,0:T(8,128)(2,1)S(1)}, bf16[256,512]{1,0:T(8,128)(2,1)S(1)}, u32[]{:S(2)}, u32[]{:S(2)}) collective-permute-start(bf16[256,512]{1,0:T(8,128)(2,1)S(1)} %shard_map.123.refs_0_), channel_id=1, source_target_pairs={{64,0},{96,32},{0,64},{32,96},{65,1},{97,33},{1,65},{33,97},{66,2}... | collective-permute-start | bytes 786440 | tf_op jit(solution)/shard_map/ppermute | solution.py:36
  113.8 31.7 %collective-permute-start.8 = (bf16[256,512]{1,0:T(8,128)(2,1)S(1)}, bf16[256,512]{1,0:T(8,128)(2,1)S(1)}, u32[]{:S(2)}, u32[]{:S(2)}) collective-permute-start(bf16[256,512]{1,0:T(8,128)(2,1)S(1)} %shard_map.123.refs_0_), channel_id=1, source_target_pairs={{96,0},{0,32},{32,64},{64,96},{97,1},{1,33},{33,65},{65,97},{98,2}... | collective-permute-start | bytes 786440 | tf_op jit(solution)/shard_map/ppermute | solution.py:36
  118.5 32.2 %collective-permute-start.3 = (bf16[256,512]{1,0:T(8,128)(2,1)S(1)}, bf16[256,512]{1,0:T(8,128)(2,1)S(1)}, u32[]{:S(2)}, u32[]{:S(2)}) collective-permute-start(bf16[256,512]{1,0:T(8,128)(2,1)S(1)} %shard_map.122.refs_0_), channel_id=1, source_target_pairs={{32,0},{64,32},{96,64},{0,96},{33,1},{65,33},{97,65},{1,97},{34,2}... | collective-permute-start | bytes 786440 | tf_op jit(solution)/shard_map/ppermute | solution.py:36
  120.0 30.6 %collective-permute-start.4 = (bf16[256,512]{1,0:T(8,128)(2,1)S(1)}, bf16[256,512]{1,0:T(8,128)(2,1)S(1)}, u32[]{:S(2)}, u32[]{:S(2)}) collective-permute-start(bf16[256,512]{1,0:T(8,128)(2,1)S(1)} %shard_map.122.refs_0_), channel_id=1, source_target_pairs={{64,0},{96,32},{0,64},{32,96},{65,1},{97,33},{1,65},{33,97},{66,2}... | collective-permute-start | bytes 786440 | tf_op jit(solution)/shard_map/ppermute | solution.py:36
  121.3 29.4 %collective-permute-start.5 = (bf16[256,512]{1,0:T(8,128)(2,1)S(1)}, bf16[256,512]{1,0:T(8,128)(2,1)S(1)}, u32[]{:S(2)}, u32[]{:S(2)}) collective-permute-start(bf16[256,512]{1,0:T(8,128)(2,1)S(1)} %shard_map.122.refs_0_), channel_id=1, source_target_pairs={{96,0},{0,32},{32,64},{64,96},{97,1},{1,33},{33,65},{65,97},{98,2}... | collective-permute-start | bytes 786440 | tf_op jit(solution)/shard_map/ppermute | solution.py:36
  150.7 4.6 %copy-start.3 = (pred[256,3072]{1,0:T(32,128)(4,1)S(1)}, pred[256,3072]{1,0:T(32,128)(4,1)}, u32[]{:S(2)}) copy-start(pred[256,3072]{1,0:T(32,128)(4,1)} %convolution_compare_fusion) | copy-start | bytes 2359300
  242.5 29.2 %collective-permute-start.10 = (bf16[256,1024]{1,0:T(8,128)(2,1)S(1)}, bf16[256,1024]{1,0:T(8,128)(2,1)S(1)}, u32[]{:S(2)}, u32[]{:S(2)}) collective-permute-start(bf16[256,1024]{1,0:T(8,128)(2,1)S(1)} %shard_map.125), channel_id=1, source_target_pairs={{64,0},{96,32},{0,64},{32,96},{65,1},{97,33},{1,65},{33,97},{66,2}... | collective-permute-start | bytes 1572872 | tf_op jit(solution)/shard_map/ppermute | solution.py:36
  244.3 27.4 %collective-permute-start.11 = (bf16[256,1024]{1,0:T(8,128)(2,1)S(1)}, bf16[256,1024]{1,0:T(8,128)(2,1)S(1)}, u32[]{:S(2)}, u32[]{:S(2)}) collective-permute-start(bf16[256,1024]{1,0:T(8,128)(2,1)S(1)} %shard_map.125), channel_id=1, source_target_pairs={{96,0},{0,32},{32,64},{64,96},{97,1},{1,33},{33,65},{65,97},{98,2}... | collective-permute-start | bytes 1572872 | tf_op jit(solution)/shard_map/ppermute | solution.py:36
  245.2 26.5 %collective-permute-start.9 = (bf16[256,1024]{1,0:T(8,128)(2,1)S(1)}, bf16[256,1024]{1,0:T(8,128)(2,1)S(1)}, u32[]{:S(2)}, u32[]{:S(2)}) collective-permute-start(bf16[256,1024]{1,0:T(8,128)(2,1)S(1)} %shard_map.125), channel_id=1, source_target_pairs={{32,0},{64,32},{96,64},{0,96},{33,1},{65,33},{97,65},{1,97},{34,2}... | collective-permute-start | bytes 1572872 | tf_op jit(solution)/shard_map/ppermute | solution.py:36
  271.8 9.6 %copy-start.15 = (bf16[256,8]{0,1:T(8,128)(2,1)S(1)}, bf16[256,8]{0,1:T(8,128)(2,1)}, u32[]{:S(2)}) copy-start(bf16[256,8]{0,1:T(8,128)(2,1)} %param.19) | copy-start | bytes 12292
  272.9 86.0 %all-to-all-start.3 = ((bf16[128,24,1024]{2,1,0:T(8,128)(2,1)}), bf16[128,24,1024]{2,1,0:T(8,128)(2,1)}, u32[]{:S(2)}, u32[]{:S(2)}) async-start(bf16[128,24,1024]{2,1,0:T(8,128)(2,1)} %bitcast.34), calls=%async_computation.3 | async-start | bytes 12582912 | tf_op jit(solution)/shard_map/all_to_all | solution.py:387
  (9 other events, 11.7 us)
Sparse Core Ops, SparseCore 0:
  10.3 78.0 all-gather.2
  90.6 54.8 all-gather.4

commit v5 on v4

--- a/solution.py
+++ b/solution.py
@@ -20,6 +20,7 @@
 QUERY_TILE = 128
 HIDDEN_TILE = 256
 NORM_TILE = 64
+EXPERT_VMEM = 40
 
 
 def rms_scale(row_data, gain):
@@ -248,8 +249,8 @@
         grid=(wide + parts,),
         out_shape=jax.ShapeDtypeStruct(arrived.shape, arrived.dtype),
         in_specs=[
-            pl.BlockSpec((parts, rows, width), lambda i: (0, 0, 0)),
-            pl.BlockSpec((parts, 1, width), lambda i: (0, 0, 0)),
+            pl.BlockSpec(memory_space=pltpu.VMEM),
+            pl.BlockSpec(memory_space=pltpu.VMEM),
             pl.BlockSpec((1, model_width, HIDDEN_TILE), lambda i: (0, 0, jnp.minimum(i, wide - 1))),
             pl.BlockSpec(
                 (1, model_width, HIDDEN_TILE), lambda i: (0, 0, wide + jnp.minimum(i, wide - 1))
@@ -261,7 +262,7 @@
             pltpu.VMEM((parts, rows, width), jnp.bfloat16),
             pltpu.VMEM((wide, rows, HIDDEN_TILE), jnp.bfloat16),
         ],
-        compiler_params=pltpu.CompilerParams(vmem_limit_bytes=54 * 2**20),
+        compiler_params=pltpu.CompilerParams(vmem_limit_bytes=EXPERT_VMEM * 2**20),
         cost_estimate=pl.CostEstimate(
             flops=6 * rows * model_width * FFW,
             bytes_accessed=4 * rows * model_width + 6 * model_width * FFW,

time: 372 us -> 371 us (level)
  Pallas kernels: 42.9 us -> 38.5 us
    pallas_call x1, Pallas kernels: 25.9 us -> 21.6 us  [run_expert(): pl.pallas_call(functools.partial(expert_kernel, wide=wide), grid=(wide +...]
  transfers between devices with their start and end apart: 17 -> 17, of which waited for: 7 -> 7; matrix products, arithmetic and copies ran while one was open for 7% -> 7% of each run, Pallas kernels for 10% -> 9%
where the time goes in v5:
time: 371 us; the launch traced here: 370 us
  waiting for transfers between devices  148 us (40%)
  blocking collectives  86.2 us (23%)
  starting transfers between devices  43.4 us (12%)
  Pallas kernels  38.5 us (10%)
  matrix products  21.1 us (6%)
  between operations  14.4 us (4%)
  local copies, waits for them, and re-layouts  9.56 us (3%)
  other arithmetic  8.79 us (2%)
    all_to_all x1, blocking collectives, on_device(): lax.all_to_all(outbound.reshape(experts_all, capacity, col_width), ('grp'...  86.2 us
    all_to_all x1, waiting for transfers between devices, on_device(): lax.all_to_all(result.reshape(experts_all, capacity, col_width), ('grp',...  73.6 us
    all_gather x1, waiting for transfers between devices, on_device(): w_query_all = lax.all_gather(w_query, 'fsdp', axis=0, tiled=True)  22 us
    pallas_call x1, Pallas kernels, run_expert(): pl.pallas_call(functools.partial(expert_kernel, wide=wide), grid=(wide +...  21.6 us
    all_to_all x1, waiting for transfers between devices, on_device(): lax.all_to_all(jnp.tile(w_both, (fsdp_size // 2, 1, 1)), 'fsdp', split_ax...  20.4 us
    ppermute x9, starting transfers between devices, from_group(): lax.ppermute(rows, 'grp', [((i + shift) % SIDE, i) for i in range(SIDE)])  17.6 us
    all_gather x1, waiting for transfers between devices, on_device(): w_out_all = lax.all_gather(w_turned, 'fsdp', axis=0, tiled=True)  15.1 us
    ppermute x1, waiting for transfers between devices, on_device(): lax.ppermute(w_out_block, ('grp', 'fsdp'), [(g * fsdp_size + f, f // 8 *...  11.1 us
  transfers between devices with their start and end apart: 17, of which 7 were waited for; matrix products, arithmetic and copies ran while one was open for 7% of the time, Pallas kernels for 9%

profile of v5, /device:TPU:5, one launch (start us, length us, event | category | flops | bytes accessed | tf_op | source)
XLA Modules:
  0.0 370.0 jit_solution(11940591275386680673)
XLA Ops:
  13.9 8.2 %all-to-all-start = ((bf16[32,128,128]{2,1,0:T(8,128)(2,1)}), bf16[32,128,128]{2,1,0:T(8,128)(2,1)S(1)}, u32[]{:S(2)}, u32[]{:S(2)}) async-start(bf16[32,128,128]{2,1,0:T(8,128)(2,1)} %bitcast.4), calls=%async_computation | async-start | bytes 2097152 | tf_op jit(solution)/shard_map/all_to_all | solution.py:304
  22.2 20.4 %all-to-all-done = bf16[32,128,128]{2,1,0:T(8,128)(2,1)S(1)} async-done(((bf16[32,128,128]{2,1,0:T(8,128)(2,1)}), bf16[32,128,128]{2,1,0:T(8,128)(2,1)S(1)}, u32[]{:S(2)}, u32[]{:S(2)}) %all-to-all-start) | async-done | bytes 1048608 | tf_op jit(solution)/shard_map/all_to_all | solution.py:304
  42.6 3.4 collective-permute-start
  46.0 2.3 convolution_convert_fusion.3
  49.1 11.1 %collective-permute-done = bf16[1024,128]{1,0:T(8,128)(2,1)S(1)} collective-permute-done((bf16[1024,128]{1,0:T(8,128)(2,1)}, bf16[1024,128]{1,0:T(8,128)(2,1)S(1)}, u32[]{:S(2)}, u32[]{:S(2)}) %collective-permute-start) | collective-permute-done | bytes 262176 | tf_op jit(solution)/shard_map/ppermute | solution.py:313
  62.7 3.7 %all-to-all-start.1 = ((bf16[16,512,128]{2,1,0:T(8,128)(2,1)}), bf16[16,512,128]{2,1,0:T(8,128)(2,1)S(1)}, u32[]{:S(2)}, u32[]{:S(2)}) async-start(bf16[16,512,128]{2,1,0:T(8,128)(2,1)} %broadcast_in_dim.18), calls=%async_computation.1 | async-start | bytes 4194304 | tf_op jit(solution)/shard_map/all_to_all | solution.py:42
  66.4 22.0 %all-gather.3.cloned.1.call-done = bf16[4096,1024]{1,0:T(8,128)(2,1)} async-done(((bf16[128,1024]{1,0:T(8,128)(2,1)}), bf16[4096,1024]{1,0:T(8,128)(2,1)}) %all-gather.3.cloned.1.call-update) | async-done | bytes 8388624 | tf_op jit(solution)/shard_map/all_gather | solution.py:300
  88.4 6.3 %convolution_convert_fusion.1.query_ref = bf16[256,1024]{1,0:T(8,128)(2,1)S(1)} fusion(bf16[256,4096]{1,0:T(8,128)(2,1)} %fusion.2, bf16[4096,1024]{1,0:T(8,128)(2,1)} %all-gather.3.cloned.1.call-done), kind=kOutput, calls=%fused_computation.11 | convolution fusion | flops 2147745792 | bytes 11010048 | tf_op jit(solution)/shard_map/dot_general | solution.py:325
  94.7 3.0 all-to-all-done.1
  102.8 3.5 shard_map.123.refs_0_
  109.4 4.4 %collective-permute-start.7 = (bf16[256,512]{1,0:T(8,128)(2,1)S(1)}, bf16[256,512]{1,0:T(8,128)(2,1)S(1)}, u32[]{:S(2)}, u32[]{:S(2)}) collective-permute-start(bf16[256,512]{1,0:T(8,128)(2,1)S(1)} %shard_map.123.refs_0_), channel_id=1, source_target_pairs={{64,0},{96,32},{0,64},{32,96},{65,1},{97,33},{1,65},{33,97},{66,2}... | collective-permute-start | bytes 786440 | tf_op jit(solution)/shard_map/ppermute | solution.py:37
  114.8 3.7 shard_map.122.refs_0_
  121.2 5.1 %collective-permute-start.5 = (bf16[256,512]{1,0:T(8,128)(2,1)S(1)}, bf16[256,512]{1,0:T(8,128)(2,1)S(1)}, u32[]{:S(2)}, u32[]{:S(2)}) collective-permute-start(bf16[256,512]{1,0:T(8,128)(2,1)S(1)} %shard_map.122.refs_0_), channel_id=1, source_target_pairs={{96,0},{0,32},{32,64},{64,96},{97,1},{1,33},{33,65},{65,97},{98,2}... | collective-permute-start | bytes 786440 | tf_op jit(solution)/shard_map/ppermute | solution.py:37
  126.3 2.7 convolution_compare_fusion
  128.9 15.1 %all-gather.5.cloned.1.call-done = bf16[32768,128]{1,0:T(8,128)(2,1)} async-done(((bf16[1024,128]{1,0:T(8,128)(2,1)}), bf16[32768,128]{1,0:T(8,128)(2,1)}) %all-gather.5.cloned.1.call-update) | async-done | bytes 8388624 | tf_op jit(solution)/shard_map/all_gather | solution.py:323
  144.1 5.1 %shard_map.124.refs_5_ = f32[256,1024]{1,0:T(8,128)} custom-call(s32[1]{0:T(128)} %bitcast.group_ref, bf16[256,512]{1,0:T(8,128)(2,1)S(1)} %shard_map.123.refs_0_, bf16[256,512]{1,0:T(8,128)(2,1)S(1)} %collective-permute-done.6.refs_1_, bf16[256,512]{1,0:T(8,128)(2,1)S(1)} %collective-permute-done.7.refs_2_, ...), custom_call_target="tpu_custom_call" | custom-call | flops 1073741824 | bytes 5242880 | tf_op jit(solution)/shard_map/pallas_call | solution.py:173
  149.2 4.6 %shard_map.125 = bf16[256,1024]{1,0:T(8,128)(2,1)S(1)} custom-call(s32[1]{0:T(128)} %bitcast.group_ref, bf16[256,512]{1,0:T(8,128)(2,1)S(1)} %shard_map.122.refs_0_, bf16[256,512]{1,0:T(8,128)(2,1)S(1)} %collective-permute-done.3.refs_1_, bf16[256,512]{1,0:T(8,128)(2,1)S(1)} %collective-permute-done.4.refs_2_, ...), custom_call_target="tpu_custom_call" | custom-call | flops 1073741824 | bytes 5242880 | tf_op jit(solution)/shard_map/pallas_call | solution.py:173
  153.8 2.9 convolution_convert_fusion
  156.7 86.2 %all_to_all.20 = bf16[128,24,1024]{2,1,0:T(8,128)(2,1)S(1)} all-to-all(bf16[128,24,1024]{2,1,0:T(8,128)(2,1)S(1)} %bitcast.32), channel_id=1, replica_groups=mesh['grp'=4,'fsdp'=32] {'grp','fsdp'}, dimensions={0} | all-to-all | bytes 12582912 | tf_op jit(solution)/shard_map/all_to_all | solution.py:368
  246.2 21.6 %shard_map.126 = bf16[4,768,1024]{2,1,0:T(8,128)(2,1)S(1)} custom-call(bf16[4,768,1024]{2,1,0:T(8,128)(2,1)S(1)} %bitcast.27, f32[4,1,1024]{2,1,0:T(1,128)S(1)} %bitcast.31, bf16[1,4096,1536]{2,1,0:T(8,128)(2,1)} %up_ref.1, bf16[1,4096,1536]{2,1,0:T(8,128)(2,1)} %up_ref.1, bf16[1,768,4096]{2,1,0:T(8,128)(2,1)} %down_ref.1), custom_call_target="tpu_custom_call" | custom-call | flops 14495514624 | bytes 31457280 | tf_op jit(solution)/shard_map/pallas_call | solution.py:247
  267.8 2.6 copy-done
  271.6 8.4 %all-to-all-start.3 = ((bf16[128,24,1024]{2,1,0:T(8,128)(2,1)}), bf16[128,24,1024]{2,1,0:T(8,128)(2,1)}, u32[]{:S(2)}, u32[]{:S(2)}) async-start(bf16[128,24,1024]{2,1,0:T(8,128)(2,1)} %bitcast.26), calls=%async_computation.3 | async-start | bytes 12582912 | tf_op jit(solution)/shard_map/all_to_all | solution.py:388
  284.1 73.6 %all-to-all-done.3 = bf16[128,24,1024]{2,1,0:T(8,128)(2,1)} async-done(((bf16[128,24,1024]{2,1,0:T(8,128)(2,1)}), bf16[128,24,1024]{2,1,0:T(8,128)(2,1)}, u32[]{:S(2)}, u32[]{:S(2)}) %all-to-all-start.3) | async-done | bytes 6291488 | tf_op jit(solution)/shard_map/all_to_all | solution.py:388
  357.6 5.5 %add_convert_fusion = bf16[256,1024]{1,0:T(8,128)(2,1)} fusion(bf16[256,1024]{1,0:T(8,128)(2,1)S(1)} %shard_map.125, bf16[256,4096]{1,0:T(8,128)(2,1)} %param.11, s32[]{:T(128)S(6)} %select_n.179, bf16[256,3072]{1,0:T(8,128)(2,1)S(1)} %fusion.3, bf16[3072,1024]{1,0:T(8,128)(2,1)} %bitcast.12), kind=kOutput, calls=%fused_computation.16 | convolution fusion | flops 1612447744 | bytes 9437188 | tf_op jit(solution)/shard_map/dot_general | solution.py:395
  (76 shorter events, 30.2 us)
Async XLA Ops:
  7.2 2.9 copy-start.4
  7.2 2.8 copy-start.13
  7.2 81.2 %all-gather.3.cloned.1.call-start = ((), (), s32[]{:S(2)}) async-start(), calls=%async_computation.4 | async-start | bytes 8650752 | tf_op jit(solution)/shard_map/all_gather | solution.py:300
  10.0 2.7 copy-start.14
  12.0 36.3 %collective-permute-start.1 = (bf16[256,4096]{1,0:T(8,128)(2,1)}, bf16[256,4096]{1,0:T(8,128)(2,1)S(1)}, u32[]{:S(2)}, u32[]{:S(2)}) collective-permute-start(bf16[256,4096]{1,0:T(8,128)(2,1)} %fusion.2), channel_id=1, source_target_pairs={{0,1},{1,0},{2,3},{3,2},{4,5},{5,4},{6,7},{7,6},{8,9},{9,8},{10,11... | collective-permute-start | bytes 6291464 | tf_op jit(solution)/shard_map/ppermute | solution.py:33
  13.9 28.7 %all-to-all-start = ((bf16[32,128,128]{2,1,0:T(8,128)(2,1)}), bf16[32,128,128]{2,1,0:T(8,128)(2,1)S(1)}, u32[]{:S(2)}, u32[]{:S(2)}) async-start(bf16[32,128,128]{2,1,0:T(8,128)(2,1)} %bitcast.4), calls=%async_computation | async-start | bytes 2097152 | tf_op jit(solution)/shard_map/all_to_all | solution.py:304
  22.1 121.9 %all-gather.5.cloned.1.call-start = ((), (), s32[]{:S(2)}) async-start(), calls=%async_computation.5 | async-start | bytes 8650752 | tf_op jit(solution)/shard_map/all_gather | solution.py:323
  42.6 17.6 %collective-permute-start = (bf16[1024,128]{1,0:T(8,128)(2,1)}, bf16[1024,128]{1,0:T(8,128)(2,1)S(1)}, u32[]{:S(2)}, u32[]{:S(2)}) collective-permute-start(bf16[1024,128]{1,0:T(8,128)(2,1)} %param.17), channel_id=1, source_target_pairs={{0,0},{1,1},{2,2},{3,3},{4,4},{5,5},{6,6},{7,7},{8,32},{9,33},{10,... | collective-permute-start | bytes 786440 | tf_op jit(solution)/shard_map/ppermute | solution.py:313
  62.7 35.0 %all-to-all-start.1 = ((bf16[16,512,128]{2,1,0:T(8,128)(2,1)}), bf16[16,512,128]{2,1,0:T(8,128)(2,1)S(1)}, u32[]{:S(2)}, u32[]{:S(2)}) async-start(bf16[16,512,128]{2,1,0:T(8,128)(2,1)} %broadcast_in_dim.18), calls=%async_computation.1 | async-start | bytes 4194304 | tf_op jit(solution)/shard_map/all_to_all | solution.py:42
  66.4 32.5 %copy-start.16 = (s32[256,8]{0,1:T(8,128)S(1)}, s32[256,8]{0,1:T(8,128)}, u32[]{:S(2)}) copy-start(s32[256,8]{0,1:T(8,128)} %param.18) | copy-start | bytes 24580
  97.7 5.2 %collective-permute-start.2 = (bf16[8192,128]{1,0:T(8,128)(2,1)S(1)}, bf16[8192,128]{1,0:T(8,128)(2,1)}, u32[]{:S(2)}, u32[]{:S(2)}) collective-permute-start(bf16[8192,128]{1,0:T(8,128)(2,1)S(1)} %bitcast.28), channel_id=1, source_target_pairs={{0,1},{1,0},{2,3},{3,2},{4,5},{5,4},{6,7},{7,6},{8,9},{9,8},{10,11... | collective-permute-start | bytes 6291464 | tf_op jit(solution)/shard_map/ppermute | solution.py:33
  107.2 14.1 %collective-permute-start.6 = (bf16[256,512]{1,0:T(8,128)(2,1)S(1)}, bf16[256,512]{1,0:T(8,128)(2,1)S(1)}, u32[]{:S(2)}, u32[]{:S(2)}) collective-permute-start(bf16[256,512]{1,0:T(8,128)(2,1)S(1)} %shard_map.123.refs_0_), channel_id=1, source_target_pairs={{32,0},{64,32},{96,64},{0,96},{33,1},{65,33},{97,65},{1,97},{34,2}... | collective-permute-start | bytes 786440 | tf_op jit(solution)/shard_map/ppermute | solution.py:37
  109.4 34.7 %collective-permute-start.7 = (bf16[256,512]{1,0:T(8,128)(2,1)S(1)}, bf16[256,512]{1,0:T(8,128)(2,1)S(1)}, u32[]{:S(2)}, u32[]{:S(2)}) collective-permute-start(bf16[256,512]{1,0:T(8,128)(2,1)S(1)} %shard_map.123.refs_0_), channel_id=1, source_target_pairs={{64,0},{96,32},{0,64},{32,96},{65,1},{97,33},{1,65},{33,97},{66,2}... | collective-permute-start | bytes 786440 | tf_op jit(solution)/shard_map/ppermute | solution.py:37
  113.7 30.3 %collective-permute-start.8 = (bf16[256,512]{1,0:T(8,128)(2,1)S(1)}, bf16[256,512]{1,0:T(8,128)(2,1)S(1)}, u32[]{:S(2)}, u32[]{:S(2)}) collective-permute-start(bf16[256,512]{1,0:T(8,128)(2,1)S(1)} %shard_map.123.refs_0_), channel_id=1, source_target_pairs={{96,0},{0,32},{32,64},{64,96},{97,1},{1,33},{33,65},{65,97},{98,2}... | collective-permute-start | bytes 786440 | tf_op jit(solution)/shard_map/ppermute | solution.py:37
  118.5 30.7 %collective-permute-start.3 = (bf16[256,512]{1,0:T(8,128)(2,1)S(1)}, bf16[256,512]{1,0:T(8,128)(2,1)S(1)}, u32[]{:S(2)}, u32[]{:S(2)}) collective-permute-start(bf16[256,512]{1,0:T(8,128)(2,1)S(1)} %shard_map.122.refs_0_), channel_id=1, source_target_pairs={{32,0},{64,32},{96,64},{0,96},{33,1},{65,33},{97,65},{1,97},{34,2}... | collective-permute-start | bytes 786440 | tf_op jit(solution)/shard_map/ppermute | solution.py:37
  120.0 29.2 %collective-permute-start.4 = (bf16[256,512]{1,0:T(8,128)(2,1)S(1)}, bf16[256,512]{1,0:T(8,128)(2,1)S(1)}, u32[]{:S(2)}, u32[]{:S(2)}) collective-permute-start(bf16[256,512]{1,0:T(8,128)(2,1)S(1)} %shard_map.122.refs_0_), channel_id=1, source_target_pairs={{64,0},{96,32},{0,64},{32,96},{65,1},{97,33},{1,65},{33,97},{66,2}... | collective-permute-start | bytes 786440 | tf_op jit(solution)/shard_map/ppermute | solution.py:37
  121.2 28.0 %collective-permute-start.5 = (bf16[256,512]{1,0:T(8,128)(2,1)S(1)}, bf16[256,512]{1,0:T(8,128)(2,1)S(1)}, u32[]{:S(2)}, u32[]{:S(2)}) collective-permute-start(bf16[256,512]{1,0:T(8,128)(2,1)S(1)} %shard_map.122.refs_0_), channel_id=1, source_target_pairs={{96,0},{0,32},{32,64},{64,96},{97,1},{1,33},{33,65},{65,97},{98,2}... | collective-permute-start | bytes 786440 | tf_op jit(solution)/shard_map/ppermute | solution.py:37
  149.2 4.6 %copy-start.5 = (pred[256,3072]{1,0:T(32,128)(4,1)S(1)}, pred[256,3072]{1,0:T(32,128)(4,1)}, u32[]{:S(2)}) copy-start(pred[256,3072]{1,0:T(32,128)(4,1)} %convolution_compare_fusion) | copy-start | bytes 2359300
  156.7 89.5 %copy-start.1 = (f32[4096]{0:T(1024)S(1)}, f32[4096]{0:T(1024)}, u32[]{:S(2)}) copy-start(f32[4096]{0:T(1024)} %param.13) | copy-start | bytes 49156
  242.9 27.5 %collective-permute-start.10 = (bf16[256,1024]{1,0:T(8,128)(2,1)S(1)}, bf16[256,1024]{1,0:T(8,128)(2,1)S(1)}, u32[]{:S(2)}, u32[]{:S(2)}) collective-permute-start(bf16[256,1024]{1,0:T(8,128)(2,1)S(1)} %shard_map.125), channel_id=1, source_target_pairs={{64,0},{96,32},{0,64},{32,96},{65,1},{97,33},{1,65},{33,97},{66,2}... | collective-permute-start | bytes 1572872 | tf_op jit(solution)/shard_map/ppermute | solution.py:37
  244.7 25.7 %collective-permute-start.11 = (bf16[256,1024]{1,0:T(8,128)(2,1)S(1)}, bf16[256,1024]{1,0:T(8,128)(2,1)S(1)}, u32[]{:S(2)}, u32[]{:S(2)}) collective-permute-start(bf16[256,1024]{1,0:T(8,128)(2,1)S(1)} %shard_map.125), channel_id=1, source_target_pairs={{96,0},{0,32},{32,64},{64,96},{97,1},{1,33},{33,65},{65,97},{98,2}... | collective-permute-start | bytes 1572872 | tf_op jit(solution)/shard_map/ppermute | solution.py:37
  245.6 24.8 %collective-permute-start.9 = (bf16[256,1024]{1,0:T(8,128)(2,1)S(1)}, bf16[256,1024]{1,0:T(8,128)(2,1)S(1)}, u32[]{:S(2)}, u32[]{:S(2)}) collective-permute-start(bf16[256,1024]{1,0:T(8,128)(2,1)S(1)} %shard_map.125), channel_id=1, source_target_pairs={{32,0},{64,32},{96,64},{0,96},{33,1},{65,33},{97,65},{1,97},{34,2}... | collective-permute-start | bytes 1572872 | tf_op jit(solution)/shard_map/ppermute | solution.py:37
  270.5 9.6 %copy-start.17 = (bf16[256,8]{0,1:T(8,128)(2,1)S(1)}, bf16[256,8]{0,1:T(8,128)(2,1)}, u32[]{:S(2)}) copy-start(bf16[256,8]{0,1:T(8,128)(2,1)} %param.19) | copy-start | bytes 12292
  271.6 86.0 %all-to-all-start.3 = ((bf16[128,24,1024]{2,1,0:T(8,128)(2,1)}), bf16[128,24,1024]{2,1,0:T(8,128)(2,1)}, u32[]{:S(2)}, u32[]{:S(2)}) async-start(bf16[128,24,1024]{2,1,0:T(8,128)(2,1)} %bitcast.26), calls=%async_computation.3 | async-start | bytes 12582912 | tf_op jit(solution)/shard_map/all_to_all | solution.py:388
  (11 other events, 17.0 us)
Sparse Core Ops, SparseCore 0:
  10.3 78.0 all-gather.2
  90.6 53.4 all-gather.4

commit v6 on v5

--- a/solution.py
+++ b/solution.py
@@ -247,7 +247,7 @@
     return pl.pallas_call(
         functools.partial(expert_kernel, wide=wide),
         grid=(wide + parts,),
-        out_shape=jax.ShapeDtypeStruct(arrived.shape, arrived.dtype),
+        out_shape=pltpu.HBM(arrived.shape, arrived.dtype),
         in_specs=[
             pl.BlockSpec(memory_space=pltpu.VMEM),
             pl.BlockSpec(memory_space=pltpu.VMEM),

time: 371 us -> 370 us (level)
  transfers between devices with their start and end apart: 17 -> 17, of which waited for: 7 -> 8; matrix products, arithmetic and copies ran while one was open for 7% -> 7% of each run, Pallas kernels for 9% -> 10%
where the time goes in v6:
time: 370 us; the launch traced here: 369 us
  waiting for transfers between devices  149 us (40%)
  blocking collectives  86.1 us (23%)
  starting transfers between devices  43.2 us (12%)
  Pallas kernels  39.7 us (11%)
  matrix products  21.3 us (6%)
  between operations  14.4 us (4%)
  other arithmetic  8.79 us (2%)
  local copies, waits for them, and re-layouts  6.81 us (2%)
    all_to_all x1, blocking collectives, on_device(): lax.all_to_all(outbound.reshape(experts_all, capacity, col_width), ('grp'...  86.1 us
    all_to_all x1, waiting for transfers between devices, on_device(): lax.all_to_all(result.reshape(experts_all, capacity, col_width), ('grp',...  73.6 us
    pallas_call x1, Pallas kernels, run_expert(): pl.pallas_call(functools.partial(expert_kernel, wide=wide), grid=(wide +...  22.8 us
    all_gather x1, waiting for transfers between devices, on_device(): w_query_all = lax.all_gather(w_query, 'fsdp', axis=0, tiled=True)  21.9 us
    all_to_all x1, waiting for transfers between devices, on_device(): lax.all_to_all(jnp.tile(w_both, (fsdp_size // 2, 1, 1)), 'fsdp', split_ax...  20.5 us
    ppermute x9, starting transfers between devices, from_group(): lax.ppermute(rows, 'grp', [((i + shift) % SIDE, i) for i in range(SIDE)])  17.7 us
    all_gather x1, waiting for transfers between devices, on_device(): w_out_all = lax.all_gather(w_turned, 'fsdp', axis=0, tiled=True)  15.2 us
    ppermute x1, waiting for transfers between devices, on_device(): lax.ppermute(w_out_block, ('grp', 'fsdp'), [(g * fsdp_size + f, f // 8 *...  11.1 us
  transfers between devices with their start and end apart: 17, of which 8 were waited for; matrix products, arithmetic and copies ran while one was open for 7% of the time, Pallas kernels for 10%

profile of v6, /device:TPU:5, one launch (start us, length us, event | category | flops | bytes accessed | tf_op | source)
XLA Modules:
  0.0 369.0 jit_solution(17331350672467823463)
XLA Ops:
  13.9 8.2 %all-to-all-start = ((bf16[32,128,128]{2,1,0:T(8,128)(2,1)}), bf16[32,128,128]{2,1,0:T(8,128)(2,1)S(1)}, u32[]{:S(2)}, u32[]{:S(2)}) async-start(bf16[32,128,128]{2,1,0:T(8,128)(2,1)} %bitcast.4), calls=%async_computation | async-start | bytes 2097152 | tf_op jit(solution)/shard_map/all_to_all | solution.py:304
  22.2 20.5 %all-to-all-done = bf16[32,128,128]{2,1,0:T(8,128)(2,1)S(1)} async-done(((bf16[32,128,128]{2,1,0:T(8,128)(2,1)}), bf16[32,128,128]{2,1,0:T(8,128)(2,1)S(1)}, u32[]{:S(2)}, u32[]{:S(2)}) %all-to-all-start) | async-done | bytes 1048608 | tf_op jit(solution)/shard_map/all_to_all | solution.py:304
  42.7 3.3 collective-permute-start
  46.0 2.3 convolution_convert_fusion.3
  49.1 11.1 %collective-permute-done = bf16[1024,128]{1,0:T(8,128)(2,1)S(1)} collective-permute-done((bf16[1024,128]{1,0:T(8,128)(2,1)}, bf16[1024,128]{1,0:T(8,128)(2,1)S(1)}, u32[]{:S(2)}, u32[]{:S(2)}) %collective-permute-start) | collective-permute-done | bytes 262176 | tf_op jit(solution)/shard_map/ppermute | solution.py:313
  62.7 3.7 %all-to-all-start.1 = ((bf16[16,512,128]{2,1,0:T(8,128)(2,1)}), bf16[16,512,128]{2,1,0:T(8,128)(2,1)S(1)}, u32[]{:S(2)}, u32[]{:S(2)}) async-start(bf16[16,512,128]{2,1,0:T(8,128)(2,1)} %broadcast_in_dim.18), calls=%async_computation.1 | async-start | bytes 4194304 | tf_op jit(solution)/shard_map/all_to_all | solution.py:42
  66.4 21.9 %all-gather.3.cloned.1.call-done = bf16[4096,1024]{1,0:T(8,128)(2,1)} async-done(((bf16[128,1024]{1,0:T(8,128)(2,1)}), bf16[4096,1024]{1,0:T(8,128)(2,1)}) %all-gather.3.cloned.1.call-update) | async-done | bytes 8388624 | tf_op jit(solution)/shard_map/all_gather | solution.py:300
  88.3 6.3 %convolution_convert_fusion.1.query_ref = bf16[256,1024]{1,0:T(8,128)(2,1)S(1)} fusion(bf16[256,4096]{1,0:T(8,128)(2,1)} %fusion.2, bf16[4096,1024]{1,0:T(8,128)(2,1)} %all-gather.3.cloned.1.call-done), kind=kOutput, calls=%fused_computation.11 | convolution fusion | flops 2147745792 | bytes 11010048 | tf_op jit(solution)/shard_map/dot_general | solution.py:325
  94.7 3.0 all-to-all-done.1
  102.8 3.5 shard_map.123.refs_0_
  107.1 2.3 collective-permute-start.6
  109.4 4.3 %collective-permute-start.7 = (bf16[256,512]{1,0:T(8,128)(2,1)S(1)}, bf16[256,512]{1,0:T(8,128)(2,1)S(1)}, u32[]{:S(2)}, u32[]{:S(2)}) collective-permute-start(bf16[256,512]{1,0:T(8,128)(2,1)S(1)} %shard_map.123.refs_0_), channel_id=1, source_target_pairs={{64,0},{96,32},{0,64},{32,96},{65,1},{97,33},{1,65},{33,97},{66,2}... | collective-permute-start | bytes 786440 | tf_op jit(solution)/shard_map/ppermute | solution.py:37
  114.8 3.7 shard_map.122.refs_0_
  121.2 5.1 %collective-permute-start.5 = (bf16[256,512]{1,0:T(8,128)(2,1)S(1)}, bf16[256,512]{1,0:T(8,128)(2,1)S(1)}, u32[]{:S(2)}, u32[]{:S(2)}) collective-permute-start(bf16[256,512]{1,0:T(8,128)(2,1)S(1)} %shard_map.122.refs_0_), channel_id=1, source_target_pairs={{96,0},{0,32},{32,64},{64,96},{97,1},{1,33},{33,65},{65,97},{98,2}... | collective-permute-start | bytes 786440 | tf_op jit(solution)/shard_map/ppermute | solution.py:37
  126.3 2.6 convolution_compare_fusion
  128.9 15.2 %all-gather.5.cloned.1.call-done = bf16[32768,128]{1,0:T(8,128)(2,1)} async-done(((bf16[1024,128]{1,0:T(8,128)(2,1)}), bf16[32768,128]{1,0:T(8,128)(2,1)}) %all-gather.5.cloned.1.call-update) | async-done | bytes 8388624 | tf_op jit(solution)/shard_map/all_gather | solution.py:323
  144.2 5.1 %shard_map.124.refs_5_ = f32[256,1024]{1,0:T(8,128)} custom-call(s32[1]{0:T(128)} %bitcast.group_ref, bf16[256,512]{1,0:T(8,128)(2,1)S(1)} %shard_map.123.refs_0_, bf16[256,512]{1,0:T(8,128)(2,1)S(1)} %collective-permute-done.6.refs_1_, bf16[256,512]{1,0:T(8,128)(2,1)S(1)} %collective-permute-done.7.refs_2_, ...), custom_call_target="tpu_custom_call" | custom-call | flops 1073741824 | bytes 5242880 | tf_op jit(solution)/shard_map/pallas_call | solution.py:173
  149.3 4.6 %shard_map.125 = bf16[256,1024]{1,0:T(8,128)(2,1)S(1)} custom-call(s32[1]{0:T(128)} %bitcast.group_ref, bf16[256,512]{1,0:T(8,128)(2,1)S(1)} %shard_map.122.refs_0_, bf16[256,512]{1,0:T(8,128)(2,1)S(1)} %collective-permute-done.3.refs_1_, bf16[256,512]{1,0:T(8,128)(2,1)S(1)} %collective-permute-done.4.refs_2_, ...), custom_call_target="tpu_custom_call" | custom-call | flops 1073741824 | bytes 5242880 | tf_op jit(solution)/shard_map/pallas_call | solution.py:173
  153.9 3.1 convolution_convert_fusion
  157.0 86.1 %all_to_all.20 = bf16[128,24,1024]{2,1,0:T(8,128)(2,1)S(1)} all-to-all(bf16[128,24,1024]{2,1,0:T(8,128)(2,1)S(1)} %bitcast.33), channel_id=1, replica_groups=mesh['grp'=4,'fsdp'=32] {'grp','fsdp'}, dimensions={0} | all-to-all | bytes 12582912 | tf_op jit(solution)/shard_map/all_to_all | solution.py:368
  246.4 22.8 %shard_map.126 = bf16[4,768,1024]{2,1,0:T(8,128)(2,1)} custom-call(bf16[4,768,1024]{2,1,0:T(8,128)(2,1)S(1)} %bitcast.26, f32[4,1,1024]{2,1,0:T(1,128)S(1)} %bitcast.32, bf16[1,4096,1536]{2,1,0:T(8,128)(2,1)} %up_ref.1, bf16[1,4096,1536]{2,1,0:T(8,128)(2,1)} %up_ref.1, bf16[1,768,4096]{2,1,0:T(8,128)(2,1)S(1)} %bitcast.31), custom_call_target="tpu_custom_call" | custom-call | flops 14495514624 | bytes 31457280 | tf_op jit(solution)/shard_map/pallas_call | solution.py:247
  270.7 8.3 %all-to-all-start.3 = ((bf16[128,24,1024]{2,1,0:T(8,128)(2,1)}), bf16[128,24,1024]{2,1,0:T(8,128)(2,1)}, u32[]{:S(2)}, u32[]{:S(2)}) async-start(bf16[128,24,1024]{2,1,0:T(8,128)(2,1)} %bitcast.38), calls=%async_computation.3 | async-start | bytes 12582912 | tf_op jit(solution)/shard_map/all_to_all | solution.py:388
  283.1 73.6 %all-to-all-done.3 = bf16[128,24,1024]{2,1,0:T(8,128)(2,1)} async-done(((bf16[128,24,1024]{2,1,0:T(8,128)(2,1)}), bf16[128,24,1024]{2,1,0:T(8,128)(2,1)}, u32[]{:S(2)}, u32[]{:S(2)}) %all-to-all-start.3) | async-done | bytes 6291488 | tf_op jit(solution)/shard_map/all_to_all | solution.py:388
  356.7 5.5 %add_convert_fusion = bf16[256,1024]{1,0:T(8,128)(2,1)} fusion(bf16[256,1024]{1,0:T(8,128)(2,1)S(1)} %shard_map.125, bf16[256,4096]{1,0:T(8,128)(2,1)} %param.11, s32[]{:T(128)S(6)} %select_n.179, bf16[256,3072]{1,0:T(8,128)(2,1)S(1)} %fusion.3, bf16[3072,1024]{1,0:T(8,128)(2,1)} %bitcast.12), kind=kOutput, calls=%fused_computation.16 | convolution fusion | flops 1612447744 | bytes 9437188 | tf_op jit(solution)/shard_map/dot_general | solution.py:395
  (79 shorter events, 28.4 us)
Async XLA Ops:
  7.2 2.9 copy-start.3
  7.2 81.2 %all-gather.3.cloned.1.call-start = ((), (), s32[]{:S(2)}) async-start(), calls=%async_computation.4 | async-start | bytes 8650752 | tf_op jit(solution)/shard_map/all_gather | solution.py:300
  12.0 36.3 %collective-permute-start.1 = (bf16[256,4096]{1,0:T(8,128)(2,1)}, bf16[256,4096]{1,0:T(8,128)(2,1)S(1)}, u32[]{:S(2)}, u32[]{:S(2)}) collective-permute-start(bf16[256,4096]{1,0:T(8,128)(2,1)} %fusion.2), channel_id=1, source_target_pairs={{0,1},{1,0},{2,3},{3,2},{4,5},{5,4},{6,7},{7,6},{8,9},{9,8},{10,11... | collective-permute-start | bytes 6291464 | tf_op jit(solution)/shard_map/ppermute | solution.py:33
  13.9 28.8 %all-to-all-start = ((bf16[32,128,128]{2,1,0:T(8,128)(2,1)}), bf16[32,128,128]{2,1,0:T(8,128)(2,1)S(1)}, u32[]{:S(2)}, u32[]{:S(2)}) async-start(bf16[32,128,128]{2,1,0:T(8,128)(2,1)} %bitcast.4), calls=%async_computation | async-start | bytes 2097152 | tf_op jit(solution)/shard_map/all_to_all | solution.py:304
  22.1 122.0 %all-gather.5.cloned.1.call-start = ((), (), s32[]{:S(2)}) async-start(), calls=%async_computation.5 | async-start | bytes 8650752 | tf_op jit(solution)/shard_map/all_gather | solution.py:323
  42.7 17.5 %collective-permute-start = (bf16[1024,128]{1,0:T(8,128)(2,1)}, bf16[1024,128]{1,0:T(8,128)(2,1)S(1)}, u32[]{:S(2)}, u32[]{:S(2)}) collective-permute-start(bf16[1024,128]{1,0:T(8,128)(2,1)} %param.17), channel_id=1, source_target_pairs={{0,0},{1,1},{2,2},{3,3},{4,4},{5,5},{6,6},{7,7},{8,32},{9,33},{10,... | collective-permute-start | bytes 786440 | tf_op jit(solution)/shard_map/ppermute | solution.py:313
  62.7 35.0 %all-to-all-start.1 = ((bf16[16,512,128]{2,1,0:T(8,128)(2,1)}), bf16[16,512,128]{2,1,0:T(8,128)(2,1)S(1)}, u32[]{:S(2)}, u32[]{:S(2)}) async-start(bf16[16,512,128]{2,1,0:T(8,128)(2,1)} %broadcast_in_dim.18), calls=%async_computation.1 | async-start | bytes 4194304 | tf_op jit(solution)/shard_map/all_to_all | solution.py:42
  66.4 32.5 %copy-start.15 = (s32[256,8]{0,1:T(8,128)S(1)}, s32[256,8]{0,1:T(8,128)}, u32[]{:S(2)}) copy-start(s32[256,8]{0,1:T(8,128)} %param.18) | copy-start | bytes 24580
  97.7 5.2 %collective-permute-start.2 = (bf16[8192,128]{1,0:T(8,128)(2,1)S(1)}, bf16[8192,128]{1,0:T(8,128)(2,1)}, u32[]{:S(2)}, u32[]{:S(2)}) collective-permute-start(bf16[8192,128]{1,0:T(8,128)(2,1)S(1)} %bitcast.27), channel_id=1, source_target_pairs={{0,1},{1,0},{2,3},{3,2},{4,5},{5,4},{6,7},{7,6},{8,9},{9,8},{10,11... | collective-permute-start | bytes 6291464 | tf_op jit(solution)/shard_map/ppermute | solution.py:33
  107.1 14.1 %collective-permute-start.6 = (bf16[256,512]{1,0:T(8,128)(2,1)S(1)}, bf16[256,512]{1,0:T(8,128)(2,1)S(1)}, u32[]{:S(2)}, u32[]{:S(2)}) collective-permute-start(bf16[256,512]{1,0:T(8,128)(2,1)S(1)} %shard_map.123.refs_0_), channel_id=1, source_target_pairs={{32,0},{64,32},{96,64},{0,96},{33,1},{65,33},{97,65},{1,97},{34,2}... | collective-permute-start | bytes 786440 | tf_op jit(solution)/shard_map/ppermute | solution.py:37
  109.4 34.7 %collective-permute-start.7 = (bf16[256,512]{1,0:T(8,128)(2,1)S(1)}, bf16[256,512]{1,0:T(8,128)(2,1)S(1)}, u32[]{:S(2)}, u32[]{:S(2)}) collective-permute-start(bf16[256,512]{1,0:T(8,128)(2,1)S(1)} %shard_map.123.refs_0_), channel_id=1, source_target_pairs={{64,0},{96,32},{0,64},{32,96},{65,1},{97,33},{1,65},{33,97},{66,2}... | collective-permute-start | bytes 786440 | tf_op jit(solution)/shard_map/ppermute | solution.py:37
  113.8 30.4 %collective-permute-start.8 = (bf16[256,512]{1,0:T(8,128)(2,1)S(1)}, bf16[256,512]{1,0:T(8,128)(2,1)S(1)}, u32[]{:S(2)}, u32[]{:S(2)}) collective-permute-start(bf16[256,512]{1,0:T(8,128)(2,1)S(1)} %shard_map.123.refs_0_), channel_id=1, source_target_pairs={{96,0},{0,32},{32,64},{64,96},{97,1},{1,33},{33,65},{65,97},{98,2}... | collective-permute-start | bytes 786440 | tf_op jit(solution)/shard_map/ppermute | solution.py:37
  118.5 30.8 %collective-permute-start.3 = (bf16[256,512]{1,0:T(8,128)(2,1)S(1)}, bf16[256,512]{1,0:T(8,128)(2,1)S(1)}, u32[]{:S(2)}, u32[]{:S(2)}) collective-permute-start(bf16[256,512]{1,0:T(8,128)(2,1)S(1)} %shard_map.122.refs_0_), channel_id=1, source_target_pairs={{32,0},{64,32},{96,64},{0,96},{33,1},{65,33},{97,65},{1,97},{34,2}... | collective-permute-start | bytes 786440 | tf_op jit(solution)/shard_map/ppermute | solution.py:37
  120.0 29.3 %collective-permute-start.4 = (bf16[256,512]{1,0:T(8,128)(2,1)S(1)}, bf16[256,512]{1,0:T(8,128)(2,1)S(1)}, u32[]{:S(2)}, u32[]{:S(2)}) collective-permute-start(bf16[256,512]{1,0:T(8,128)(2,1)S(1)} %shard_map.122.refs_0_), channel_id=1, source_target_pairs={{64,0},{96,32},{0,64},{32,96},{65,1},{97,33},{1,65},{33,97},{66,2}... | collective-permute-start | bytes 786440 | tf_op jit(solution)/shard_map/ppermute | solution.py:37
  121.2 28.1 %collective-permute-start.5 = (bf16[256,512]{1,0:T(8,128)(2,1)S(1)}, bf16[256,512]{1,0:T(8,128)(2,1)S(1)}, u32[]{:S(2)}, u32[]{:S(2)}) collective-permute-start(bf16[256,512]{1,0:T(8,128)(2,1)S(1)} %shard_map.122.refs_0_), channel_id=1, source_target_pairs={{96,0},{0,32},{32,64},{64,96},{97,1},{1,33},{33,65},{65,97},{98,2}... | collective-permute-start | bytes 786440 | tf_op jit(solution)/shard_map/ppermute | solution.py:37
  149.3 4.6 %copy-start.4 = (pred[256,3072]{1,0:T(32,128)(4,1)S(1)}, pred[256,3072]{1,0:T(32,128)(4,1)}, u32[]{:S(2)}) copy-start(pred[256,3072]{1,0:T(32,128)(4,1)} %convolution_compare_fusion) | copy-start | bytes 2359300
  153.9 92.5 %slice-start = ((s8[6291456]{0:T(1024)(128)(4,1)}), s8[4194304]{0:T(1024)(128)(4,1)S(1)}, s32[]{:S(2)}) async-start(s8[6291456]{0:T(1024)(128)(4,1)} %bitcast.30), calls=%async_computation.6 | async-start | bytes 8388608
  157.0 89.4 %slice-start.1 = ((s8[6291456]{0:T(1024)(128)(4,1)}), s8[2097152]{0:T(1024)(128)(4,1)S(1)}, s32[]{:S(2)}) async-start(s8[6291456]{0:T(1024)(128)(4,1)} %bitcast.30), calls=%async_computation.7 | async-start | bytes 4194304
  157.0 89.4 %copy-start = (f32[4096]{0:T(1024)S(1)}, f32[4096]{0:T(1024)}, u32[]{:S(2)}) copy-start(f32[4096]{0:T(1024)} %param.13) | copy-start | bytes 49156
  243.1 26.1 %collective-permute-start.10 = (bf16[256,1024]{1,0:T(8,128)(2,1)S(1)}, bf16[256,1024]{1,0:T(8,128)(2,1)S(1)}, u32[]{:S(2)}, u32[]{:S(2)}) collective-permute-start(bf16[256,1024]{1,0:T(8,128)(2,1)S(1)} %shard_map.125), channel_id=1, source_target_pairs={{64,0},{96,32},{0,64},{32,96},{65,1},{97,33},{1,65},{33,97},{66,2}... | collective-permute-start | bytes 1572872 | tf_op jit(solution)/shard_map/ppermute | solution.py:37
  244.9 24.8 %collective-permute-start.11 = (bf16[256,1024]{1,0:T(8,128)(2,1)S(1)}, bf16[256,1024]{1,0:T(8,128)(2,1)S(1)}, u32[]{:S(2)}, u32[]{:S(2)}) collective-permute-start(bf16[256,1024]{1,0:T(8,128)(2,1)S(1)} %shard_map.125), channel_id=1, source_target_pairs={{96,0},{0,32},{32,64},{64,96},{97,1},{1,33},{33,65},{65,97},{98,2}... | collective-permute-start | bytes 1572872 | tf_op jit(solution)/shard_map/ppermute | solution.py:37
  245.8 23.9 %collective-permute-start.9 = (bf16[256,1024]{1,0:T(8,128)(2,1)S(1)}, bf16[256,1024]{1,0:T(8,128)(2,1)S(1)}, u32[]{:S(2)}, u32[]{:S(2)}) collective-permute-start(bf16[256,1024]{1,0:T(8,128)(2,1)S(1)} %shard_map.125), channel_id=1, source_target_pairs={{32,0},{64,32},{96,64},{0,96},{33,1},{65,33},{97,65},{1,97},{34,2}... | collective-permute-start | bytes 1572872 | tf_op jit(solution)/shard_map/ppermute | solution.py:37
  269.7 9.3 %copy-start.16 = (bf16[256,8]{0,1:T(8,128)(2,1)S(1)}, bf16[256,8]{0,1:T(8,128)(2,1)}, u32[]{:S(2)}) copy-start(bf16[256,8]{0,1:T(8,128)(2,1)} %param.19) | copy-start | bytes 12292
  270.7 86.0 %all-to-all-start.3 = ((bf16[128,24,1024]{2,1,0:T(8,128)(2,1)}), bf16[128,24,1024]{2,1,0:T(8,128)(2,1)}, u32[]{:S(2)}, u32[]{:S(2)}) async-start(bf16[128,24,1024]{2,1,0:T(8,128)(2,1)} %bitcast.38), calls=%async_computation.3 | async-start | bytes 12582912 | tf_op jit(solution)/shard_map/all_to_all | solution.py:388
  (12 other events, 19.6 us)
Sparse Core Ops, SparseCore 0:
  10.3 78.0 all-gather.2
  90.6 53.5 all-gather.4

commit v7 on v6

--- a/solution.py
+++ b/solution.py
@@ -148,13 +148,26 @@
 def project_kernel(group_ref, *refs, groups):
     part_refs, (weight_ref, *before, out_ref, total) = refs[:groups], refs[groups:]
     step = pl.program_id(0)
-    weights = jnp.concatenate([weight_ref[0, i] for i in range(weight_ref.shape[1])], axis=1)
+    blocks = weight_ref.shape[1]
+
+    def times_weights(rows):
+        return jnp.concatenate(
+            [
+                jnp.dot(
+                    rows,
+                    jnp.concatenate([weight_ref[0, i], weight_ref[0, i + 1]], axis=1),
+                    preferred_element_type=jnp.float32,
+                )
+                for i in range(0, blocks, 2)
+            ],
+            axis=1,
+        )
 
     for index in range(groups):
 
         @pl.when(step == index)
         def _(index=index):
-            product = jnp.dot(part_refs[index][...], weights, preferred_element_type=jnp.float32)
+            product = times_weights(part_refs[index][...])
             if index > 0:
                 product += total[...]
             elif before:
@@ -322,13 +335,19 @@
     w_turned, kv_local = lax.optimization_barrier((w_turned, kv_local))
     w_out_all = lax.all_gather(w_turned, "fsdp", axis=0, tiled=True)
     kv_mine = from_chips(kv_local)
-    query = jnp.dot(normed, w_query_all, preferred_element_type=jnp.float32).astype(jnp.bfloat16)
-    kv_mine, query = lax.optimization_barrier((kv_mine, query))
+    piece_cols = PIECE_HEADS * HEAD_DIMENSION
+    queries = [
+        jnp.dot(
+            normed, w_query_all[:, start : start + piece_cols], preferred_element_type=jnp.float32
+        ).astype(jnp.bfloat16)
+        for start in range(0, head_width, piece_cols)
+    ]
+    kv_mine, queries = lax.optimization_barrier((kv_mine, queries))
     gathered = (kv_mine, to_other_core(kv_mine))
     rank_array = my_rank.astype(jnp.int32).reshape(1)
     pieces = []
-    for head in range(0, head_width // HEAD_DIMENSION, PIECE_HEADS):
-        piece = attend(rank_array, query, gathered, head, PIECE_HEADS)
+    for query in queries:
+        piece = attend(rank_array, query, gathered, 0, PIECE_HEADS)
         pieces.append([piece] + [from_group(piece, shift) for shift in range(1, head_groups)])
     w_out_cols = w_out_all.reshape(head_groups, fsdp_size // head_groups, *w_out.shape)
     group_array = current_group.astype(jnp.int32).reshape(1)

time: 370 us -> 369 us (level)
  blocking collectives: 86.1 us -> 82.1 us
    all_to_all x1, blocking collectives: 86.1 us -> 82.1 us  [on_device(): lax.all_to_all(outbound.reshape(experts_all, capacity, col_width), ('grp'...]
    dot_general x1 -> x2, matrix products: 6.34 us -> 7.82 us  [on_device(): jnp.dot(normed, w_query_all[:, start:start + piece_cols], preferred_eleme...]
  transfers between devices with their start and end apart: 17 -> 17, of which waited for: 8 -> 8; matrix products, arithmetic and copies ran while one was open for 7% -> 8% of each run, Pallas kernels for 10% -> 10%
where the time goes in v7:
time: 369 us; the launch traced here: 368 us
  waiting for transfers between devices  147 us (40%)
  blocking collectives  82.1 us (22%)
  starting transfers between devices  45.3 us (12%)
  Pallas kernels  39.3 us (11%)
  matrix products  22.7 us (6%)
  between operations  14.3 us (4%)
  other arithmetic  10.7 us (3%)
  local copies, waits for them, and re-layouts  5.87 us (2%)
    all_to_all x1, blocking collectives, on_device(): lax.all_to_all(outbound.reshape(experts_all, capacity, col_width), ('grp'...  82.1 us
    all_to_all x1, waiting for transfers between devices, on_device(): lax.all_to_all(result.reshape(experts_all, capacity, col_width), ('grp',...  72.5 us
    pallas_call x1, Pallas kernels, run_expert(): pl.pallas_call(functools.partial(expert_kernel, wide=wide), grid=(wide +...  22.8 us
    all_gather x1, waiting for transfers between devices, on_device(): w_query_all = lax.all_gather(w_query, 'fsdp', axis=0, tiled=True)  22.2 us
    all_to_all x1, waiting for transfers between devices, on_device(): lax.all_to_all(jnp.tile(w_both, (fsdp_size // 2, 1, 1)), 'fsdp', split_ax...  20.6 us
    ppermute x9, starting transfers between devices, from_group(): lax.ppermute(rows, 'grp', [((i + shift) % SIDE, i) for i in range(SIDE)])  19.7 us
    all_gather x1, waiting for transfers between devices, on_device(): w_out_all = lax.all_gather(w_turned, 'fsdp', axis=0, tiled=True)  17.6 us
    ppermute x1, waiting for transfers between devices, on_device(): lax.ppermute(w_out_block, ('grp', 'fsdp'), [(g * fsdp_size + f, f // 8 *...  9.98 us
  transfers between devices with their start and end apart: 17, of which 8 were waited for; matrix products, arithmetic and copies ran while one was open for 8% of the time, Pallas kernels for 10%

profile of v7, /device:TPU:5, one launch (start us, length us, event | category | flops | bytes accessed | tf_op | source)
XLA Modules:
  0.0 367.7 jit_solution(13184704356580586344)
XLA Ops:
  10.1 2.7 fusion.2
  14.7 8.2 %all-to-all-start = ((bf16[32,128,128]{2,1,0:T(8,128)(2,1)}), bf16[32,128,128]{2,1,0:T(8,128)(2,1)S(1)}, u32[]{:S(2)}, u32[]{:S(2)}) async-start(bf16[32,128,128]{2,1,0:T(8,128)(2,1)} %bitcast.4), calls=%async_computation | async-start | bytes 2097152 | tf_op jit(solution)/shard_map/all_to_all | solution.py:317
  22.9 20.6 %all-to-all-done = bf16[32,128,128]{2,1,0:T(8,128)(2,1)S(1)} async-done(((bf16[32,128,128]{2,1,0:T(8,128)(2,1)}), bf16[32,128,128]{2,1,0:T(8,128)(2,1)S(1)}, u32[]{:S(2)}, u32[]{:S(2)}) %all-to-all-start) | async-done | bytes 1048608 | tf_op jit(solution)/shard_map/all_to_all | solution.py:317
  43.6 3.4 collective-permute-start
  47.0 2.3 convolution_convert_fusion.2
  50.0 10.0 %collective-permute-done = bf16[1024,128]{1,0:T(8,128)(2,1)S(1)} collective-permute-done((bf16[1024,128]{1,0:T(8,128)(2,1)}, bf16[1024,128]{1,0:T(8,128)(2,1)S(1)}, u32[]{:S(2)}, u32[]{:S(2)}) %collective-permute-start) | collective-permute-done | bytes 262176 | tf_op jit(solution)/shard_map/ppermute | solution.py:326
  62.5 3.7 %all-to-all-start.1 = ((bf16[16,512,128]{2,1,0:T(8,128)(2,1)}), bf16[16,512,128]{2,1,0:T(8,128)(2,1)S(1)}, u32[]{:S(2)}, u32[]{:S(2)}) async-start(bf16[16,512,128]{2,1,0:T(8,128)(2,1)} %broadcast_in_dim.18), calls=%async_computation.1 | async-start | bytes 4194304 | tf_op jit(solution)/shard_map/all_to_all | solution.py:42
  66.2 22.2 %all-gather.3.cloned.1.call-done = bf16[4096,1024]{1,0:T(8,128)(2,1)} async-done(((bf16[128,1024]{1,0:T(8,128)(2,1)}), bf16[4096,1024]{1,0:T(8,128)(2,1)}) %all-gather.3.cloned.1.call-update) | async-done | bytes 8388624 | tf_op jit(solution)/shard_map/all_gather | solution.py:313
  88.4 4.9 %fusion.11.query_ref = bf16[256,512]{1,0:T(8,128)(2,1)} fusion(bf16[256,4096]{1,0:T(8,128)(2,1)} %fusion.2, bf16[4096,1024]{1,0:T(8,128)(2,1)} %all-gather.3.cloned.1.call-done), kind=kOutput, calls=%fused_computation.16 | convolution fusion | flops 1073872896 | bytes 6553600 | tf_op jit(solution)/shard_map/dot_general | solution.py:340
  93.6 2.9 fusion.8.query_ref
  103.2 3.6 shard_map.123.refs_0_
  108.8 5.5 %collective-permute-start.7 = (bf16[256,512]{1,0:T(8,128)(2,1)S(1)}, bf16[256,512]{1,0:T(8,128)(2,1)S(1)}, u32[]{:S(2)}, u32[]{:S(2)}) collective-permute-start(bf16[256,512]{1,0:T(8,128)(2,1)S(1)} %shard_map.123.refs_0_), channel_id=1, source_target_pairs={{64,0},{96,32},{0,64},{32,96},{65,1},{97,33},{1,65},{33,97},{66,2}... | collective-permute-start | bytes 786440 | tf_op jit(solution)/shard_map/ppermute | solution.py:37
  114.2 3.6 shard_map.122.refs_0_
  120.7 6.2 %collective-permute-start.5 = (bf16[256,512]{1,0:T(8,128)(2,1)S(1)}, bf16[256,512]{1,0:T(8,128)(2,1)S(1)}, u32[]{:S(2)}, u32[]{:S(2)}) collective-permute-start(bf16[256,512]{1,0:T(8,128)(2,1)S(1)} %shard_map.122.refs_0_), channel_id=1, source_target_pairs={{96,0},{0,32},{32,64},{64,96},{97,1},{1,33},{33,65},{65,97},{98,2}... | collective-permute-start | bytes 786440 | tf_op jit(solution)/shard_map/ppermute | solution.py:37
  126.9 2.7 convolution_compare_fusion
  129.5 17.6 %all-gather.5.cloned.1.call-done = bf16[32768,128]{1,0:T(8,128)(2,1)} async-done(((bf16[1024,128]{1,0:T(8,128)(2,1)}), bf16[32768,128]{1,0:T(8,128)(2,1)}) %all-gather.5.cloned.1.call-update) | async-done | bytes 8388624 | tf_op jit(solution)/shard_map/all_gather | solution.py:336
  147.1 4.9 %shard_map.124.refs_5_ = f32[256,1024]{1,0:T(8,128)} custom-call(s32[1]{0:T(128)} %bitcast.group_ref, bf16[256,512]{1,0:T(8,128)(2,1)S(1)} %shard_map.123.refs_0_, bf16[256,512]{1,0:T(8,128)(2,1)S(1)} %collective-permute-done.6.refs_1_, bf16[256,512]{1,0:T(8,128)(2,1)S(1)} %collective-permute-done.7.refs_2_, ...), custom_call_target="tpu_custom_call" | custom-call | flops 1073741824 | bytes 5242880 | tf_op jit(solution)/shard_map/pallas_call | solution.py:186
  152.0 4.4 %shard_map.125 = bf16[256,1024]{1,0:T(8,128)(2,1)S(1)} custom-call(s32[1]{0:T(128)} %bitcast.group_ref, bf16[256,512]{1,0:T(8,128)(2,1)S(1)} %shard_map.122.refs_0_, bf16[256,512]{1,0:T(8,128)(2,1)S(1)} %collective-permute-done.3.refs_1_, bf16[256,512]{1,0:T(8,128)(2,1)S(1)} %collective-permute-done.4.refs_2_, ...), custom_call_target="tpu_custom_call" | custom-call | flops 1073741824 | bytes 5242880 | tf_op jit(solution)/shard_map/pallas_call | solution.py:186
  156.4 3.0 convolution_convert_fusion
  159.5 82.1 %all_to_all.20 = bf16[128,24,1024]{2,1,0:T(8,128)(2,1)S(1)} all-to-all(bf16[128,24,1024]{2,1,0:T(8,128)(2,1)S(1)} %bitcast.33), channel_id=1, replica_groups=mesh['grp'=4,'fsdp'=32] {'grp','fsdp'}, dimensions={0} | all-to-all | bytes 12582912 | tf_op jit(solution)/shard_map/all_to_all | solution.py:387
  244.9 22.8 %shard_map.126 = bf16[4,768,1024]{2,1,0:T(8,128)(2,1)} custom-call(bf16[4,768,1024]{2,1,0:T(8,128)(2,1)S(1)} %bitcast.26, f32[4,1,1024]{2,1,0:T(1,128)S(1)} %bitcast.32, bf16[1,4096,1536]{2,1,0:T(8,128)(2,1)} %up_ref.1, bf16[1,4096,1536]{2,1,0:T(8,128)(2,1)} %up_ref.1, bf16[1,768,4096]{2,1,0:T(8,128)(2,1)S(1)} %bitcast.31), custom_call_target="tpu_custom_call" | custom-call | flops 14495514624 | bytes 31457280 | tf_op jit(solution)/shard_map/pallas_call | solution.py:260
  269.8 8.0 %all-to-all-start.3 = ((bf16[128,24,1024]{2,1,0:T(8,128)(2,1)}), bf16[128,24,1024]{2,1,0:T(8,128)(2,1)}, u32[]{:S(2)}, u32[]{:S(2)}) async-start(bf16[128,24,1024]{2,1,0:T(8,128)(2,1)} %bitcast.38), calls=%async_computation.3 | async-start | bytes 12582912 | tf_op jit(solution)/shard_map/all_to_all | solution.py:407
  283.0 72.5 %all-to-all-done.3 = bf16[128,24,1024]{2,1,0:T(8,128)(2,1)} async-done(((bf16[128,24,1024]{2,1,0:T(8,128)(2,1)}), bf16[128,24,1024]{2,1,0:T(8,128)(2,1)}, u32[]{:S(2)}, u32[]{:S(2)}) %all-to-all-start.3) | async-done | bytes 6291488 | tf_op jit(solution)/shard_map/all_to_all | solution.py:407
  355.4 5.4 %add_convert_fusion = bf16[256,1024]{1,0:T(8,128)(2,1)} fusion(bf16[256,1024]{1,0:T(8,128)(2,1)S(1)} %shard_map.125, bf16[256,4096]{1,0:T(8,128)(2,1)} %param.11, s32[]{:T(128)S(6)} %select_n.179, bf16[256,3072]{1,0:T(8,128)(2,1)S(1)} %fusion.7, bf16[3072,1024]{1,0:T(8,128)(2,1)} %bitcast.12), kind=kOutput, calls=%fused_computation.21 | convolution fusion | flops 1612447744 | bytes 9437188 | tf_op jit(solution)/shard_map/dot_general | solution.py:414
  (70 shorter events, 30.2 us)
Async XLA Ops:
  7.2 81.2 %all-gather.3.cloned.1.call-start = ((), (), s32[]{:S(2)}) async-start(), calls=%async_computation.4 | async-start | bytes 8650752 | tf_op jit(solution)/shard_map/all_gather | solution.py:313
  7.9 5.5 %copy-start.7 = (bf16[128,256]{1,0:T(8,128)(2,1)S(1)}, bf16[128,256]{1,0:T(8,128)(2,1)}, u32[]{:S(2)}) copy-start(bf16[128,256]{1,0:T(8,128)(2,1)} %param.16) | copy-start | bytes 196612
  12.7 36.5 %collective-permute-start.1 = (bf16[256,4096]{1,0:T(8,128)(2,1)}, bf16[256,4096]{1,0:T(8,128)(2,1)S(1)}, u32[]{:S(2)}, u32[]{:S(2)}) collective-permute-start(bf16[256,4096]{1,0:T(8,128)(2,1)} %fusion.2), channel_id=1, source_target_pairs={{0,1},{1,0},{2,3},{3,2},{4,5},{5,4},{6,7},{7,6},{8,9},{9,8},{10,11... | collective-permute-start | bytes 6291464 | tf_op jit(solution)/shard_map/ppermute | solution.py:33
  14.7 28.9 %all-to-all-start = ((bf16[32,128,128]{2,1,0:T(8,128)(2,1)}), bf16[32,128,128]{2,1,0:T(8,128)(2,1)S(1)}, u32[]{:S(2)}, u32[]{:S(2)}) async-start(bf16[32,128,128]{2,1,0:T(8,128)(2,1)} %bitcast.4), calls=%async_computation | async-start | bytes 2097152 | tf_op jit(solution)/shard_map/all_to_all | solution.py:317
  22.9 124.2 %all-gather.5.cloned.1.call-start = ((), (), s32[]{:S(2)}) async-start(), calls=%async_computation.5 | async-start | bytes 8650752 | tf_op jit(solution)/shard_map/all_gather | solution.py:336
  43.6 16.4 %collective-permute-start = (bf16[1024,128]{1,0:T(8,128)(2,1)}, bf16[1024,128]{1,0:T(8,128)(2,1)S(1)}, u32[]{:S(2)}, u32[]{:S(2)}) collective-permute-start(bf16[1024,128]{1,0:T(8,128)(2,1)} %param.17), channel_id=1, source_target_pairs={{0,0},{1,1},{2,2},{3,3},{4,4},{5,5},{6,6},{7,7},{8,32},{9,33},{10,... | collective-permute-start | bytes 786440 | tf_op jit(solution)/shard_map/ppermute | solution.py:326
  62.5 35.3 %all-to-all-start.1 = ((bf16[16,512,128]{2,1,0:T(8,128)(2,1)}), bf16[16,512,128]{2,1,0:T(8,128)(2,1)S(1)}, u32[]{:S(2)}, u32[]{:S(2)}) async-start(bf16[16,512,128]{2,1,0:T(8,128)(2,1)} %broadcast_in_dim.18), calls=%async_computation.1 | async-start | bytes 4194304 | tf_op jit(solution)/shard_map/all_to_all | solution.py:42
  93.6 5.7 %copy-start.9 = (s32[256,8]{0,1:T(8,128)S(1)}, s32[256,8]{0,1:T(8,128)}, u32[]{:S(2)}) copy-start(s32[256,8]{0,1:T(8,128)} %param.18) | copy-start | bytes 24580
  97.8 5.4 %collective-permute-start.2 = (bf16[8192,128]{1,0:T(8,128)(2,1)S(1)}, bf16[8192,128]{1,0:T(8,128)(2,1)}, u32[]{:S(2)}, u32[]{:S(2)}) collective-permute-start(bf16[8192,128]{1,0:T(8,128)(2,1)S(1)} %bitcast.27), channel_id=1, source_target_pairs={{0,1},{1,0},{2,3},{3,2},{4,5},{5,4},{6,7},{7,6},{8,9},{9,8},{10,11... | collective-permute-start | bytes 6291464 | tf_op jit(solution)/shard_map/ppermute | solution.py:33
  103.2 11.1 %copy-start.1 = (bf16[256,512]{1,0:T(8,128)(2,1)S(1)}, bf16[256,512]{1,0:T(8,128)(2,1)}, u32[]{:S(2)}) copy-start(bf16[256,512]{1,0:T(8,128)(2,1)} %fusion.11.query_ref) | copy-start | bytes 786436
  106.8 13.9 %collective-permute-start.6 = (bf16[256,512]{1,0:T(8,128)(2,1)S(1)}, bf16[256,512]{1,0:T(8,128)(2,1)S(1)}, u32[]{:S(2)}, u32[]{:S(2)}) collective-permute-start(bf16[256,512]{1,0:T(8,128)(2,1)S(1)} %shard_map.123.refs_0_), channel_id=1, source_target_pairs={{32,0},{64,32},{96,64},{0,96},{33,1},{65,33},{97,65},{1,97},{34,2}... | collective-permute-start | bytes 786440 | tf_op jit(solution)/shard_map/ppermute | solution.py:37
  108.8 38.3 %collective-permute-start.7 = (bf16[256,512]{1,0:T(8,128)(2,1)S(1)}, bf16[256,512]{1,0:T(8,128)(2,1)S(1)}, u32[]{:S(2)}, u32[]{:S(2)}) collective-permute-start(bf16[256,512]{1,0:T(8,128)(2,1)S(1)} %shard_map.123.refs_0_), channel_id=1, source_target_pairs={{64,0},{96,32},{0,64},{32,96},{65,1},{97,33},{1,65},{33,97},{66,2}... | collective-permute-start | bytes 786440 | tf_op jit(solution)/shard_map/ppermute | solution.py:37
  114.2 32.9 %collective-permute-start.8 = (bf16[256,512]{1,0:T(8,128)(2,1)S(1)}, bf16[256,512]{1,0:T(8,128)(2,1)S(1)}, u32[]{:S(2)}, u32[]{:S(2)}) collective-permute-start(bf16[256,512]{1,0:T(8,128)(2,1)S(1)} %shard_map.123.refs_0_), channel_id=1, source_target_pairs={{96,0},{0,32},{32,64},{64,96},{97,1},{1,33},{33,65},{65,97},{98,2}... | collective-permute-start | bytes 786440 | tf_op jit(solution)/shard_map/ppermute | solution.py:37
  117.9 34.1 %collective-permute-start.3 = (bf16[256,512]{1,0:T(8,128)(2,1)S(1)}, bf16[256,512]{1,0:T(8,128)(2,1)S(1)}, u32[]{:S(2)}, u32[]{:S(2)}) collective-permute-start(bf16[256,512]{1,0:T(8,128)(2,1)S(1)} %shard_map.122.refs_0_), channel_id=1, source_target_pairs={{32,0},{64,32},{96,64},{0,96},{33,1},{65,33},{97,65},{1,97},{34,2}... | collective-permute-start | bytes 786440 | tf_op jit(solution)/shard_map/ppermute | solution.py:37
  119.4 32.6 %collective-permute-start.4 = (bf16[256,512]{1,0:T(8,128)(2,1)S(1)}, bf16[256,512]{1,0:T(8,128)(2,1)S(1)}, u32[]{:S(2)}, u32[]{:S(2)}) collective-permute-start(bf16[256,512]{1,0:T(8,128)(2,1)S(1)} %shard_map.122.refs_0_), channel_id=1, source_target_pairs={{64,0},{96,32},{0,64},{32,96},{65,1},{97,33},{1,65},{33,97},{66,2}... | collective-permute-start | bytes 786440 | tf_op jit(solution)/shard_map/ppermute | solution.py:37
  120.7 31.4 %collective-permute-start.5 = (bf16[256,512]{1,0:T(8,128)(2,1)S(1)}, bf16[256,512]{1,0:T(8,128)(2,1)S(1)}, u32[]{:S(2)}, u32[]{:S(2)}) collective-permute-start(bf16[256,512]{1,0:T(8,128)(2,1)S(1)} %shard_map.122.refs_0_), channel_id=1, source_target_pairs={{96,0},{0,32},{32,64},{64,96},{97,1},{1,33},{33,65},{65,97},{98,2}... | collective-permute-start | bytes 786440 | tf_op jit(solution)/shard_map/ppermute | solution.py:37
  156.4 88.5 %slice-start = ((s8[6291456]{0:T(1024)(128)(4,1)}), s8[4194304]{0:T(1024)(128)(4,1)S(1)}, s32[]{:S(2)}) async-start(s8[6291456]{0:T(1024)(128)(4,1)} %bitcast.30), calls=%async_computation.6 | async-start | bytes 8388608
  159.5 85.4 %slice-start.1 = ((s8[6291456]{0:T(1024)(128)(4,1)}), s8[2097152]{0:T(1024)(128)(4,1)S(1)}, s32[]{:S(2)}) async-start(s8[6291456]{0:T(1024)(128)(4,1)} %bitcast.30), calls=%async_computation.7 | async-start | bytes 4194304
  159.5 85.4 %copy-start = (f32[4096]{0:T(1024)S(1)}, f32[4096]{0:T(1024)}, u32[]{:S(2)}) copy-start(f32[4096]{0:T(1024)} %param.13) | copy-start | bytes 49156
  241.6 26.1 %collective-permute-start.10 = (bf16[256,1024]{1,0:T(8,128)(2,1)S(1)}, bf16[256,1024]{1,0:T(8,128)(2,1)S(1)}, u32[]{:S(2)}, u32[]{:S(2)}) collective-permute-start(bf16[256,1024]{1,0:T(8,128)(2,1)S(1)} %shard_map.125), channel_id=1, source_target_pairs={{64,0},{96,32},{0,64},{32,96},{65,1},{97,33},{1,65},{33,97},{66,2}... | collective-permute-start | bytes 1572872 | tf_op jit(solution)/shard_map/ppermute | solution.py:37
  243.4 24.8 %collective-permute-start.11 = (bf16[256,1024]{1,0:T(8,128)(2,1)S(1)}, bf16[256,1024]{1,0:T(8,128)(2,1)S(1)}, u32[]{:S(2)}, u32[]{:S(2)}) collective-permute-start(bf16[256,1024]{1,0:T(8,128)(2,1)S(1)} %shard_map.125), channel_id=1, source_target_pairs={{96,0},{0,32},{32,64},{64,96},{97,1},{1,33},{33,65},{65,97},{98,2}... | collective-permute-start | bytes 1572872 | tf_op jit(solution)/shard_map/ppermute | solution.py:37
  244.3 23.9 %collective-permute-start.9 = (bf16[256,1024]{1,0:T(8,128)(2,1)S(1)}, bf16[256,1024]{1,0:T(8,128)(2,1)S(1)}, u32[]{:S(2)}, u32[]{:S(2)}) collective-permute-start(bf16[256,1024]{1,0:T(8,128)(2,1)S(1)} %shard_map.125), channel_id=1, source_target_pairs={{32,0},{64,32},{96,64},{0,96},{33,1},{65,33},{97,65},{1,97},{34,2}... | collective-permute-start | bytes 1572872 | tf_op jit(solution)/shard_map/ppermute | solution.py:37
  269.8 8.1 %copy-start.10 = (bf16[256,8]{0,1:T(8,128)(2,1)S(1)}, bf16[256,8]{0,1:T(8,128)(2,1)}, u32[]{:S(2)}) copy-start(bf16[256,8]{0,1:T(8,128)(2,1)} %param.19) | copy-start | bytes 12292
  269.8 85.7 %all-to-all-start.3 = ((bf16[128,24,1024]{2,1,0:T(8,128)(2,1)}), bf16[128,24,1024]{2,1,0:T(8,128)(2,1)}, u32[]{:S(2)}, u32[]{:S(2)}) async-start(bf16[128,24,1024]{2,1,0:T(8,128)(2,1)} %bitcast.38), calls=%async_computation.3 | async-start | bytes 12582912 | tf_op jit(solution)/shard_map/all_to_all | solution.py:407
  (7 other events, 20.3 us)
Sparse Core Ops, SparseCore 0:
  10.3 78.0 all-gather.2
  90.6 56.4 all-gather.4
